TPU v7x, 32 devices: a whole 2x2x4 slice. The times are simulated.
32 devices in a mesh: ctx: 8 (over z, y), fsdp: 4 (over x, core).
Axes of the slice: x: 2, y: 2, z: 4, core: 2. Of those that a mesh axis runs over, the one named last changes fastest.
Arguments:
- tokens: bfloat16 [4096, 1152], P(('ctx', 'fsdp')), may hold values from -6 to 6
- cotangent: bfloat16 [4096, 1152], P(('ctx', 'fsdp')), may hold values from -6 to 6
- block_table: int32 [64], replicated, may hold values from 0 to 63, as said below
- sequence_ids: int32 [4096], replicated, may hold values from 0 to 1, as said below
- w_query: bfloat16 [1152, 1024], P('fsdp'), may hold values from -0.1875 to 0.1875
- w_key: bfloat16 [1152, 256], P('fsdp'), may hold values from -0.1875 to 0.1875
- w_value: bfloat16 [1152, 256], P('fsdp'), may hold values from -0.1875 to 0.1875
- w_out: bfloat16 [1024, 1152], P('fsdp'), may hold values from -0.1875 to 0.1875
- w_in: bfloat16 [1152, 2, 6912], P('fsdp'), may hold values from -0.1875 to 0.1875
- w_down: bfloat16 [6912, 1152], P('fsdp'), may hold values from -0.078125 to 0.078125
- gain_attn_in: bfloat16 [1152], P('fsdp'), may hold values from 0.099609375 to 1.8984375
- gain_attn_out: bfloat16 [1152], P('fsdp'), may hold values from 0.099609375 to 1.8984375
- gain_ffn_in: bfloat16 [1152], P('fsdp'), may hold values from 0.099609375 to 1.8984375
- gain_ffn_out: bfloat16 [1152], P('fsdp'), may hold values from 0.099609375 to 1.8984375
- gain_query: bfloat16 [256], P('fsdp'), may hold values from 0.099609375 to 1.8984375
- gain_key: bfloat16 [256], P('fsdp'), may hold values from 0.099609375 to 1.8984375
Outputs:
- block_out: bfloat16 [4096, 1152], P(('ctx', 'fsdp'))
- grad_tokens: float32 [4096, 1152], P(('ctx', 'fsdp'))
- grad_query: float32 [1152, 1024], P('fsdp')
- grad_key: float32 [1152, 256], P('fsdp')
- grad_value: float32 [1152, 256], P('fsdp')
- grad_out: float32 [1024, 1152], P('fsdp')
- grad_in: float32 [1152, 2, 6912], P('fsdp')
- grad_down: float32 [6912, 1152], P('fsdp')
- grad_gain_attn_in: float32 [1152], P('fsdp')
- grad_gain_attn_out: float32 [1152], P('fsdp')
- grad_gain_ffn_in: float32 [1152], P('fsdp')
- grad_gain_ffn_out: float32 [1152], P('fsdp')
- grad_gain_query: float32 [256], P('fsdp')
- grad_gain_key: float32 [256], P('fsdp')
Inputs may be any that keep to these rules, and one draw needn't show every extreme that they name: Device d of ctx+fsdp (ctx slowest) holds rows of stream blocks block_table[2 d] and block_table[2 d + 1]; these two sum to 63, and every block appears once. `sequence_ids`: 0 on the places of the first sequence, then 1 on those of the second; each sequence has 1024 places or more.
All inputs are finite; a program needn't handle non-finite values.
Results may differ from a plain program's by a relative error of at most 0.023.
Values may be sent and summed in bfloat16 or wider, within the bound.
No kernel may reach another device: no remote copies, remote signals or barrier semaphores. Data moves between devices by JAX's collectives and lax.ppermute only.
A program may use at most 384 MiB of HBM per device.

v0:
```python
import math

import jax
import jax.numpy as jnp
from jax import lax
from jax.sharding import PartitionSpec as P

H = 4
HD = 256


EPS = 1e-06


def rms_norm(values, scaling):
    return values * lax.rsqrt(jnp.mean(values * values, axis=-1, keepdims=True) + EPS) * scaling


def rotate(values, angles):
    half_width = values.shape[-1] // 2
    cosine = jnp.cos(angles)
    sine_part = jnp.sin(angles)
    first_half = values[..., :half_width]
    second_half = values[..., half_width:]
    return jnp.concatenate(
        [
            first_half * cosine - second_half * sine_part,
            second_half * cosine + first_half * sine_part,
        ],
        axis=-1,
    )


def place_rows(block_table, sequence_ids, layout_rows, half_block):
    stream = block_table[layout_rows // half_block] * half_block + layout_rows % half_block
    boundary = jnp.sum((sequence_ids == 0).astype(jnp.int32))
    sequence = sequence_ids[stream]
    position = stream - sequence * boundary
    return (position, sequence)


def angles_of(position, half_width):
    inverse = 1000000.0 ** (-jnp.arange(half_width, dtype=jnp.float32) / half_width)
    return position.astype(jnp.float32)[:, None] * inverse[None, :]


def over_blocks(step, initial, key_rows, value_rows):
    total_rows = key_rows.shape[0]
    block_width = math.gcd(total_rows, 2048)
    block_count = total_rows // block_width
    offsets = jnp.arange(block_count, dtype=jnp.int32) * block_width

    def scan_step(running, section):
        key_block, value_block, offset = section
        return step(running, (key_block, value_block), offset)

    return lax.scan(
        scan_step,
        initial,
        (
            key_rows.reshape(block_count, block_width, -1),
            value_rows.reshape(block_count, block_width, -1),
            offsets,
        ),
    )


def body(
    tokens,
    cotangent,
    block_table,
    sequence_ids,
    w_query,
    w_key,
    w_value,
    w_out,
    w_in,
    w_down,
    gain_attn_in,
    gain_attn_out,
    gain_ffn_in,
    gain_ffn_out,
    gain_query,
    gain_key,
):
    row_count = tokens.shape[0]
    half_block = row_count // 2
    head_count = H
    head_dim = HD
    first_row = lax.axis_index(("ctx", "fsdp")) * row_count
    local_rows = first_row + jnp.arange(row_count, dtype=jnp.int32)
    position, sequence = place_rows(block_table, sequence_ids, local_rows, half_block)
    local_angles = angles_of(position, head_dim // 2)
    gathered = (
        lax.all_gather(w_query, "fsdp", axis=0, tiled=True),
        lax.all_gather(w_key, "fsdp", axis=0, tiled=True),
        lax.all_gather(w_value, "fsdp", axis=0, tiled=True),
        lax.all_gather(w_out, "fsdp", axis=0, tiled=True),
        lax.all_gather(gain_attn_in, "fsdp", axis=0, tiled=True),
        lax.all_gather(gain_attn_out, "fsdp", axis=0, tiled=True),
        lax.all_gather(gain_ffn_in, "fsdp", axis=0, tiled=True),
        lax.all_gather(gain_ffn_out, "fsdp", axis=0, tiled=True),
        lax.all_gather(gain_query, "fsdp", axis=0, tiled=True),
        lax.all_gather(gain_key, "fsdp", axis=0, tiled=True),
    )
    query_mat, key_mat, value_mat, out_mat = (gathered[0], gathered[1], gathered[2], gathered[3])
    attn_in_gain, attn_out_gain, ffn_in_gain, ffn_out_gain, query_gain, key_gain = [
        member.astype(jnp.float32) for member in gathered[4:]
    ]
    inputs = tokens.astype(jnp.float32)
    first_norm, first_back = jax.vjp(rms_norm, inputs, attn_in_gain)
    first_low = first_norm.astype(jnp.bfloat16)
    query_raw = jnp.dot(first_low, query_mat, preferred_element_type=jnp.float32)
    key_raw = jnp.dot(first_low, key_mat, preferred_element_type=jnp.float32)
    value_raw = jnp.dot(first_low, value_mat, preferred_element_type=jnp.float32)

    def prepare(query_in, key_in, query_scaling, key_scaling):
        query_heads = rms_norm(query_in.reshape(row_count, head_count, head_dim), query_scaling)
        query_turned = rotate(query_heads, local_angles[:, None, :]) * head_dim ** (-0.5)
        key_turned = rotate(rms_norm(key_in, key_scaling), local_angles)
        return (query_turned, key_turned)

    (query_turned, key_turned), prepare_back = jax.vjp(
        prepare, query_raw, key_raw, query_gain, key_gain
    )
    queries = query_turned.astype(jnp.bfloat16)
    key_rows = key_turned.astype(jnp.bfloat16)
    value_rows = value_raw.astype(jnp.bfloat16)

    def visible(offset, amount):
        other_rows = offset + jnp.arange(amount, dtype=jnp.int32)
        other_pos, other_seq = place_rows(block_table, sequence_ids, other_rows, half_block)
        return (other_seq[None, :] == sequence[:, None]) & (other_pos[None, :] <= position[:, None])

    key_portion = lax.all_gather(key_rows, ("ctx", "fsdp"), axis=0, tiled=True)
    largest = jnp.full((head_count, row_count), -1e30, jnp.float32)
    allowed = visible(jnp.int32(0), key_portion.shape[0])[None]
    scores = jnp.einsum("qhd,kd->hqk", queries, key_portion, preferred_element_type=jnp.float32)
    scores = jnp.where(allowed, scores, -1e30)
    updated = jnp.maximum(largest, jnp.max(scores, axis=-1))
    weights = jnp.where(allowed, jnp.exp(scores - updated[..., None]), 0.0)
    mass_sum = jnp.sum(weights, axis=-1)
    largest, mass_sum = (updated, mass_sum)
    back_keys, back_values = (
        lax.all_gather(key_rows, ("ctx", "fsdp"), axis=0, tiled=True),
        lax.all_gather(value_rows, ("ctx", "fsdp"), axis=0, tiled=True),
    )
    log_total = largest + jnp.log(mass_sum)

    def chances(portion, offset):
        key_portion = portion[0]
        allowed = visible(offset, key_portion.shape[0])[None]
        scores = jnp.einsum("qhd,kd->hqk", queries, key_portion, preferred_element_type=jnp.float32)
        return jnp.where(
            allowed, jnp.exp(jnp.where(allowed, scores, -1e30) - log_total[..., None]), 0.0
        )

    def produce(running, portion, offset):
        weighted, remainder = running
        probabilities = chances(portion, offset)
        probs_low = probabilities.astype(jnp.bfloat16)
        probs_rest = (probabilities - probs_low.astype(jnp.float32)).astype(jnp.bfloat16)
        weighted = weighted + jnp.einsum(
            "hqk,kd->qhd", probs_low, portion[1], preferred_element_type=jnp.float32
        )
        remainder = remainder + jnp.einsum(
            "hqk,kd->qhd", probs_rest, portion[1], preferred_element_type=jnp.float32
        )
        return ((weighted, remainder), None)

    zero_heads = jnp.zeros((row_count, head_count, head_dim), jnp.float32)
    (heads_out, remainder), _ = over_blocks(
        produce, (zero_heads, zero_heads), back_keys, back_values
    )
    heads_exact = heads_out + remainder
    heads_low = heads_out.astype(jnp.bfloat16).reshape(row_count, head_count * head_dim)
    attn_raw = jnp.dot(heads_low, out_mat, preferred_element_type=jnp.float32)
    attn_normed, attn_back = jax.vjp(rms_norm, attn_raw, attn_out_gain)
    hidden = inputs + attn_normed
    second_norm, second_back = jax.vjp(rms_norm, hidden, ffn_in_gain)
    second_low = second_norm.astype(jnp.bfloat16)
    columns = second_low
    gate_up = jnp.einsum(
        "td,dkf->tkf",
        columns,
        lax.all_gather(w_in, "fsdp", axis=0, tiled=True),
        preferred_element_type=jnp.float32,
    )

    def activate(gate_part, upper_part):
        return jax.nn.gelu(gate_part, approximate=True) * upper_part

    act_value, act_back = jax.vjp(activate, gate_up[:, 0], gate_up[:, 1])
    act_low = act_value.astype(jnp.bfloat16)
    columns = act_low
    ffn_raw = jnp.dot(
        columns,
        lax.all_gather(w_down, "fsdp", axis=0, tiled=True),
        preferred_element_type=jnp.float32,
    )
    ffn_normed, ffn_back = jax.vjp(rms_norm, ffn_raw, ffn_out_gain)
    block_out = (hidden + ffn_normed).astype(jnp.bfloat16)
    upstream = cotangent.astype(jnp.float32)
    d_ffn, d_gain_ffn_out = ffn_back(upstream)
    d_ffn_low = d_ffn.astype(jnp.bfloat16)
    d_act = lax.dot_general(
        d_ffn_low,
        lax.all_gather(w_down, "fsdp", axis=0, tiled=True),
        (((1,), (1,)), ((), ())),
        preferred_element_type=jnp.float32,
    )
    d_gate, d_upper = act_back(d_act)
    d_gate_up = jnp.stack([d_gate, d_upper], axis=1).astype(jnp.bfloat16)
    columns = act_low
    grad_down = lax.psum_scatter(
        jnp.einsum("tf,td->fd", columns, d_ffn_low, preferred_element_type=jnp.float32).astype(
            jnp.bfloat16
        ),
        "fsdp",
        scatter_dimension=0,
        tiled=True,
    )
    columns = second_low
    grad_in = lax.psum_scatter(
        jnp.einsum("td,tkf->dkf", columns, d_gate_up, preferred_element_type=jnp.float32).astype(
            jnp.bfloat16
        ),
        "fsdp",
        scatter_dimension=0,
        tiled=True,
    )
    d_second = jnp.einsum(
        "tkf,dkf->td",
        d_gate_up,
        lax.all_gather(w_in, "fsdp", axis=0, tiled=True),
        preferred_element_type=jnp.float32,
    )
    d_hidden_extra, d_gain_ffn_in = second_back(d_second)
    d_hidden = upstream + d_hidden_extra
    d_attn, d_gain_attn_out = attn_back(d_hidden)
    d_attn_low = d_attn.astype(jnp.bfloat16)
    d_heads_low = (
        jnp.dot(d_attn_low, out_mat.T, preferred_element_type=jnp.float32)
        .astype(jnp.bfloat16)
        .reshape(row_count, head_count, head_dim)
    )
    grad_out_part = jnp.dot(heads_low.T, d_attn_low, preferred_element_type=jnp.float32)
    row_dots = jnp.transpose(jnp.sum(d_heads_low.astype(jnp.float32) * heads_exact, axis=-1))

    def reverse(running, portion, offset):
        key_portion, value_portion = portion
        probabilities = chances(portion, offset)
        d_probs = jnp.einsum(
            "qhd,kd->hqk", d_heads_low, value_portion, preferred_element_type=jnp.float32
        )
        d_scores = (probabilities * (d_probs - row_dots[..., None])).astype(jnp.bfloat16)
        running = running + jnp.einsum(
            "hqk,kd->qhd", d_scores, key_portion, preferred_element_type=jnp.float32
        )
        d_key_part = jnp.einsum(
            "hqk,qhd->kd", d_scores, queries, preferred_element_type=jnp.float32
        )
        d_value_part = jnp.einsum(
            "hqk,qhd->kd",
            probabilities.astype(jnp.bfloat16),
            d_heads_low,
            preferred_element_type=jnp.float32,
        )
        return (running, jnp.concatenate([d_key_part, d_value_part], axis=1))

    d_queries, key_terms = over_blocks(
        reverse, jnp.zeros((row_count, head_count, head_dim), jnp.float32), back_keys, back_values
    )
    key_terms = key_terms.reshape(-1, 2 * head_dim)
    own_sums = lax.psum_scatter(key_terms, ("ctx", "fsdp"), scatter_dimension=0, tiled=True)
    d_query_raw, d_key_raw, d_gain_query, d_gain_key = prepare_back(
        (d_queries, own_sums[:, :head_dim])
    )
    query_low = d_query_raw.astype(jnp.bfloat16)
    key_low = d_key_raw.astype(jnp.bfloat16)
    value_low = own_sums[:, head_dim:].astype(jnp.bfloat16)
    d_first = jnp.dot(query_low, query_mat.T, preferred_element_type=jnp.float32)
    d_first = d_first + jnp.dot(key_low, key_mat.T, preferred_element_type=jnp.float32)
    d_first = d_first + jnp.dot(value_low, value_mat.T, preferred_element_type=jnp.float32)
    grad_query_part = jnp.dot(first_low.T, query_low, preferred_element_type=jnp.float32)
    grad_key_part = jnp.dot(first_low.T, key_low, preferred_element_type=jnp.float32)
    grad_value_part = jnp.dot(first_low.T, value_low, preferred_element_type=jnp.float32)
    d_inputs_extra, d_gain_attn_in = first_back(d_first)
    grad_tokens = d_hidden + d_inputs_extra
    shared = (
        lax.psum_scatter(
            grad_query_part.astype(jnp.bfloat16), "fsdp", scatter_dimension=0, tiled=True
        ).astype(jnp.float32),
        lax.psum_scatter(
            grad_key_part.astype(jnp.bfloat16), "fsdp", scatter_dimension=0, tiled=True
        ).astype(jnp.float32),
        lax.psum_scatter(
            grad_value_part.astype(jnp.bfloat16), "fsdp", scatter_dimension=0, tiled=True
        ).astype(jnp.float32),
        lax.psum_scatter(
            grad_out_part.astype(jnp.bfloat16), "fsdp", scatter_dimension=0, tiled=True
        ).astype(jnp.float32),
        lax.psum_scatter(
            d_gain_attn_in.astype(jnp.bfloat16), "fsdp", scatter_dimension=0, tiled=True
        ).astype(jnp.float32),
        lax.psum_scatter(
            d_gain_attn_out.astype(jnp.bfloat16), "fsdp", scatter_dimension=0, tiled=True
        ).astype(jnp.float32),
        lax.psum_scatter(
            d_gain_ffn_in.astype(jnp.bfloat16), "fsdp", scatter_dimension=0, tiled=True
        ).astype(jnp.float32),
        lax.psum_scatter(
            d_gain_ffn_out.astype(jnp.bfloat16), "fsdp", scatter_dimension=0, tiled=True
        ).astype(jnp.float32),
        lax.psum_scatter(
            d_gain_query.astype(jnp.bfloat16), "fsdp", scatter_dimension=0, tiled=True
        ).astype(jnp.float32),
        lax.psum_scatter(
            d_gain_key.astype(jnp.bfloat16), "fsdp", scatter_dimension=0, tiled=True
        ).astype(jnp.float32),
    )
    totals = (
        lax.psum(shared[0].astype(jnp.bfloat16), "ctx").astype(jnp.float32),
        lax.psum(shared[1].astype(jnp.bfloat16), "ctx").astype(jnp.float32),
        lax.psum(shared[2].astype(jnp.bfloat16), "ctx").astype(jnp.float32),
        lax.psum(shared[3].astype(jnp.bfloat16), "ctx").astype(jnp.float32),
        lax.psum(grad_in, "ctx").astype(jnp.float32),
        lax.psum(grad_down, "ctx").astype(jnp.float32),
        lax.psum(shared[4].astype(jnp.bfloat16), "ctx").astype(jnp.float32),
        lax.psum(shared[5].astype(jnp.bfloat16), "ctx").astype(jnp.float32),
        lax.psum(shared[6].astype(jnp.bfloat16), "ctx").astype(jnp.float32),
        lax.psum(shared[7].astype(jnp.bfloat16), "ctx").astype(jnp.float32),
        lax.psum(shared[8].astype(jnp.bfloat16), "ctx").astype(jnp.float32),
        lax.psum(shared[9].astype(jnp.bfloat16), "ctx").astype(jnp.float32),
    )
    return (
        block_out,
        grad_tokens,
        totals[0],
        totals[1],
        totals[2],
        totals[3],
        totals[4],
        totals[5],
        totals[6],
        totals[7],
        totals[8],
        totals[9],
        totals[10],
        totals[11],
    )


def solution(mesh):
    in_specs = (
        P(("ctx", "fsdp"), None),
        P(("ctx", "fsdp"), None),
        P(),
        P(),
        P("fsdp", None),
        P("fsdp", None),
        P("fsdp", None),
        P("fsdp", None),
        P("fsdp", None, None),
        P("fsdp", None),
        P("fsdp"),
        P("fsdp"),
        P("fsdp"),
        P("fsdp"),
        P("fsdp"),
        P("fsdp"),
    )
    out_specs = (
        P(("ctx", "fsdp"), None),
        P(("ctx", "fsdp"), None),
        P("fsdp", None),
        P("fsdp", None),
        P("fsdp", None),
        P("fsdp", None),
        P("fsdp", None, None),
        P("fsdp", None),
        P("fsdp"),
        P("fsdp"),
        P("fsdp"),
        P("fsdp"),
        P("fsdp"),
        P("fsdp"),
    )
    return jax.shard_map(body, mesh=mesh, in_specs=in_specs, out_specs=out_specs, check_vma=False)
```

profile of v0, /device:TPU:1, one launch (start us, length us, event | category | flops | bytes accessed | tf_op | source)
XLA Modules:
  0.0 1820.9 jit_solution(3403862448025064748)
XLA Ops:
  15.8 11.7 all-reduce.19
  33.4 8.8 all_gather.48
  75.1 36.0 %select_multiply_fusion.2 = s32[4096]{0:T(1024)S(1)} fusion(pred[4096]{0:T(1024)(128)(4,1)S(1)} %compare_reduce_fusion.114, pred[4096]{0:T(1024)(128)(4,1)S(1)} %compare_reduce_fusion.115, pred[4096]{0:T(1024)(128)(4,1)S(1)} %compare_reduce_fusion.116, pred[4096]{0:T(1024)(128)(4,1)S(1)} %compare_reduce_fusion.117, ...), kind=kLoop, calls=%fused_computation.405 | loop fusion | flops 237568 | bytes 266468 | tf_op jit(solution)/shard_map/mul | solution.py:35
  111.2 23.2 %gather_fusion.4 = s32[4096]{0:T(1024)S(1)} fusion(s32[4096]{0:T(1024)S(1)} %copy-done, s32[4096]{0:T(1024)S(1)} %broadcast_clamp_fusion.2), kind=kCustom, calls=%fused_computation.4 | custom fusion | bytes 49152 | tf_op jit(solution)/shard_map/gather | solution.py:37
  146.9 15.6 all-gather.7.cloned.1.call-done
  162.5 182.4 %while.30 = (s32[]{:T(128)}, f32[128,4,256]{0,2,1:T(8,128)S(1)}, f32[128,4,256]{0,2,1:T(8,128)S(1)}, bf16[2,2048,256]{2,1,0:T(8,128)(2,1)}, s32[2]{0:T(128)S(1)}...) while((s32[]{:T(128)}, f32[128,4,256]{0,2,1:T(8,128)S(1)}, ...), condition=%wide.region_8.9_spmd.clone, body=%wide.region_6.8_spmd.clone.sunk | while | flops 1621817344 | bytes 44154988 | solution.py:57
  192.8 36.0 %select_multiply_fusion.5 = s32[2048]{0:T(1024)S(1)} fusion(pred[2048]{0:T(1024)(128)(4,1)S(1)} %get-tuple-element.1441, pred[2048]{0:T(1024)(128)(4,1)S(1)} %get-tuple-element.1442, pred[2048]{0:T(1024)(128)(4,1)S(1)} %get-tuple-element.1443, pred[2048]{0:T(1024)(128)(4,1)S(1)} %get-tuple-element.1444, pred[2048]{0:T(1024)(128)(4,1)S(1)} %get-tuple-element.1445, ...), kind=kLoop, calls=%fused_computation.102.clone.1 | loop fusion | flops 118784 | bytes 133348 | tf_op jit(solution)/shard_map/while/body/eval_jaxpr/mul | solution.py:35
  229.5 11.8 gather_fusion
  283.9 35.9 %select_multiply_fusion.5 = s32[2048]{0:T(1024)S(1)} fusion(pred[2048]{0:T(1024)(128)(4,1)S(1)} %get-tuple-element.1441, pred[2048]{0:T(1024)(128)(4,1)S(1)} %get-tuple-element.1442, pred[2048]{0:T(1024)(128)(4,1)S(1)} %get-tuple-element.1443, pred[2048]{0:T(1024)(128)(4,1)S(1)} %get-tuple-element.1444, pred[2048]{0:T(1024)(128)(4,1)S(1)} %get-tuple-element.1445, ...), kind=kLoop, calls=%fused_computation.102.clone.1 | loop fusion | flops 118784 | bytes 133348 | tf_op jit(solution)/shard_map/while/body/eval_jaxpr/mul | solution.py:35
  320.6 11.8 gather_fusion
  347.9 32.9 %all-gather.15.cloned.1.call-done = bf16[1152,2,6912]{2,0,1:T(8,128)(2,1)} async-done(((bf16[288,2,6912]{2,0,1:T(8,128)(2,1)}), bf16[1152,2,6912]{2,0,1:T(8,128)(2,1)}) %all-gather.15.cloned.1.call-update) | async-done | bytes 31850512 | tf_op jit(solution)/shard_map/all_gather | solution.py:186
  380.7 19.4 %fusion.100 = f32[128,2,6912]{2,0,1:T(8,128)} fusion(bf16[1152,2,6912]{2,0,1:T(8,128)(2,1)} %all-gather.15.cloned.1.call-done, f32[128,1152]{1,0:T(8,128)S(1)} %get-tuple-element.722, f32[1152]{0:T(1024)S(1)} %convert_element_type.225, f32[128]{0:T(128)S(1)} %fusion.112), kind=kOutput, calls=%fused_computation.414 | convolution fusion | flops 4077305856 | bytes 39523328 | tf_op jit(solution)/shard_map/td,dkf->tkf/dot_general | solution.py:183
  404.6 78.7 %all-gather.17.cloned.1.call-done = bf16[6912,1152]{1,0:T(8,128)(2,1)} async-done(((bf16[1728,1152]{1,0:T(8,128)(2,1)}), bf16[6912,1152]{1,0:T(8,128)(2,1)}) %all-gather.17.cloned.1.call-update) | async-done | bytes 15925264 | tf_op jit(solution)/shard_map/all_gather | solution.py:198
  493.3 10.4 fusion.59
  503.7 16.0 multiply_reduce_fusion
  522.8 201.7 %while.31 = (s32[]{:T(128)}, f32[128,4,256]{0,2,1:T(8,128)}, f32[2,2048,512]{2,1,0:T(8,128)}, bf16[2,2048,256]{2,1,0:T(8,128)(2,1)}, s32[2]{0:T(128)S(1)}, /*ind...) while((s32[]{:T(128)}, f32[128,4,256]{0,2,1:T(8,128)}, ...), condition=%wide.region_18.19_spmd.clone, body=%wide.region_16.18_spmd.clone.sunk | while | flops 2695297024 | bytes 111004016 | solution.py:57
  553.1 35.2 %select_multiply_fusion.6 = s32[2048]{0:T(1024)S(1)} fusion(pred[2048]{0:T(1024)(128)(4,1)S(1)} %get-tuple-element.1575, pred[2048]{0:T(1024)(128)(4,1)S(1)} %get-tuple-element.1576, pred[2048]{0:T(1024)(128)(4,1)S(1)} %get-tuple-element.1577, pred[2048]{0:T(1024)(128)(4,1)S(1)} %get-tuple-element.1578, pred[2048]{0:T(1024)(128)(4,1)S(1)} %get-tuple-element.1579, ...), kind=kLoop, calls=%fused_computation.209.clone.1 | loop fusion | flops 118784 | bytes 133348 | tf_op jit(solution)/shard_map/while/body/eval_jaxpr/mul | solution.py:35
  589.0 11.8 gather_fusion.1
  653.9 35.2 %select_multiply_fusion.6 = s32[2048]{0:T(1024)S(1)} fusion(pred[2048]{0:T(1024)(128)(4,1)S(1)} %get-tuple-element.1575, pred[2048]{0:T(1024)(128)(4,1)S(1)} %get-tuple-element.1576, pred[2048]{0:T(1024)(128)(4,1)S(1)} %get-tuple-element.1577, pred[2048]{0:T(1024)(128)(4,1)S(1)} %get-tuple-element.1578, pred[2048]{0:T(1024)(128)(4,1)S(1)} %get-tuple-element.1579, ...), kind=kLoop, calls=%fused_computation.209.clone.1 | loop fusion | flops 118784 | bytes 133348 | tf_op jit(solution)/shard_map/while/body/eval_jaxpr/mul | solution.py:35
  689.8 11.8 gather_fusion.1
  733.3 134.1 %reduce-scatter.8.cloned.1.call-done = f32[128,512]{1,0:T(8,128)} async-done(((f32[4096,512]{1,0:T(8,128)}), f32[128,512]{1,0:T(8,128)}) %reduce-scatter.8.cloned.1.call-update) | async-done | bytes 262160 | tf_op jit(solution)/shard_map/reduce_scatter | solution.py:275
  872.5 8.4 convolution_convert_fusion.1
  882.5 15.5 convolution_convert_fusion
  905.1 35.8 %reduce-scatter.16.cloned.1.call-done = bf16[256,1152]{1,0:T(8,128)(2,1)} async-done(((bf16[1024,1152]{1,0:T(8,128)(2,1)}), bf16[256,1152]{1,0:T(8,128)(2,1)}) %reduce-scatter.16.cloned.1.call-update) | async-done | bytes 589840 | tf_op jit(solution)/shard_map/reduce_scatter | solution.py:300
  940.8 24.4 %reduce-scatter.12.cloned.1.call-done = bf16[288,256]{1,0:T(8,128)(2,1)} async-done(((bf16[1152,256]{1,0:T(8,128)(2,1)}), bf16[288,256]{1,0:T(8,128)(2,1)}) %reduce-scatter.12.cloned.1.call-update) | async-done | bytes 147472 | tf_op jit(solution)/shard_map/reduce_scatter | solution.py:294
  965.3 24.6 %reduce-scatter.14.cloned.1.call-done = bf16[288,256]{1,0:T(8,128)(2,1)} async-done(((bf16[1152,256]{1,0:T(8,128)(2,1)}), bf16[288,256]{1,0:T(8,128)(2,1)}) %reduce-scatter.14.cloned.1.call-update) | async-done | bytes 147472 | tf_op jit(solution)/shard_map/reduce_scatter | solution.py:297
  989.9 124.2 %reduce-scatter.20.cloned.1.call-done = bf16[1728,1152]{1,0:T(8,128)(2,1)} async-done(((bf16[6912,1152]{1,0:T(8,128)(2,1)}), bf16[1728,1152]{1,0:T(8,128)(2,1)}) %reduce-scatter.20.cloned.1.call-update) | async-done | bytes 3981328 | tf_op jit(solution)/shard_map/reduce_scatter | solution.py:215
  1114.0 227.8 %reduce-scatter.18.cloned.1.call-done = bf16[288,2,6912]{2,0,1:T(8,128)(2,1)} async-done(((bf16[1152,2,6912]{2,0,1:T(8,128)(2,1)}), bf16[288,2,6912]{2,0,1:T(8,128)(2,1)}) %reduce-scatter.18.cloned.1.call-update) | async-done | bytes 7962640 | tf_op jit(solution)/shard_map/reduce_scatter | solution.py:224
  1346.8 10.8 all-reduce.18
  1358.1 19.2 %all-reduce.16 = (bf16[288]{0:T(512)(128)(2,1)S(1)}, bf16[288]{0:T(512)(128)(2,1)S(1)}, bf16[288]{0:T(512)(128)(2,1)S(1)}, bf16[288]{0:T(512)(128)(2,1)S(1)}, bf...) all-reduce(bf16[288]{0:T(512)(128)(2,1)S(1)} %dynamic-slice.7, ...), channel_id=1, replica_groups=mesh['ctx'=8,'fsdp'=4] {'ctx'}, use_global_device_ids=true, to_apply=%region_37.38 | all-reduce | flops 1280 | bytes 5120 | tf_op jit(solution)/shard_map/psum | solution.py:329
  1381.7 388.6 %all-reduce.22.cloned.1.call-done = (bf16[288,2,6912]{2,0,1:T(8,128)(2,1)}, bf16[288,1024]{1,0:T(8,128)(2,1)}, bf16[288,256]{1,0:T(8,128)(2,1)}, bf16[288,256]{1...) async-done(((bf16[288,2,6912]{2,0,1:T(8,128)(2,1)}, bf16[288,1024]{1,0:T(8,128)(2,1)}, bf16[288,256]{1,0:T(8,128)(2,1)}, ...) | async-done | bytes 13418512 | tf_op jit(solution)/shard_map/psum | solution.py:327
  1777.9 32.5 %copy.140 = f32[288,2,6912]{2,1,0:T(2,128)} copy(bf16[288,2,6912]{2,0,1:T(8,128)(2,1)} %get-tuple-element.702) | data formatting | bytes 23887872
  (565 shorter events, 314.0 us)
Async XLA Ops:
  7.2 47.5 %copy-start.13 = (bf16[128,1152]{1,0:T(8,128)(2,1)S(1)}, bf16[128,1152]{1,0:T(8,128)(2,1)}, u32[]{:S(2)}) copy-start(bf16[128,1152]{1,0:T(8,128)(2,1)} %param.20) | copy-start | bytes 884740
  7.2 39.0 %copy-start.51 = (bf16[288,256]{1,0:T(8,128)(2,1)S(1)}, bf16[288,256]{1,0:T(8,128)(2,1)}, u32[]{:S(2)}) copy-start(bf16[288,256]{1,0:T(8,128)(2,1)} %param.26) | copy-start | bytes 442372
  7.2 129.3 %all-gather.11.cloned.1.call-start = ((), (), s32[]{:S(2)}) async-start(), calls=%async_computation.9 | async-start | bytes 2949120 | tf_op jit(solution)/shard_map/all_gather | solution.py:95
  7.9 134.2 %all-gather.9.cloned.1.call-start = ((), (), s32[]{:S(2)}) async-start(), calls=%async_computation.8 | async-start | bytes 2162688 | tf_op jit(solution)/shard_map/all_gather | solution.py:145
  27.5 109.0 %copy-start.49 = (f32[1152]{0:T(1024)}, f32[1152]{0:T(1024)S(1)}, u32[]{:S(2)}) copy-start(f32[1152]{0:T(1024)S(1)} %convert_element_type.215) | copy-start | bytes 13828
  42.9 93.6 %copy-start.56 = (f32[128]{0:T(128)}, f32[128]{0:T(128)S(1)}, u32[]{:S(2)}) copy-start(f32[128]{0:T(128)S(1)} %fusion.109) | copy-start | bytes 1540
  45.5 94.1 %copy-start.42 = (f32[128,128]{1,0:T(8,128)}, f32[128,128]{1,0:T(8,128)S(1)}, u32[]{:S(2)}) copy-start(f32[128,128]{1,0:T(8,128)S(1)} %get-tuple-element.977) | copy-start | bytes 196612
  45.5 94.1 %copy-start.44 = (f32[128,128]{1,0:T(8,128)}, f32[128,128]{1,0:T(8,128)S(1)}, u32[]{:S(2)}) copy-start(f32[128,128]{1,0:T(8,128)S(1)} %get-tuple-element.978) | copy-start | bytes 196612
  46.2 116.3 %all-gather.7.cloned.1.call-start = ((), (), s32[]{:S(2)}) async-start(), calls=%async_computation.7 | async-start | bytes 2162688 | tf_op jit(solution)/shard_map/all_gather | solution.py:146
  55.6 289.3 %all-gather.13.cloned.1.call-start = ((), (), s32[]{:S(2)}) async-start(), calls=%async_computation.10 | async-start | bytes 2949120 | tf_op jit(solution)/shard_map/all_gather | solution.py:98
  56.2 324.5 %all-gather.15.cloned.1.call-start = ((), (), s32[]{:S(2)}) async-start(), calls=%async_computation.11 | async-start | bytes 39813120 | tf_op jit(solution)/shard_map/all_gather | solution.py:186
  63.6 47.6 %copy-start = (s32[4096]{0:T(1024)S(1)}, s32[4096]{0:T(1024)}, u32[]{:S(2)}) copy-start(s32[4096]{0:T(1024)} %param.23) | copy-start | bytes 49156
  63.6 419.6 %all-gather.17.cloned.1.call-start = ((), (), s32[]{:S(2)}) async-start(), calls=%async_computation.12 | async-start | bytes 19906560 | tf_op jit(solution)/shard_map/all_gather | solution.py:198
  64.2 803.2 %reduce-scatter.8.cloned.1.call-start = ((), (), s32[]{:S(2)}) async-start(), calls=%async_computation.13 | async-start | bytes 8650752 | tf_op jit(solution)/shard_map/reduce_scatter | solution.py:275
  64.3 75.1 %copy-start.61 = (f32[256]{0:T(256)}, f32[256]{0:T(256)S(1)}, u32[]{:S(2)}) copy-start(f32[256]{0:T(256)S(1)} %convert_element_type.221) | copy-start | bytes 3076
  404.6 86.9 %copy-start.8 = (bf16[128,6912]{1,0:T(8,128)(2,1)}, bf16[128,6912]{1,0:T(8,128)(2,1)S(1)}, u32[]{:S(2)}) copy-start(bf16[128,6912]{1,0:T(8,128)(2,1)S(1)} %multiply_convert_fusion.1) | copy-start | bytes 5308420
  724.6 180.4 %reduce-scatter.10.cloned.1.call-start = ((), (), s32[]{:S(2)}) async-start(), calls=%async_computation.14 | async-start | bytes 2949120 | tf_op jit(solution)/shard_map/reduce_scatter | solution.py:291
  730.7 136.7 %copy-start.66 = (f32[128]{0:T(128)S(1)}, f32[128]{0:T(128)}, u32[]{:S(2)}) copy-start(f32[128]{0:T(128)} %copy-done.65) | copy-start | bytes 1540
  730.8 136.7 %copy-start.68 = (f32[128]{0:T(128)S(1)}, f32[128]{0:T(128)}, u32[]{:S(2)}) copy-start(f32[128]{0:T(128)} %copy-done.67) | copy-start | bytes 1540
  730.8 137.9 %copy-start.39 = (f32[128,256]{1,0:T(8,128)S(1)}, f32[128,256]{1,0:T(8,128)}, u32[]{:S(2)}) copy-start(f32[128,256]{1,0:T(8,128)} %copy-done.38) | copy-start | bytes 393220
  730.8 137.9 %copy-start.60 = (f32[256]{0:T(256)S(1)}, f32[256]{0:T(256)}, u32[]{:S(2)}) copy-start(f32[256]{0:T(256)} %copy-done.59) | copy-start | bytes 3076
  730.8 137.9 %copy-start.64 = (f32[128]{0:T(128)S(1)}, f32[128]{0:T(128)}, u32[]{:S(2)}) copy-start(f32[128]{0:T(128)} %copy-done.63) | copy-start | bytes 1540
  730.8 138.0 %copy-start.72 = (f32[128]{0:T(128)S(1)}, f32[128]{0:T(128)}, u32[]{:S(2)}) copy-start(f32[128]{0:T(128)} %copy-done.71) | copy-start | bytes 1540
  730.8 210.0 %reduce-scatter.16.cloned.1.call-start = ((), (), s32[]{:S(2)}) async-start(), calls=%async_computation.17 | async-start | bytes 2949120 | tf_op jit(solution)/shard_map/reduce_scatter | solution.py:300
  733.3 139.3 %copy-start.9 = (bf16[128,6912]{1,0:T(8,128)(2,1)S(1)}, bf16[128,6912]{1,0:T(8,128)(2,1)}, u32[]{:S(2)}) copy-start(bf16[128,6912]{1,0:T(8,128)(2,1)} %copy-done.8) | copy-start | bytes 5308420
  733.3 139.3 %copy-start.41 = (bf16[128,1152]{1,0:T(8,128)(2,1)S(1)}, bf16[128,1152]{1,0:T(8,128)(2,1)}, u32[]{:S(2)}) copy-start(bf16[128,1152]{1,0:T(8,128)(2,1)} %copy-done.40) | copy-start | bytes 884740
  733.3 232.0 %reduce-scatter.12.cloned.1.call-start = ((), (), s32[]{:S(2)}) async-start(), calls=%async_computation.15 | async-start | bytes 737280 | tf_op jit(solution)/shard_map/reduce_scatter | solution.py:294
  870.2 119.6 %reduce-scatter.14.cloned.1.call-start = ((), (), s32[]{:S(2)}) async-start(), calls=%async_computation.16 | async-start | bytes 737280 | tf_op jit(solution)/shard_map/reduce_scatter | solution.py:297
  872.5 241.6 %reduce-scatter.20.cloned.1.call-start = ((), (), s32[]{:S(2)}) async-start(), calls=%async_computation.19 | async-start | bytes 19906560 | tf_op jit(solution)/shard_map/reduce_scatter | solution.py:215
  880.9 460.9 %reduce-scatter.18.cloned.1.call-start = ((), (), s32[]{:S(2)}) async-start(), calls=%async_computation.18 | async-start | bytes 39813120 | tf_op jit(solution)/shard_map/reduce_scatter | solution.py:224
  898.0 872.3 %all-reduce.22.cloned.1.call-start = ((), (), s32[]{:S(2)}) async-start(), calls=%async_computation.20 | async-start | bytes 26836992 | tf_op jit(solution)/shard_map/psum | solution.py:327
  1343.3 37.3 %copy-start.25 = (f32[128,1152]{1,0:T(8,128)S(1)}, f32[128,1152]{1,0:T(8,128)}, u32[]{:S(2)}) copy-start(f32[128,1152]{1,0:T(8,128)} %copy-done.24) | copy-start | bytes 1769476
  (69 other events, 509.6 us)
Sparse Core Ops, SparseCore 0:
  9.6 26.8 all-gather.10
  46.3 57.4 all-gather.8
  107.2 55.2 all-gather.6
  163.9 22.8 all-gather.12
  188.8 191.8 all-gather.14
  382.1 101.0 all-gather.16
  724.7 142.6 reduce-scatter.7
  870.5 34.4 reduce-scatter.9
  907.8 33.0 reduce-scatter.15
  943.2 22.0 reduce-scatter.11
  967.8 22.0 reduce-scatter.13
  992.9 121.0 reduce-scatter.19
  1116.8 224.9 reduce-scatter.17
  1347.1 423.0 all-reduce.21
where the time goes:
time: 1830 us; the launch traced here: 1820 us
  waiting for transfers between devices  1100 us (60%)
  other arithmetic  349 us (19%)
  local copies, waits for them, and re-layouts  170 us (9%)
  matrix products  128 us (7%)
  blocking collectives  58.2 us (3%)
    psum x1, waiting for transfers between devices, body(): lax.psum(grad_in, 'ctx').astype(jnp.float32)  389 us
    reduce_scatter x1, waiting for transfers between devices, body(): lax.psum_scatter(jnp.einsum('td,tkf->dkf', columns, d_gate_up, preferred_...  228 us
    mul x5, other arithmetic, place_rows(): block_table[layout_rows // half_block] * half_block  178 us
    reduce_scatter x1, waiting for transfers between devices, body(): lax.psum_scatter(key_terms, ('ctx', 'fsdp'), scatter_dimension=0, tiled=T...  134 us
    reduce_scatter x1, waiting for transfers between devices, body(): lax.psum_scatter(jnp.einsum('tf,td->fd', columns, d_ffn_low, preferred_el...  124 us
    gather x179, other arithmetic, place_rows(): block_table[layout_rows // half_block] * half_block  115 us
    all_gather x1, waiting for transfers between devices, body(): lax.all_gather(w_down, 'fsdp', axis=0, tiled=True)  78.7 us
    gather x6, local copies, waits for them, and re-layouts, place_rows(): sequence = sequence_ids[stream]  72 us
  transfers between devices with their start and end apart: 14, of which 11 were waited for; matrix products, arithmetic and copies ran while one was open for 20% of the time, Pallas kernels for 0%

commit v1 on v0

v1 whole, which is shorter than its diff:
```python
import functools
import math

import jax
import jax.numpy as jnp
from jax import lax
from jax.experimental import pallas as pl
from jax.experimental.pallas import tpu as pltpu
from jax.sharding import PartitionSpec as P

H = 4
HD = 256
EPS = 1e-06
AXES = ("ctx", "fsdp")
BF = jnp.bfloat16
F32 = jnp.float32
KEY_BLOCK = 512


def rms_norm(values, scaling):
    return values * lax.rsqrt(jnp.mean(values * values, axis=-1, keepdims=True) + EPS) * scaling


def rotate(values, cosine, sine):
    half_width = values.shape[-1] // 2
    first_half = values[..., :half_width]
    second_half = values[..., half_width:]
    return jnp.concatenate(
        [first_half * cosine - second_half * sine, second_half * cosine + first_half * sine],
        axis=-1,
    )


def after(value, *earlier):
    return lax.optimization_barrier((value, *earlier))[0]


def swap(value, offset):
    count = lax.axis_size("ctx") * lax.axis_size("fsdp")
    return lax.ppermute(value, AXES, [(i, i ^ offset) for i in range(count)])


def join(*parts):
    return jnp.concatenate(parts, axis=0)


def gather_group(value):
    pair = join(value, swap(value, 2))
    return join(pair, swap(pair, 1))


def scatter_group(terms):
    half = terms.shape[0] // 2
    pair = terms[:half] + swap(terms[half:].astype(BF), 1).astype(F32)
    quarter = half // 2
    return pair[:quarter] + swap(pair[quarter:].astype(BF), 2).astype(F32)


def wide_offsets():
    highs = [8 * s for s in range(lax.axis_size("ctx") // 2)]
    chip = [low + high for low in (0, 4, 2, 6) for high in highs]
    return chip + [1 + o for o in chip]


def gather_wide(value):
    highs = lax.axis_size("ctx") // 2
    line = join(value, *[swap(value, 8 * s) for s in range(1, highs)])
    half = line.shape[0] // 2
    along_y, along_x = swap(line, 4), swap(line, 2)
    corner = (swap(along_y[:half], 2), swap(along_x[half:], 4))
    chip = join(line, along_y, along_x, *corner)
    return join(chip, swap(chip, 1))


def scatter_wide(terms):
    highs = lax.axis_size("ctx") // 2
    half = terms.shape[0] // 2
    chip = terms[:half].astype(F32) + swap(terms[half:], 1).astype(F32)
    line, along_y, along_x, corner = jnp.split(chip, 4, axis=0)
    mid = line.shape[0] // 2
    corner = corner.astype(BF)
    from_x, from_y = swap(corner[:mid], 2), swap(corner[mid:], 4)
    along_y = join(along_y[:mid] + from_x.astype(F32), along_y[mid:])
    along_x = join(along_x[:mid], along_x[mid:] + from_y.astype(F32))
    line = (
        line
        + swap(along_y.astype(BF), 4).astype(F32)
        + swap(along_x.astype(BF), 2).astype(F32)
    )
    rows = line.shape[0] // highs
    total = line[:rows]
    for s in range(1, highs):
        total = total + swap(line[s * rows : (s + 1) * rows].astype(BF), 8 * s).astype(F32)
    return total


def sum_over_ctx(value):
    count, me = lax.axis_size("ctx"), lax.axis_index("ctx")
    highs, low, high = count // 2, me % 2, me // 2
    rows, columns = value.shape
    parts = value.reshape(highs, 2, rows // count, columns)
    line = lax.dynamic_index_in_dim(parts, low, 1, keepdims=False) + swap(
        lax.dynamic_index_in_dim(parts, 1 - low, 1, keepdims=False).astype(BF), 4
    ).astype(F32)
    total = lax.dynamic_index_in_dim(line, high, 0, keepdims=False)
    line_low = line.astype(BF)
    for s in range(1, highs):
        total = total + swap(
            lax.dynamic_index_in_dim(line_low, high ^ s, 0, keepdims=False), 8 * s
        ).astype(F32)
    total = total.astype(BF)
    line = jnp.zeros(line_low.shape, BF)
    for s in range(highs):
        piece = total if s == 0 else swap(total, 8 * s)
        line = lax.dynamic_update_index_in_dim(line, piece, high ^ s, 0)
    other = swap(line, 4)
    even, odd = jnp.where(low == 0, line, other), jnp.where(low == 0, other, line)
    return jnp.stack([even, odd], axis=1).reshape(rows, columns).astype(F32)


def in_place(pieces, me, axis):
    size = pieces[0].shape[axis]
    shape = list(pieces[0].shape)
    shape[axis] = size * len(pieces)
    out = jnp.zeros(shape, pieces[0].dtype)
    for offset, piece in enumerate(pieces):
        out = lax.dynamic_update_slice_in_dim(out, piece, (me ^ offset) * size, axis)
    return out


def gather_rows(value, me):
    pair = join(value, swap(value, 2))
    other = swap(pair, 1)
    rows = value.shape[0]
    return in_place([value, other[:rows], pair[rows:], other[rows:]], me, 0)


def scatter_rows(value, me):
    rows = value.shape[0] // 4
    return scatter_group(
        join(*[lax.dynamic_slice_in_dim(value, (me ^ o) * rows, rows, 0) for o in (0, 2, 1, 3)])
    )


def attend_kernel(blocks, q, q_place, q_start, k, v, probs, heads, mass):
    step = pl.program_id(0)

    @pl.when(step == 0)
    def _():
        heads[...] = jnp.zeros_like(heads)
        mass[...] = jnp.zeros_like(mass)

    scores = lax.dot_general(
        k[...], q[...], (((1,), (1,)), ((), ())), preferred_element_type=F32
    )
    rows = k.shape[0]
    block = 64
    place, start = q_place[...], q_start[...]
    total = jnp.zeros_like(mass)
    for i in range(rows // block):
        first = blocks[step * (rows // block) + i] * block
        keys = first + lax.broadcasted_iota(jnp.int32, (block, scores.shape[1]), 0)
        allowed = (keys <= place) & (keys >= start)
        weights = jnp.where(allowed, jnp.exp(scores[i * block : (i + 1) * block]), 0.0)
        probs[i * block : (i + 1) * block, :] = weights.astype(BF)
        total = total + jnp.sum(weights, axis=0, keepdims=True)
    mass[...] += total
    heads[...] += lax.dot_general(
        v[...], probs[...], (((0,), (0,)), ((), ())), preferred_element_type=F32
    )


def attend(blocks, queries, q_place, q_start, pairs):
    head_rows = queries.shape[0]
    keys = pairs.shape[0]
    return pl.pallas_call(
        attend_kernel,
        grid_spec=pltpu.PrefetchScalarGridSpec(
            num_scalar_prefetch=1,
            grid=(keys // KEY_BLOCK,),
            in_specs=[
                pl.BlockSpec((head_rows, HD), lambda i, b: (0, 0)),
                pl.BlockSpec((1, head_rows), lambda i, b: (0, 0)),
                pl.BlockSpec((1, head_rows), lambda i, b: (0, 0)),
                pl.BlockSpec((KEY_BLOCK, HD), lambda i, b: (i, 0)),
                pl.BlockSpec((KEY_BLOCK, HD), lambda i, b: (i, 1)),
            ],
            out_specs=[
                pl.BlockSpec((KEY_BLOCK, head_rows), lambda i, b: (i, 0)),
                pl.BlockSpec((HD, head_rows), lambda i, b: (0, 0)),
                pl.BlockSpec((1, head_rows), lambda i, b: (0, 0)),
            ],
        ),
        out_shape=[
            jax.ShapeDtypeStruct((keys, head_rows), BF),
            jax.ShapeDtypeStruct((HD, head_rows), F32),
            jax.ShapeDtypeStruct((1, head_rows), F32),
        ],
        compiler_params=pltpu.CompilerParams(vmem_limit_bytes=32 * 2**20),
        cost_estimate=pl.CostEstimate(
            flops=4 * keys * head_rows * HD,
            bytes_accessed=keys * (head_rows + 2 * HD) * 2,
            transcendentals=keys * head_rows,
        ),
        name="attend",
    )(blocks, queries, q_place, q_start, pairs, pairs)


def attend_back_kernel(q, d_heads, inverse, dots, probs, k, v, d_queries, d_pairs):
    @pl.when(pl.program_id(0) == 0)
    def _():
        d_queries[...] = jnp.zeros_like(d_queries)

    d_probs = lax.dot_general(
        v[...], d_heads[...], (((1,), (1,)), ((), ())), preferred_element_type=F32
    )
    chance = probs[...].astype(F32) * inverse[...]
    d_scores = (chance * (d_probs - dots[...])).astype(BF)
    d_pairs[:, :HD] = jnp.dot(d_scores, q[...], preferred_element_type=F32).astype(BF)
    d_pairs[:, HD:] = jnp.dot(
        chance.astype(BF), d_heads[...], preferred_element_type=F32
    ).astype(BF)
    d_queries[...] += lax.dot_general(
        k[...], d_scores, (((0,), (0,)), ((), ())), preferred_element_type=F32
    )


def attend_back(queries, d_heads, inverse, dots, probs, pairs):
    head_rows = queries.shape[0]
    keys = pairs.shape[0]
    whole = pl.BlockSpec((head_rows, HD), lambda i: (0, 0))
    line = pl.BlockSpec((1, head_rows), lambda i: (0, 0))
    return pl.pallas_call(
        attend_back_kernel,
        grid=(keys // KEY_BLOCK,),
        in_specs=[
            whole,
            whole,
            line,
            line,
            pl.BlockSpec((KEY_BLOCK, head_rows), lambda i: (i, 0)),
            pl.BlockSpec((KEY_BLOCK, HD), lambda i: (i, 0)),
            pl.BlockSpec((KEY_BLOCK, HD), lambda i: (i, 1)),
        ],
        out_specs=[
            pl.BlockSpec((HD, head_rows), lambda i: (0, 0)),
            pl.BlockSpec((KEY_BLOCK, 2 * HD), lambda i: (i, 0)),
        ],
        out_shape=[
            jax.ShapeDtypeStruct((HD, head_rows), F32),
            jax.ShapeDtypeStruct((keys, 2 * HD), BF),
        ],
        compiler_params=pltpu.CompilerParams(vmem_limit_bytes=32 * 2**20),
        cost_estimate=pl.CostEstimate(
            flops=8 * keys * head_rows * HD,
            bytes_accessed=keys * (head_rows + 4 * HD) * 2,
            transcendentals=0,
        ),
        name="attend_back",
    )(queries, d_heads, inverse, dots, probs, pairs, pairs)


def left_of(owner, part):
    return pl.multiple_of(owner * part - part % 128 * (owner % 2), 128)


def carve_kernel(part, mine, w, *outs):
    wide = outs[0].shape[2]
    for offset, out in enumerate(outs):
        out[...] = w[:, :, pl.ds(left_of(mine[0] ^ offset, part), wide)]


def carve(w, mine, part, wide):
    rows, step = w.shape[1], 48
    return pl.pallas_call(
        functools.partial(carve_kernel, part),
        grid_spec=pltpu.PrefetchScalarGridSpec(
            num_scalar_prefetch=1,
            grid=(rows // step,),
            in_specs=[pl.BlockSpec((2, step, w.shape[2]), lambda i, m: (0, i, 0))],
            out_specs=[pl.BlockSpec((2, step, wide), lambda i, m: (0, i, 0))] * 4,
        ),
        out_shape=[jax.ShapeDtypeStruct((2, rows, wide), BF)] * 4,
        compiler_params=pltpu.CompilerParams(vmem_limit_bytes=32 * 2**20),
        name="carve",
    )(mine[None], w)


def lay_kernel(places, own, core, x2, y2, x3, y3, out):
    step = pl.program_id(0)
    for i, source in enumerate((own, own, core, core, x2, y2, x3, y3)):

        @pl.when(step == i)
        def _(source=source):
            out[...] = source[...]


def lay(places, own, core, x2, y2, x3, y3):
    half, wide = x2.shape[1], x2.shape[2]
    shape = (2, half, wide)
    still = pl.BlockSpec(shape, lambda i, p: (0, 0, 0))
    return pl.pallas_call(
        lay_kernel,
        grid_spec=pltpu.PrefetchScalarGridSpec(
            num_scalar_prefetch=1,
            grid=(8,),
            in_specs=[
                pl.BlockSpec(shape, lambda i, p: (0, jnp.minimum(i, 1), 0)),
                pl.BlockSpec(shape, lambda i, p: (0, jnp.clip(i - 2, 0, 1), 0)),
            ]
            + [still] * 4,
            out_specs=pl.BlockSpec(shape, lambda i, p: (0, p[i], 0)),
        ),
        out_shape=jax.ShapeDtypeStruct((2, 8 * half, wide), BF),
        compiler_params=pltpu.CompilerParams(vmem_limit_bytes=32 * 2**20),
        name="lay",
    )(places, own, core, x2, y2, x3, y3)


def contract(left, right, left_dim, right_dim):
    return lax.dot_general(
        left, right, (((left_dim,), (right_dim,)), ((), ())), preferred_element_type=F32
    )


def gelu_and_slope(x):
    scale = math.sqrt(2.0 / math.pi)
    square = x * x
    turn = jnp.tanh(x * (scale + (scale * 0.044715) * square))
    share = 0.5 + 0.5 * turn
    slope = share + (0.5 * x) * (1.0 - turn * turn) * (scale + (3 * scale * 0.044715) * square)
    return x * share, slope


def ffn_kernel(mine, second, d_ffn, w_gate, w_up, w_down, *rest):
    outs, down, act, d_both, both_sum = rest[:4], *rest[4:]
    step = pl.program_id(1)
    rows, slab = second.shape[0], 256
    width = down.shape[0]

    def products(r):
        at = pl.ds(r * slab, slab)
        return (
            contract(second[at, :], w_gate[0], 1, 0),
            contract(second[at, :], w_up[0], 1, 0),
            contract(d_ffn[at, :], w_down[...], 1, 1),
        )

    ahead = products(0)
    for r in range(rows // slab):
        at = pl.ds(r * slab, slab)
        gate, upper, d_act = ahead
        if r + 1 < rows // slab:
            ahead = products(r + 1)
        value, slope = gelu_and_slope(gate)
        act[at, :] = (value * upper).astype(BF)
        d_both[at, :width] = (d_act * upper * slope).astype(BF)
        d_both[at, width:] = (d_act * value).astype(BF)
    grad_both = contract(second[...], d_both[...], 0, 0)
    grad_down = contract(act[...], d_ffn[...], 0, 0)

    @pl.when(step == 0)
    def _():
        both_sum[...] = grad_both
        down[...] = grad_down

    @pl.when(step > 0)
    def _():
        both_sum[...] += grad_both
        down[...] += grad_down

    @pl.when(step == pl.num_programs(1) - 1)
    def _():
        quarter = second.shape[1] // 4
        for offset, out in enumerate(outs):
            at = pl.ds(pl.multiple_of((mine[0] ^ offset) * quarter, 32), quarter)
            out[0] = both_sum[at, :width].astype(BF)
            out[1] = both_sum[at, width:].astype(BF)


def ffn_gradients(mine, second_all, d_ffn_all, in_mat, down_mat, first, last):
    tokens, model = second_all.shape
    slab, width = min(2048, tokens), 256
    columns = (last - first) * width
    tall = pl.BlockSpec((slab, model), lambda j, t, m: (t, 0))
    return pl.pallas_call(
        ffn_kernel,
        grid_spec=pltpu.PrefetchScalarGridSpec(
            num_scalar_prefetch=1,
            grid=(last - first, tokens // slab),
            in_specs=[
                tall,
                tall,
                pl.BlockSpec((1, model, width), lambda j, t, m: (0, 0, j + first)),
                pl.BlockSpec((1, model, width), lambda j, t, m: (1, 0, j + first)),
                pl.BlockSpec((width, model), lambda j, t, m: (j + first, 0)),
            ],
            out_specs=[pl.BlockSpec((2, model // 4, width), lambda j, t, m: (0, 0, j))] * 4
            + [pl.BlockSpec((width, model), lambda j, t, m: (j, 0))],
            scratch_shapes=[
                pltpu.VMEM((slab, width), BF),
                pltpu.VMEM((slab, 2 * width), BF),
                pltpu.VMEM((model, 2 * width), F32),
            ],
        ),
        out_shape=[jax.ShapeDtypeStruct((2, model // 4, columns), BF)] * 4
        + [jax.ShapeDtypeStruct((columns, model), F32)],
        compiler_params=pltpu.CompilerParams(vmem_limit_bytes=56 * 2**20),
        cost_estimate=pl.CostEstimate(
            flops=12 * tokens * model * columns,
            bytes_accessed=4 * tokens * model * (last - first),
            transcendentals=tokens * columns,
        ),
        name="ffn_gradients",
    )(mine[None], second_all, d_ffn_all, in_mat, in_mat, down_mat)


def unfold_kernel(part, mine, *refs):
    out, sources = refs[-1], refs[:-1]
    ranges = len(sources) // 4
    extra = part % 128
    for m in range(4):

        @pl.when(mine[0] == m)
        def _(m=m):
            for side in range(2):
                rows = [
                    jnp.concatenate(
                        [sources[r * 4 + (m ^ owner)][side] for r in range(ranges)], axis=1
                    ).astype(F32)
                    for owner in range(4)
                ]
                wide = rows[0].shape[1]
                cut = wide - 128
                left = lax.broadcasted_iota(jnp.int32, (rows[0].shape[0], 128), 1) < extra
                pieces = []
                for even, odd in (rows[:2], rows[2:]):
                    shared = jnp.where(left, even[:, cut:], odd[:, :128])
                    pieces += [even[:, :cut], shared, odd[:, 128:]]
                out[:, side, :] = jnp.concatenate(pieces, axis=1)


def unfold(mine, part, ranges):
    sources = [piece for pieces in ranges for piece in pieces]
    rows, step = sources[0].shape[1], 16
    return pl.pallas_call(
        functools.partial(unfold_kernel, part),
        grid_spec=pltpu.PrefetchScalarGridSpec(
            num_scalar_prefetch=1,
            grid=(rows // step,),
            in_specs=[
                pl.BlockSpec((2, step, s.shape[2]), lambda i, m: (0, i, 0)) for s in sources
            ],
            out_specs=pl.BlockSpec((step, 2, 4 * part), lambda i, m: (i, 0, 0)),
        ),
        out_shape=jax.ShapeDtypeStruct((rows, 2, 4 * part), F32),
        compiler_params=pltpu.CompilerParams(vmem_limit_bytes=32 * 2**20),
        name="unfold",
    )(mine[None], *sources)


def activate(gate_part, upper_part):
    return jax.nn.gelu(gate_part, approximate=True) * upper_part


def pick(table, index):
    hit = index[:, None] == jnp.arange(table.shape[0], dtype=jnp.int32)[None, :]
    return jnp.sum(jnp.where(hit, table[None, :], 0), axis=1)


def dot(left, right):
    return jnp.dot(left, right, preferred_element_type=F32)


def dot_rows(left, right):
    return lax.dot_general(left, right, (((0,), (0,)), ((), ())), preferred_element_type=F32)


def dot_columns(left, right):
    return lax.dot_general(left, right, (((1,), (1,)), ((), ())), preferred_element_type=F32)


def body(
    tokens,
    cotangent,
    block_table,
    sequence_ids,
    w_query,
    w_key,
    w_value,
    w_out,
    w_in,
    w_down,
    gain_attn_in,
    gain_attn_out,
    gain_ffn_in,
    gain_ffn_out,
    gain_query,
    gain_key,
):
    rows = tokens.shape[0]
    block = rows // 2
    model, part = w_in.shape[0] * 4, w_down.shape[0]
    mine = lax.axis_index("fsdp")
    me = lax.axis_index("ctx") * 4 + mine

    sizes = [g.shape[0] for g in (gain_attn_in, gain_attn_out, gain_ffn_in, gain_ffn_out, gain_query, gain_key)]
    width = 384
    packed = jnp.stack(
        [
            jnp.pad(g, (0, width - g.shape[0]))
            for g in (gain_attn_in, gain_attn_out, gain_ffn_in, gain_ffn_out, gain_query, gain_key)
        ]
    )
    packed = jnp.pad(packed, ((0, 10), (0, 0)))
    all_gains = gather_rows(packed, mine).reshape(4, 16, width).astype(F32)
    attn_in_gain, attn_out_gain, ffn_in_gain, ffn_out_gain, query_gain, key_gain = [
        all_gains[:, i, :size].reshape(4 * size) for i, size in enumerate(sizes)
    ]

    pair_mat = gather_rows(jnp.concatenate([w_key, w_value], axis=1), mine)
    query_mat = gather_rows(after(w_query, pair_mat), mine)
    out_mat = gather_rows(after(w_out, query_mat), mine)

    wide = -(-part // 256) * 256
    low_bit = lax.axis_index("ctx") % 2
    own, to_core, to_x, to_corner = carve(jnp.swapaxes(w_in, 0, 1), mine, part, wide)
    quarter = model // 4
    half = quarter // 2
    to_x, to_corner = [
        lax.dynamic_slice_in_dim(c, low_bit * half, half, 1) for c in (to_x, to_corner)
    ]
    from_x = swap(after(to_x, query_mat), 2)
    from_corner = swap(after(to_corner, query_mat), 3)
    places = jnp.stack(
        [mine * 2, mine * 2 + 1, (mine ^ 1) * 2, (mine ^ 1) * 2 + 1]
        + [(mine ^ o) * 2 + bit for o in (2, 3) for bit in (low_bit, 1 - low_bit)]
    )
    in_mat = lay(
        places, own, swap(to_core, 1), from_x, swap(from_x, 4), from_corner, swap(from_corner, 4)
    )
    gate_mat, up_mat = in_mat[0], in_mat[1]
    down_mat = lax.dynamic_update_slice_in_dim(
        jnp.zeros((wide, model), BF), w_down, part % 128 * (mine % 2), 0
    )

    boundary = jnp.sum((sequence_ids == 0).astype(jnp.int32))
    everyone = me ^ jnp.array(wide_offsets(), jnp.int32)
    blocks = pick(block_table, jnp.stack([2 * everyone, 2 * everyone + 1], axis=1).reshape(-1))
    place = (blocks[:2, None] * block + jnp.arange(block, dtype=jnp.int32)[None, :]).reshape(-1)
    start = jnp.where(place >= boundary, boundary, 0)
    position = place - start
    inverse_angle = 1000000.0 ** (-jnp.arange(HD // 2, dtype=F32) / (HD // 2))
    angles = position.astype(F32)[:, None] * inverse_angle[None, :]
    cosine, sine = jnp.cos(angles), jnp.sin(angles)

    inputs = tokens.astype(F32)
    first_norm, first_back = jax.vjp(rms_norm, inputs, attn_in_gain)
    first_low = first_norm.astype(BF)

    def prepare_key(key_in, key_scaling):
        return rotate(rms_norm(key_in, key_scaling), cosine, sine)

    def prepare_query(query_in, query_scaling):
        query_heads = rms_norm(query_in.reshape(rows, H, HD), query_scaling)
        return rotate(query_heads, cosine[:, None, :], sine[:, None, :]) * HD ** (-0.5)

    pair_raw = dot(first_low, pair_mat)
    key_turned, key_back = jax.vjp(prepare_key, pair_raw[:, :HD], key_gain)
    pairs = gather_wide(
        jnp.concatenate([key_turned.astype(BF), pair_raw[:, HD:].astype(BF)], axis=1)
    )
    query_turned, query_back = jax.vjp(prepare_query, dot(first_low, query_mat), query_gain)
    queries = jnp.swapaxes(query_turned.astype(BF), 0, 1).reshape(H * rows, HD)

    probs, weighted, mass = attend(
        blocks, queries, jnp.tile(place, H)[None], jnp.tile(start, H)[None], pairs
    )
    inverse = 1.0 / mass
    heads = (weighted * inverse).T
    heads_low = jnp.swapaxes(heads.astype(BF).reshape(H, rows, HD), 0, 1).reshape(rows, H * HD)
    attn_raw = dot(heads_low, out_mat)
    attn_normed, attn_back = jax.vjp(rms_norm, attn_raw, attn_out_gain)
    hidden = inputs + attn_normed
    second_norm, second_back = jax.vjp(rms_norm, hidden, ffn_in_gain)
    second_low = second_norm.astype(BF)

    second_group = gather_group(second_low)
    gate, upper = dot(second_group, gate_mat), dot(second_group, up_mat)
    act_value, act_back = jax.vjp(activate, gate, upper)
    ffn_raw = scatter_group(dot(act_value.astype(BF), down_mat))
    ffn_normed, ffn_back = jax.vjp(rms_norm, ffn_raw, ffn_out_gain)
    block_out = (hidden + ffn_normed).astype(BF)
    upstream = cotangent.astype(F32)
    d_ffn, d_gain_ffn_out = ffn_back(upstream)
    d_ffn_low = d_ffn.astype(BF)
    d_ffn_group = gather_group(d_ffn_low)
    d_gate, d_upper = act_back(dot_columns(d_ffn_group, down_mat))
    d_second = scatter_group(
        dot_columns(d_gate.astype(BF), gate_mat) + dot_columns(d_upper.astype(BF), up_mat)
    )
    d_hidden_extra, d_gain_ffn_in = second_back(d_second)
    d_hidden = upstream + d_hidden_extra
    d_attn, d_gain_attn_out = attn_back(d_hidden)
    d_attn_low = d_attn.astype(BF)

    d_heads = jnp.swapaxes(
        dot_columns(d_attn_low, out_mat).astype(BF).reshape(rows, H, HD), 0, 1
    ).reshape(H * rows, HD)
    dots = jnp.sum(d_heads.astype(F32) * heads, axis=1)[None]
    d_queries, d_pairs = attend_back(queries, d_heads, inverse, dots, probs, pairs)
    own_sums = scatter_wide(d_pairs)
    d_queries = jnp.swapaxes(d_queries.T.reshape(H, rows, HD), 0, 1)
    d_query_raw, d_gain_query = query_back(d_queries)
    query_low = d_query_raw.astype(BF)
    d_key_raw, d_gain_key = key_back(own_sums[:, :HD])
    pair_low = jnp.concatenate([d_key_raw, own_sums[:, HD:]], axis=1).astype(BF)
    d_first = dot_columns(query_low, query_mat) + dot_columns(pair_low, pair_mat)
    d_inputs_extra, d_gain_attn_in = first_back(d_first)
    grad_tokens = d_hidden + d_inputs_extra

    grad_out = sum_over_ctx(scatter_rows(dot_rows(heads_low, d_attn_low), mine))
    grad_query = sum_over_ctx(scatter_rows(dot_rows(first_low, query_low), mine))
    gain_rows = jnp.stack(
        [d_gain_attn_in, d_gain_attn_out, d_gain_ffn_in, d_gain_ffn_out]
        + [
            jnp.pad(g.reshape(4, -1), ((0, 0), (0, model // 4 - g.shape[0] // 4))).reshape(-1)
            for g in (d_gain_query, d_gain_key)
        ],
        axis=1,
    )
    gain_rows = jnp.pad(gain_rows, ((0, 0), (0, 122)))
    tail = sum_over_ctx(
        scatter_rows(jnp.concatenate([dot_rows(first_low, pair_low), gain_rows], axis=1), mine)
    )
    grad_key, grad_value = tail[:, :HD], tail[:, HD : 2 * HD]
    gain_grads = [tail[: size, 2 * HD + i] for i, size in enumerate(sizes)]

    second_all = gather_wide(second_low)
    d_ffn_all = gather_wide(d_ffn_low)
    blocks_of_columns = wide // 256
    cuts = [blocks_of_columns * i // 3 for i in range(4)]
    ranges, downs = [], []
    for first, last in zip(cuts[:-1], cuts[1:]):
        *sides, down = ffn_gradients(mine, second_all, d_ffn_all, in_mat, down_mat, first, last)
        ranges.append([sides[0]] + [swap(sides[o], o) for o in (1, 2, 3)])
        downs.append(down)
    grad_in = unfold(mine, part, ranges)
    grad_down = lax.dynamic_slice_in_dim(join(*downs), part % 128 * (mine % 2), part, 0)

    return (
        block_out,
        grad_tokens,
        grad_query,
        grad_key,
        grad_value,
        grad_out,
        grad_in,
        grad_down,
        *gain_grads,
    )


def solution(mesh):
    in_specs = (
        P(AXES, None),
        P(AXES, None),
        P(),
        P(),
        P("fsdp", None),
        P("fsdp", None),
        P("fsdp", None),
        P("fsdp", None),
        P("fsdp", None, None),
        P("fsdp", None),
        P("fsdp"),
        P("fsdp"),
        P("fsdp"),
        P("fsdp"),
        P("fsdp"),
        P("fsdp"),
    )
    out_specs = (
        P(AXES, None),
        P(AXES, None),
        P("fsdp", None),
        P("fsdp", None),
        P("fsdp", None),
        P("fsdp", None),
        P("fsdp", None, None),
        P("fsdp", None),
        P("fsdp"),
        P("fsdp"),
        P("fsdp"),
        P("fsdp"),
        P("fsdp"),
        P("fsdp"),
    )
    return jax.shard_map(body, mesh=mesh, in_specs=in_specs, out_specs=out_specs, check_vma=False)
```

time: 1830 us -> 756 us (0.41)
  waiting for transfers between devices: 1100 us -> 236 us
  other arithmetic: 349 us -> 58.8 us
  Pallas kernels: 0 us -> 175 us
  starting transfers between devices: 0.78 us -> 109 us
  matrix products: 128 us -> 42.9 us
  blocking collectives: 58.2 us -> 0 us
  local copies, waits for them, and re-layouts: 170 us -> 121 us
    reduce_scatter x7 -> x0, waiting for transfers between devices: 578 us -> none  [the longest x1 228 us: body(): lax.psum_scatter(jnp.einsum('td,tkf->dkf', columns, d_gate_up, preferred_...]
    psum x1 -> x0, waiting for transfers between devices: 389 us -> none  [body(): lax.psum(grad_in, 'ctx').astype(jnp.float32)]
    ppermute x0 -> x92, waiting for transfers between devices: none -> 236 us  [swap(): return lax.ppermute(value, AXES, [(i, i ^ offset) for i in range(count)])]
    mul x7 -> x2, other arithmetic: 179 us -> 0.04 us  [the longest x1 0.04 us: prepare_query(): rotate(query_heads, cosine[:, None, :], sine[:, None, :]) * HD ** (-0.5)]
    pallas_call x0 -> x8, Pallas kernels: none -> 175 us  [the longest x3 142 us: ffn_gradients(): pl.pallas_call(ffn_kernel, grid_spec=pltpu.PrefetchScalarGridSpec(num_sca...]
    all_gather x6 -> x0, waiting for transfers between devices: 127 us -> none  [the longest x1 78.7 us: body(): lax.all_gather(w_down, 'fsdp', axis=0, tiled=True)]
    gather x185 -> x0, other arithmetic: 115 us -> none  [the longest x179 115 us: place_rows(): block_table[layout_rows // half_block] * half_block]
    ppermute x0 -> x92, starting transfers between devices: none -> 109 us  [swap(): return lax.ppermute(value, AXES, [(i, i ^ offset) for i in range(count)])]
  transfers between devices with their start and end apart: 14 -> 92, of which waited for: 11 -> 35; matrix products, arithmetic and copies ran while one was open for 20% -> 27% of each run, Pallas kernels for 0% -> 11%
where the time goes in v1:
time: 756 us; the launch traced here: 746 us
  waiting for transfers between devices  236 us (31%)
  Pallas kernels  175 us (23%)
  local copies, waits for them, and re-layouts  121 us (16%)
  starting transfers between devices  109 us (14%)
  other arithmetic  58.8 us (8%)
  matrix products  42.9 us (6%)
    ppermute x92, waiting for transfers between devices, swap(): return lax.ppermute(value, AXES, [(i, i ^ offset) for i in range(count)])  236 us
    pallas_call x3, Pallas kernels, ffn_gradients(): pl.pallas_call(ffn_kernel, grid_spec=pltpu.PrefetchScalarGridSpec(num_sca...  142 us
    ppermute x92, starting transfers between devices, swap(): return lax.ppermute(value, AXES, [(i, i ^ offset) for i in range(count)])  109 us
    unnamed x192, local copies, waits for them, and re-layouts  49.8 us
    concatenate x15, other arithmetic, join(): return jnp.concatenate(parts, axis=0)  22.5 us
    dot_general x6, matrix products, dot_columns(): lax.dot_general(left, right, (((1,), (1,)), ((), ())), preferred_element_...  22.3 us
    concatenate x7, local copies, waits for them, and re-layouts, join(): return jnp.concatenate(parts, axis=0)  17.9 us
    dot_general x6, matrix products, dot(): return jnp.dot(left, right, preferred_element_type=F32)  17.1 us
  transfers between devices with their start and end apart: 92, of which 35 were waited for; matrix products, arithmetic and copies ran while one was open for 27% of the time, Pallas kernels for 11%

profile of v1, /device:TPU:1, one launch (start us, length us, event | category | flops | bytes accessed | tf_op | source)
XLA Modules:
  0.0 745.7 jit_solution(16996666243133489520)
XLA Ops:
  82.0 47.2 %collective-permute-done.14 = bf16[256,1152]{1,0:T(8,128)(2,1)} collective-permute-done((bf16[256,1152]{1,0:T(8,128)(2,1)}, bf16[256,1152]{1,0:T(8,128)(2,1)}, u32[]{:S(2)}, u32[]{:S(2)}) %collective-permute-start.14) | collective-permute-done | bytes 589856 | tf_op jit(solution)/shard_map/ppermute | solution.py:40
  138.0 6.9 attend.1
  165.5 7.2 collective-permute-done.16
  205.8 5.5 fusion.14
  231.1 6.3 collective-permute-start.75
  245.7 12.0 %collective-permute-done.77 = bf16[128,1152]{1,0:T(8,128)(2,1)S(1)} collective-permute-done((bf16[128,1152]{1,0:T(8,128)(2,1)S(1)}, bf16[128,1152]{1,0:T(8,128)(2,1)S(1)}, u32[]{:S(2)}, u32[]{:S(2)}) %collective-permute-start.77) | collective-permute-done | bytes 294944 | tf_op jit(solution)/shard_map/ppermute | solution.py:40
  259.2 6.8 collective-permute-start.26
  269.8 4.7 fusion.23
  276.4 5.0 fusion.11
  281.4 7.1 fusion.13
  297.8 14.8 %collective-permute-done.28 = bf16[128,1152]{1,0:T(8,128)(2,1)S(1)} collective-permute-done((bf16[128,1152]{1,0:T(8,128)(2,1)S(1)}, bf16[128,1152]{1,0:T(8,128)(2,1)S(1)}, u32[]{:S(2)}, u32[]{:S(2)}) %collective-permute-start.28) | collective-permute-done | bytes 294944 | tf_op jit(solution)/shard_map/ppermute | solution.py:40
  318.5 7.0 attend_back.1
  345.7 9.1 %collective-permute-done.58 = bf16[256,1152]{1,0:T(8,128)(2,1)S(1)} collective-permute-done((bf16[256,1152]{1,0:T(8,128)(2,1)S(1)}, bf16[256,1152]{1,0:T(8,128)(2,1)S(1)}, u32[]{:S(2)}, u32[]{:S(2)}) %collective-permute-start.58) | collective-permute-done | bytes 589856 | tf_op jit(solution)/shard_map/ppermute | solution.py:40
  356.5 10.8 %collective-permute-done.38 = bf16[288,1024]{1,0:T(8,128)(2,1)S(1)} collective-permute-done((bf16[288,1024]{1,0:T(8,128)(2,1)S(1)}, bf16[288,1024]{1,0:T(8,128)(2,1)S(1)}, u32[]{:S(2)}, u32[]{:S(2)}) %collective-permute-start.38) | collective-permute-done | bytes 589856 | tf_op jit(solution)/shard_map/ppermute | solution.py:40
  371.6 4.6 collective-permute-done.39
  376.2 5.8 collective-permute-start.61
  407.2 4.7 collective-permute-done.44
  411.9 5.7 collective-permute-done.45
  426.7 5.3 collective-permute-done.31
  455.0 10.9 %collective-permute-start.47 = (bf16[576,640]{1,0:T(8,128)(2,1)}, bf16[576,640]{1,0:T(8,128)(2,1)}, u32[]{:S(2)}, u32[]{:S(2)}) collective-permute-start(bf16[576,640]{1,0:T(8,128)(2,1)} %copy.161), channel_id=1, source_target_pairs={{0,1},{1,0},{2,3},{3,2},{4,5},{5,4},{6,7},{7,6},{8,9},{9,8},{10,11... | collective-permute-start | bytes 2211848 | tf_op jit(solution)/shard_map/ppermute | solution.py:40
  475.4 11.0 %collective-permute-done.48 = bf16[288,640]{0,1:T(8,128)(2,1)S(1)} collective-permute-done((bf16[288,640]{0,1:T(8,128)(2,1)S(1)}, bf16[288,640]{0,1:T(8,128)(2,1)S(1)}, u32[]{:S(2)}, u32[]{:S(2)}) %collective-permute-start.48) | collective-permute-done | bytes 368672 | tf_op jit(solution)/shard_map/ppermute | solution.py:40
  487.8 4.7 collective-permute-done.49
  507.6 4.9 constant_dynamic-update-slice_fusion.27.second
  514.6 4.9 constant_dynamic-update-slice_fusion.44.d_ffn
  519.5 41.0 %ffn_gradients.3 = (bf16[2,288,512]{2,1,0:T(8,128)(2,1)}, bf16[2,288,512]{2,1,0:T(8,128)(2,1)}, bf16[2,288,512]{2,1,0:T(8,128)(2,1)}, bf16[2,288,512]{2,1,0:T(8,128)(2,1)}, f32[512,1152]{1,0:T(8,128)}) custom-call(s32[1]{0:T(128)} %bitcast.21.mine, bf16[4096,1152]{1,0:T(8,128)(2,1)} %constant_dynamic-update-slice_fusion.27.second, ...), custom_call_target="tpu_custom_call" | custom-call | flops 28991029248 | bytes 37748736 | tf_op jit(solution)/shard_map/ffn_gradients/pallas_call | solution.py:386
  560.5 41.5 %ffn_gradients.4 = (bf16[2,288,512]{2,1,0:T(8,128)(2,1)}, bf16[2,288,512]{2,1,0:T(8,128)(2,1)}, bf16[2,288,512]{2,1,0:T(8,128)(2,1)}, bf16[2,288,512]{2,1,0:T(8,128)(2,1)}, f32[512,1152]{1,0:T(8,128)}) custom-call(s32[1]{0:T(128)} %bitcast.21.mine, bf16[4096,1152]{1,0:T(8,128)(2,1)} %constant_dynamic-update-slice_fusion.27.second, ...), custom_call_target="tpu_custom_call" | custom-call | flops 28991029248 | bytes 37748736 | tf_op jit(solution)/shard_map/ffn_gradients/pallas_call | solution.py:386
  602.0 4.7 collective-permute-start.83
  608.5 59.4 %ffn_gradients.5 = (bf16[2,288,768]{2,1,0:T(8,128)(2,1)}, bf16[2,288,768]{2,1,0:T(8,128)(2,1)}, bf16[2,288,768]{2,1,0:T(8,128)(2,1)}, bf16[2,288,768]{2,1,0:T(8,128)(2,1)}, f32[768,1152]{1,0:T(8,128)}) custom-call(s32[1]{0:T(128)} %bitcast.21.mine, bf16[4096,1152]{1,0:T(8,128)(2,1)} %constant_dynamic-update-slice_fusion.27.second, ...), custom_call_target="tpu_custom_call" | custom-call | flops 43486543872 | bytes 56623104 | tf_op jit(solution)/shard_map/ffn_gradients/pallas_call | solution.py:386
  672.3 7.9 %fusion.1 = f32[1728,1152]{1,0:T(8,128)} fusion(s32[]{:T(128)S(6)} %select_n.208, f32[512,1152]{1,0:T(8,128)S(1)} %copy-done.41, f32[512,1152]{1,0:T(8,128)} %get-tuple-element.68, f32[768,1152]{1,0:T(8,128)} %get-tuple-element.69), kind=kLoop, calls=%fused_computation.4 | loop fusion | flops 3981312 | bytes 16220164 | tf_op jit(solution)/shard_map/concatenate | solution.py:44
  680.2 40.6 %collective-permute-done.87.refs_6_ = bf16[2,288,512]{2,1,0:T(8,128)(2,1)S(1)} collective-permute-done((bf16[2,288,512]{2,1,0:T(8,128)(2,1)}, bf16[2,288,512]{2,1,0:T(8,128)(2,1)S(1)}, u32[]{:S(2)}, u32[]{:S(2)}) %collective-permute-start.87) | collective-permute-done | bytes 589856 | tf_op jit(solution)/shard_map/ppermute | solution.py:40
  720.9 13.0 %collective-permute-done.88.refs_7_ = bf16[2,288,512]{2,1,0:T(8,128)(2,1)S(1)} collective-permute-done((bf16[2,288,512]{2,1,0:T(8,128)(2,1)}, bf16[2,288,512]{2,1,0:T(8,128)(2,1)S(1)}, u32[]{:S(2)}, u32[]{:S(2)}) %collective-permute-start.88) | collective-permute-done | bytes 589856 | tf_op jit(solution)/shard_map/ppermute | solution.py:40
  734.0 11.3 %unfold.1 = f32[288,2,6912]{2,1,0:T(2,128)} custom-call(s32[1]{0:T(128)} %bitcast.21.mine, bf16[2,288,512]{2,1,0:T(8,128)(2,1)S(1)} %copy-done.11, bf16[2,288,512]{2,1,0:T(8,128)(2,1)S(1)} %collective-permute-done.83.refs_1_, bf16[2,288,512]{2,1,0:T(8,128)(2,1)S(1)} %collective-permute-done.84.refs_2_, ...), custom_call_target="tpu_custom_call" | custom-call | tf_op jit(solution)/shard_map/unfold/pallas_call | solution.py:446
  (588 shorter events, 310.7 us)
Async XLA Ops:
  18.7 23.8 %collective-permute-start.4 = (bf16[288,1024]{1,0:T(8,128)(2,1)}, bf16[288,1024]{1,0:T(8,128)(2,1)}, u32[]{:S(2)}, u32[]{:S(2)}) collective-permute-start(bf16[288,1024]{1,0:T(8,128)(2,1)} %param.21), channel_id=1, source_target_pairs={{0,2},{1,3},{2,0},{3,1},{4,6},{5,7},{6,4},{7,5},{8,10},{9,11},{10,... | collective-permute-start | bytes 1769480 | tf_op jit(solution)/shard_map/ppermute | solution.py:40
  37.6 137.8 %collective-permute-start.18 = (bf16[2,288,1792]{2,1,0:T(8,128)(2,1)}, bf16[2,288,1792]{2,1,0:T(8,128)(2,1)S(1)}, u32[]{:S(2)}, u32[]{:S(2)}) collective-permute-start(bf16[2,288,1792]{2,1,0:T(8,128)(2,1)} %get-tuple-element.47), channel_id=1, source_target_pairs={{0,1},{1,0},{2,3},{3,2},{4,5},{5,4},{6,7},{7,6},{8,9},{9,8},{10,11... | collective-permute-start | bytes 6193160 | tf_op jit(solution)/shard_map/ppermute | solution.py:40
  64.6 71.6 %collective-permute-start.13 = (bf16[2048,512]{1,0:T(8,128)(2,1)}, bf16[2048,512]{1,0:T(8,128)(2,1)}, u32[]{:S(2)}, u32[]{:S(2)}) collective-permute-start(bf16[2048,512]{1,0:T(8,128)(2,1)} %get-tuple-element.191), channel_id=1, source_target_pairs={{0,1},{1,0},{2,3},{3,2},{4,5},{5,4},{6,7},{7,6},{8,9},{9,8},{10,11... | collective-permute-start | bytes 6291464 | tf_op jit(solution)/shard_map/ppermute | solution.py:40
  69.6 65.4 %collective-permute-start.19 = (bf16[2,144,1792]{2,1,0:T(8,128)(2,1)}, bf16[2,144,1792]{2,1,0:T(8,128)(2,1)S(1)}, u32[]{:S(2)}, u32[]{:S(2)}) collective-permute-start(bf16[2,144,1792]{2,1,0:T(8,128)(2,1)} %get-tuple-element.49), channel_id=1, source_target_pairs={{0,2},{1,3},{2,0},{3,1},{4,6},{5,7},{6,4},{7,5},{8,10},{9,11},{10,... | collective-permute-start | bytes 3096584 | tf_op jit(solution)/shard_map/ppermute | solution.py:40
  70.4 94.3 %collective-permute-start.21 = (bf16[2,144,1792]{2,1,0:T(8,128)(2,1)}, bf16[2,144,1792]{2,1,0:T(8,128)(2,1)}, u32[]{:S(2)}, u32[]{:S(2)}) collective-permute-start(bf16[2,144,1792]{2,1,0:T(8,128)(2,1)} %get-tuple-element.51), channel_id=1, source_target_pairs={{0,3},{1,2},{2,1},{3,0},{4,7},{5,6},{6,5},{7,4},{8,11},{9,10},{10,... | collective-permute-start | bytes 3096584 | tf_op jit(solution)/shard_map/ppermute | solution.py:40
  78.2 51.0 %collective-permute-start.14 = (bf16[256,1152]{1,0:T(8,128)(2,1)}, bf16[256,1152]{1,0:T(8,128)(2,1)}, u32[]{:S(2)}, u32[]{:S(2)}) collective-permute-start(bf16[256,1152]{1,0:T(8,128)(2,1)} %param.24), channel_id=1, source_target_pairs={{0,2},{1,3},{2,0},{3,1},{4,6},{5,7},{6,4},{7,5},{8,10},{9,11},{10,... | collective-permute-start | bytes 1769480 | tf_op jit(solution)/shard_map/ppermute | solution.py:40
  135.0 44.2 %collective-permute-start.20 = (bf16[2,144,1792]{2,1,0:T(8,128)(2,1)S(1)}, bf16[2,144,1792]{2,1,0:T(8,128)(2,1)}, u32[]{:S(2)}, u32[]{:S(2)}) collective-permute-start(bf16[2,144,1792]{2,1,0:T(8,128)(2,1)S(1)} %collective-permute-done.19.x2), channel_id=1, source_target_pairs={{0,4},{1,5},{2,6},{3,7},{4,0},{5,1},{6,2},{7,3},{8,12},{9,13},{10,... | collective-permute-start | bytes 3096584 | tf_op jit(solution)/shard_map/ppermute | solution.py:40
  164.7 24.1 %collective-permute-start.22 = (bf16[2,144,1792]{2,1,0:T(8,128)(2,1)}, bf16[2,144,1792]{2,1,0:T(8,128)(2,1)}, u32[]{:S(2)}, u32[]{:S(2)}) collective-permute-start(bf16[2,144,1792]{2,1,0:T(8,128)(2,1)} %collective-permute-done.21.x3), channel_id=1, source_target_pairs={{0,4},{1,5},{2,6},{3,7},{4,0},{5,1},{6,2},{7,3},{8,12},{9,13},{10,... | collective-permute-start | bytes 3096584 | tf_op jit(solution)/shard_map/ppermute | solution.py:40
  165.0 30.0 %collective-permute-start.67 = (bf16[128,1152]{1,0:T(8,128)(2,1)}, bf16[128,1152]{1,0:T(8,128)(2,1)}, u32[]{:S(2)}, u32[]{:S(2)}) collective-permute-start(bf16[128,1152]{1,0:T(8,128)(2,1)} %get-tuple-element.97), channel_id=1, source_target_pairs={{0,8},{1,9},{2,10},{3,11},{4,12},{5,13},{6,14},{7,15},{8,0},{9,1},... | collective-permute-start | bytes 884744 | tf_op jit(solution)/shard_map/ppermute | solution.py:40
  197.2 25.5 %collective-permute-start.70 = (bf16[512,1152]{1,0:T(8,128)(2,1)S(1)}, bf16[512,1152]{1,0:T(8,128)(2,1)S(1)}, u32[]{:S(2)}, u32[]{:S(2)}) collective-permute-start(bf16[512,1152]{1,0:T(8,128)(2,1)S(1)} %fusion.29), channel_id=1, source_target_pairs={{0,4},{1,5},{2,6},{3,7},{4,0},{5,1},{6,2},{7,3},{8,12},{9,13},{10,... | collective-permute-start | bytes 3538952 | tf_op jit(solution)/shard_map/ppermute | solution.py:40
  197.5 43.7 %collective-permute-start.71 = (bf16[512,1152]{1,0:T(8,128)(2,1)S(1)}, bf16[512,1152]{1,0:T(8,128)(2,1)S(1)}, u32[]{:S(2)}, u32[]{:S(2)}) collective-permute-start(bf16[512,1152]{1,0:T(8,128)(2,1)S(1)} %fusion.29), channel_id=1, source_target_pairs={{0,2},{1,3},{2,0},{3,1},{4,6},{5,7},{6,4},{7,5},{8,10},{9,11},{10,... | collective-permute-start | bytes 3538952 | tf_op jit(solution)/shard_map/ppermute | solution.py:40
  222.7 46.0 %collective-permute-start.72 = (bf16[256,1152]{1,0:T(8,128)(2,1)S(1)}, bf16[256,1152]{1,0:T(8,128)(2,1)S(1)}, u32[]{:S(2)}, u32[]{:S(2)}) collective-permute-start(bf16[256,1152]{1,0:T(8,128)(2,1)S(1)} %slice.342), channel_id=1, source_target_pairs={{0,2},{1,3},{2,0},{3,1},{4,6},{5,7},{6,4},{7,5},{8,10},{9,11},{10,... | collective-permute-start | bytes 1769480 | tf_op jit(solution)/shard_map/ppermute | solution.py:40
  245.3 43.4 %collective-permute-start.73 = (bf16[256,1152]{1,0:T(8,128)(2,1)S(1)}, bf16[256,1152]{1,0:T(8,128)(2,1)S(1)}, u32[]{:S(2)}, u32[]{:S(2)}) collective-permute-start(bf16[256,1152]{1,0:T(8,128)(2,1)S(1)} %slice.343), channel_id=1, source_target_pairs={{0,4},{1,5},{2,6},{3,7},{4,0},{5,1},{6,2},{7,3},{8,12},{9,13},{10,... | collective-permute-start | bytes 1769480 | tf_op jit(solution)/shard_map/ppermute | solution.py:40
  257.8 32.5 %collective-permute-start.78 = (bf16[512,1152]{1,0:T(8,128)(2,1)S(1)}, bf16[512,1152]{1,0:T(8,128)(2,1)S(1)}, u32[]{:S(2)}, u32[]{:S(2)}) collective-permute-start(bf16[512,1152]{1,0:T(8,128)(2,1)S(1)} %fusion.26), channel_id=1, source_target_pairs={{0,4},{1,5},{2,6},{3,7},{4,0},{5,1},{6,2},{7,3},{8,12},{9,13},{10,... | collective-permute-start | bytes 3538952 | tf_op jit(solution)/shard_map/ppermute | solution.py:40
  258.4 33.4 %collective-permute-start.79 = (bf16[512,1152]{1,0:T(8,128)(2,1)S(1)}, bf16[512,1152]{1,0:T(8,128)(2,1)S(1)}, u32[]{:S(2)}, u32[]{:S(2)}) collective-permute-start(bf16[512,1152]{1,0:T(8,128)(2,1)S(1)} %fusion.26), channel_id=1, source_target_pairs={{0,2},{1,3},{2,0},{3,1},{4,6},{5,7},{6,4},{7,5},{8,10},{9,11},{10,... | collective-permute-start | bytes 3538952 | tf_op jit(solution)/shard_map/ppermute | solution.py:40
  289.7 217.9 %collective-permute-start.74 = (bf16[2048,1152]{1,0:T(8,128)(2,1)}, bf16[2048,1152]{1,0:T(8,128)(2,1)}, u32[]{:S(2)}, u32[]{:S(2)}) collective-permute-start(bf16[2048,1152]{1,0:T(8,128)(2,1)} %get-tuple-element.156), channel_id=1, source_target_pairs={{0,1},{1,0},{2,3},{3,2},{4,5},{5,4},{6,7},{7,6},{8,9},{9,8},{10,11... | collective-permute-start | bytes 14155784 | tf_op jit(solution)/shard_map/ppermute | solution.py:40
  291.1 44.0 %collective-permute-start.80 = (bf16[256,1152]{1,0:T(8,128)(2,1)}, bf16[256,1152]{1,0:T(8,128)(2,1)}, u32[]{:S(2)}, u32[]{:S(2)}) collective-permute-start(bf16[256,1152]{1,0:T(8,128)(2,1)} %slice.344), channel_id=1, source_target_pairs={{0,2},{1,3},{2,0},{3,1},{4,6},{5,7},{6,4},{7,5},{8,10},{9,11},{10,... | collective-permute-start | bytes 1769480 | tf_op jit(solution)/shard_map/ppermute | solution.py:40
  292.7 47.9 %collective-permute-start.81 = (bf16[256,1152]{1,0:T(8,128)(2,1)}, bf16[256,1152]{1,0:T(8,128)(2,1)}, u32[]{:S(2)}, u32[]{:S(2)}) collective-permute-start(bf16[256,1152]{1,0:T(8,128)(2,1)} %slice.345), channel_id=1, source_target_pairs={{0,4},{1,5},{2,6},{3,7},{4,0},{5,1},{6,2},{7,3},{8,12},{9,13},{10,... | collective-permute-start | bytes 1769480 | tf_op jit(solution)/shard_map/ppermute | solution.py:40
  335.1 47.0 %collective-permute-start.29 = (bf16[2048,512]{1,0:T(8,128)(2,1)}, bf16[2048,512]{1,0:T(8,128)(2,1)}, u32[]{:S(2)}, u32[]{:S(2)}) collective-permute-start(bf16[2048,512]{1,0:T(8,128)(2,1)} %slice.261), channel_id=1, source_target_pairs={{0,1},{1,0},{2,3},{3,2},{4,5},{5,4},{6,7},{7,6},{8,9},{9,8},{10,11... | collective-permute-start | bytes 6291464 | tf_op jit(solution)/shard_map/ppermute | solution.py:40
  342.8 171.8 %collective-permute-start.82 = (bf16[2048,1152]{1,0:T(8,128)(2,1)}, bf16[2048,1152]{1,0:T(8,128)(2,1)}, u32[]{:S(2)}, u32[]{:S(2)}) collective-permute-start(bf16[2048,1152]{1,0:T(8,128)(2,1)} %get-tuple-element.152), channel_id=1, source_target_pairs={{0,1},{1,0},{2,3},{3,2},{4,5},{5,4},{6,7},{7,6},{8,9},{9,8},{10,11... | collective-permute-start | bytes 14155784 | tf_op jit(solution)/shard_map/ppermute | solution.py:40
  390.0 27.6 %collective-permute-start.30 = (bf16[256,512]{1,0:T(8,128)(2,1)S(1)}, bf16[256,512]{1,0:T(8,128)(2,1)S(1)}, u32[]{:S(2)}, u32[]{:S(2)}) collective-permute-start(bf16[256,512]{1,0:T(8,128)(2,1)S(1)} %get-tuple-element.131), channel_id=1, source_target_pairs={{0,2},{1,3},{2,0},{3,1},{4,6},{5,7},{6,4},{7,5},{8,10},{9,11},{10,... | collective-permute-start | bytes 786440 | tf_op jit(solution)/shard_map/ppermute | solution.py:40
  394.3 24.0 %collective-permute-start.32 = (bf16[256,512]{1,0:T(8,128)(2,1)S(1)}, bf16[256,512]{1,0:T(8,128)(2,1)S(1)}, u32[]{:S(2)}, u32[]{:S(2)}) collective-permute-start(bf16[256,512]{1,0:T(8,128)(2,1)S(1)} %get-tuple-element.132), channel_id=1, source_target_pairs={{0,4},{1,5},{2,6},{3,7},{4,0},{5,1},{6,2},{7,3},{8,12},{9,13},{10,... | collective-permute-start | bytes 786440 | tf_op jit(solution)/shard_map/ppermute | solution.py:40
  440.0 25.9 %collective-permute-start.66 = (bf16[4,32,1152]{2,1,0:T(8,128)(2,1)}, bf16[4,32,1152]{2,1,0:T(8,128)(2,1)}, u32[]{:S(2)}, u32[]{:S(2)}) collective-permute-start(bf16[4,32,1152]{2,1,0:T(8,128)(2,1)} %copy-done.47), channel_id=1, source_target_pairs={{0,4},{1,5},{2,6},{3,7},{4,0},{5,1},{6,2},{7,3},{8,12},{9,13},{10,... | collective-permute-start | bytes 884744 | tf_op jit(solution)/shard_map/ppermute | solution.py:40
  602.0 66.1 %collective-permute-start.83 = (bf16[2,288,512]{2,1,0:T(8,128)(2,1)S(1)}, bf16[2,288,512]{2,1,0:T(8,128)(2,1)S(1)}, u32[]{:S(2)}, u32[]{:S(2)}) collective-permute-start(bf16[2,288,512]{2,1,0:T(8,128)(2,1)S(1)} %copy-done.81), channel_id=1, source_target_pairs={{0,1},{1,0},{2,3},{3,2},{4,5},{5,4},{6,7},{7,6},{8,9},{9,8},{10,11... | collective-permute-start | bytes 1769480 | tf_op jit(solution)/shard_map/ppermute | solution.py:40
  606.6 62.2 %collective-permute-start.84 = (bf16[2,288,512]{2,1,0:T(8,128)(2,1)S(1)}, bf16[2,288,512]{2,1,0:T(8,128)(2,1)S(1)}, u32[]{:S(2)}, u32[]{:S(2)}) collective-permute-start(bf16[2,288,512]{2,1,0:T(8,128)(2,1)S(1)} %copy-done.80), channel_id=1, source_target_pairs={{0,2},{1,3},{2,0},{3,1},{4,6},{5,7},{6,4},{7,5},{8,10},{9,11},{10,... | collective-permute-start | bytes 1769480 | tf_op jit(solution)/shard_map/ppermute | solution.py:40
  607.4 63.3 %collective-permute-start.85 = (bf16[2,288,512]{2,1,0:T(8,128)(2,1)S(1)}, bf16[2,288,512]{2,1,0:T(8,128)(2,1)S(1)}, u32[]{:S(2)}, u32[]{:S(2)}) collective-permute-start(bf16[2,288,512]{2,1,0:T(8,128)(2,1)S(1)} %copy-done.79), channel_id=1, source_target_pairs={{0,3},{1,2},{2,1},{3,0},{4,7},{5,6},{6,5},{7,4},{8,11},{9,10},{10,... | collective-permute-start | bytes 1769480 | tf_op jit(solution)/shard_map/ppermute | solution.py:40
  608.4 63.1 %collective-permute-start.86 = (bf16[2,288,512]{2,1,0:T(8,128)(2,1)}, bf16[2,288,512]{2,1,0:T(8,128)(2,1)S(1)}, u32[]{:S(2)}, u32[]{:S(2)}) collective-permute-start(bf16[2,288,512]{2,1,0:T(8,128)(2,1)} %get-tuple-element.60), channel_id=1, source_target_pairs={{0,1},{1,0},{2,3},{3,2},{4,5},{5,4},{6,7},{7,6},{8,9},{9,8},{10,11... | collective-permute-start | bytes 1769480 | tf_op jit(solution)/shard_map/ppermute | solution.py:40
  667.9 66.1 %collective-permute-start.89 = (bf16[2,288,768]{2,1,0:T(8,128)(2,1)}, bf16[2,288,768]{2,1,0:T(8,128)(2,1)S(1)}, u32[]{:S(2)}, u32[]{:S(2)}) collective-permute-start(bf16[2,288,768]{2,1,0:T(8,128)(2,1)} %get-tuple-element.64), channel_id=1, source_target_pairs={{0,1},{1,0},{2,3},{3,2},{4,5},{5,4},{6,7},{7,6},{8,9},{9,8},{10,11... | collective-permute-start | bytes 2654216 | tf_op jit(solution)/shard_map/ppermute | solution.py:40
  668.1 65.8 %collective-permute-start.90 = (bf16[2,288,768]{2,1,0:T(8,128)(2,1)}, bf16[2,288,768]{2,1,0:T(8,128)(2,1)S(1)}, u32[]{:S(2)}, u32[]{:S(2)}) collective-permute-start(bf16[2,288,768]{2,1,0:T(8,128)(2,1)} %get-tuple-element.65), channel_id=1, source_target_pairs={{0,2},{1,3},{2,0},{3,1},{4,6},{5,7},{6,4},{7,5},{8,10},{9,11},{10,... | collective-permute-start | bytes 2654216 | tf_op jit(solution)/shard_map/ppermute | solution.py:40
  668.8 65.1 %collective-permute-start.91 = (bf16[2,288,768]{2,1,0:T(8,128)(2,1)}, bf16[2,288,768]{2,1,0:T(8,128)(2,1)S(1)}, u32[]{:S(2)}, u32[]{:S(2)}) collective-permute-start(bf16[2,288,768]{2,1,0:T(8,128)(2,1)} %get-tuple-element.66), channel_id=1, source_target_pairs={{0,3},{1,2},{2,1},{3,0},{4,7},{5,6},{6,5},{7,4},{8,11},{9,10},{10,... | collective-permute-start | bytes 2654216 | tf_op jit(solution)/shard_map/ppermute | solution.py:40
  670.7 50.2 %collective-permute-start.87 = (bf16[2,288,512]{2,1,0:T(8,128)(2,1)}, bf16[2,288,512]{2,1,0:T(8,128)(2,1)S(1)}, u32[]{:S(2)}, u32[]{:S(2)}) collective-permute-start(bf16[2,288,512]{2,1,0:T(8,128)(2,1)} %get-tuple-element.61), channel_id=1, source_target_pairs={{0,2},{1,3},{2,0},{3,1},{4,6},{5,7},{6,4},{7,5},{8,10},{9,11},{10,... | collective-permute-start | bytes 1769480 | tf_op jit(solution)/shard_map/ppermute | solution.py:40
  671.4 62.5 %collective-permute-start.88 = (bf16[2,288,512]{2,1,0:T(8,128)(2,1)}, bf16[2,288,512]{2,1,0:T(8,128)(2,1)S(1)}, u32[]{:S(2)}, u32[]{:S(2)}) collective-permute-start(bf16[2,288,512]{2,1,0:T(8,128)(2,1)} %get-tuple-element.62), channel_id=1, source_target_pairs={{0,3},{1,2},{2,1},{3,0},{4,7},{5,6},{6,5},{7,4},{8,11},{9,10},{10,... | collective-permute-start | bytes 1769480 | tf_op jit(solution)/shard_map/ppermute | solution.py:40
  (143 other events, 1678.4 us)

commit v2 on v1

v2 whole, which is shorter than its diff:
```python
import functools
import math

import jax
import jax.numpy as jnp
from jax import lax
from jax.experimental import pallas as pl
from jax.experimental.pallas import tpu as pltpu
from jax.sharding import PartitionSpec as P

H = 4
HD = 256
EPS = 1e-06
AXES = ("ctx", "fsdp")
BF = jnp.bfloat16
F32 = jnp.float32
KEY_BLOCK = 512
VMEM_LIMIT = 32 * 2**20
VMEM_ALL = 60 * 2**20


def root(values):
    return lax.rsqrt(jnp.mean(values * values, axis=-1, keepdims=True) + EPS)


def rms_back(values, gain, grad):
    scale = root(values)
    scaled = gain * grad
    mean = jnp.mean(values * scaled, axis=-1, keepdims=True)
    return (
        scale * scaled - values * (scale * scale * scale * mean),
        jnp.sum(grad * values * scale, axis=0, keepdims=True),
    )


def rotate(values, cosine, sine):
    half = values.shape[-1] // 2
    first, second = values[:, :half], values[:, half:]
    return jnp.concatenate(
        [first * cosine - second * sine, second * cosine + first * sine], axis=1
    )


class Flow:
    def __init__(self, steps):
        self.steps = steps
        self.result = None
        self.flying = next(steps)

    def land(self, arrays):
        try:
            self.flying = self.steps.send(arrays)
        except StopIteration as stop:
            self.flying, self.result = None, stop.value


def pace(values, *flows):
    flying = [flow.flying for flow in flows]
    values, flying = lax.optimization_barrier((values, flying))
    for flow, arrays in zip(flows, flying):
        flow.land(arrays)
    return values


def finish(flow):
    while flow.flying is not None:
        flow.land(flow.flying)
    return flow.result


def swap(value, offset):
    count = lax.axis_size("ctx") * lax.axis_size("fsdp")
    return lax.ppermute(value, AXES, [(i, i ^ offset) for i in range(count)])


def join(*parts):
    return jnp.concatenate(parts, axis=0)


def iter_once(arrays):
    return (yield arrays)


def gather_group(value):
    (other,) = yield [swap(value, 2)]
    pair = join(value, other)
    (other,) = yield [swap(pair, 1)]
    return pair, other


def scatter_group(keep, send):
    (other,) = yield [swap(send, 1)]
    half = keep.shape[0] // 2
    (far,) = yield [swap((keep[half:] + other[half:].astype(F32)).astype(BF), 2)]
    return keep[:half] + other[:half].astype(F32), far


def wide_offsets():
    highs = [8 * s for s in range(lax.axis_size("ctx") // 2)]
    chip = [low + high for low in (0, 4, 2, 6) for high in highs]
    return chip + [1 + o for o in chip]


def gather_wide(value):
    highs = lax.axis_size("ctx") // 2
    line = join(value, *(yield [swap(value, 8 * s) for s in range(1, highs)]))
    half = line.shape[0] // 2
    along_y, along_x = yield [swap(line, o) for o in (4, 2)]
    corner = yield [swap(along_y[:half], 2), swap(along_x[half:], 4)]
    chip = join(line, along_y, along_x, *corner)
    (other,) = yield [swap(chip, 1)]
    return chip, other


def scatter_wide(near, far):
    highs = lax.axis_size("ctx") // 2
    (other,) = yield [swap(far, 1)]
    chip = near.astype(F32) + other.astype(F32)
    line, along_y, along_x, corner = jnp.split(chip, 4, axis=0)
    mid = line.shape[0] // 2
    corner = corner.astype(BF)
    from_x, from_y = yield [swap(corner[:mid], 2), swap(corner[mid:], 4)]
    along_y = join(along_y[:mid] + from_x.astype(F32), along_y[mid:])
    along_x = join(along_x[:mid], along_x[mid:] + from_y.astype(F32))
    from_y, from_x = yield [swap(along_y.astype(BF), 4), swap(along_x.astype(BF), 2)]
    line = line + from_y.astype(F32) + from_x.astype(F32)
    rows = line.shape[0] // highs
    terms = yield [
        swap(line[s * rows : (s + 1) * rows].astype(BF), 8 * s) for s in range(1, highs)
    ]
    return [line[:rows], *terms]


def sum_over_ctx(value):
    count, me = lax.axis_size("ctx"), lax.axis_index("ctx")
    highs, low, high = count // 2, me % 2, me // 2
    half, step = value.shape[0] // 2, value.shape[0] // count
    (other,) = yield [swap(lax.dynamic_slice_in_dim(value, (1 - low) * half, half, 0).astype(BF), 4)]
    line = lax.dynamic_slice_in_dim(value, low * half, half, 0) + other.astype(F32)
    line_low = line.astype(BF)
    terms = yield [
        swap(lax.dynamic_slice_in_dim(line_low, (high ^ s) * step, step, 0), 8 * s)
        for s in range(1, highs)
    ]
    total = lax.dynamic_slice_in_dim(line, high * step, step, 0)
    total = (total + sum(term.astype(F32) for term in terms)).astype(BF)
    pieces = yield [swap(total, 8 * s) for s in range(1, highs)]
    line = line_low
    for s, piece in enumerate([total, *pieces]):
        line = lax.dynamic_update_slice_in_dim(line, piece, (high ^ s) * step, 0)
    (other,) = yield [swap(line, 4)]
    even, odd = jnp.where(low == 0, line, other), jnp.where(low == 0, other, line)
    return join(even, odd).astype(F32)


def gather_rows(value, me):
    (other,) = yield [swap(value, 2)]
    pair = join(value, other)
    (other,) = yield [swap(pair, 1)]
    return settle(me ^ jnp.array([0, 2, 1, 3], jnp.int32), value.shape[0], pair, other)


def exchange_columns(quarters):
    first, second = yield [swap(quarters[0], 2), swap(quarters[1], 3)]
    (first_z,) = yield [swap(first, 8)]
    second_z, second_y = yield [swap(second, 8), swap(second, 4)]
    first_y, first_far, second_far = yield [swap(first, 4), swap(first_z, 4), swap(second_y, 8)]
    return [(first, first_y, first_z, first_far), (second, second_y, second_z, second_far)]


def kernel_call(kernel, out_shape, *operands, scalars=(), scratch=(), name):
    whole = pl.BlockSpec(memory_space=pltpu.VMEM)
    return pl.pallas_call(
        kernel,
        out_shape=[jax.ShapeDtypeStruct(shape, dtype) for shape, dtype in out_shape],
        in_specs=[pl.BlockSpec(memory_space=pltpu.SMEM)] * len(scalars) + [whole] * len(operands),
        out_specs=[whole] * len(out_shape),
        scratch_shapes=[pltpu.VMEM(shape, dtype) for shape, dtype in scratch],
        compiler_params=pltpu.CompilerParams(vmem_limit_bytes=VMEM_LIMIT),
        name=name,
    )(*scalars, *operands)


def gains_kernel(mine, *refs):
    sources, (wide, narrow) = refs[:4], refs[4:]
    part, head_part = wide.shape[1] // 4, narrow.shape[1] // 4
    for m in range(4):

        @pl.when(mine[0] == m)
        def _(m=m):
            owners = [sources[m ^ r][...] for r in range(4)]
            for i in range(4):
                wide[i : i + 1, :] = jnp.concatenate(
                    [o[:, i * part : (i + 1) * part] for o in owners], axis=1
                )
            for i in range(2):
                first = 4 * part + i * head_part
                narrow[i : i + 1, :] = jnp.concatenate(
                    [o[:, first : first + head_part] for o in owners], axis=1
                )


def key_kernel(tokens, gain, key_gain, pair_mat, cosine, sine, first_low, key_raw, pairs):
    inputs = tokens[...].astype(F32)
    low = (inputs * root(inputs) * gain[0:1, :]).astype(BF)
    first_low[...] = low
    raw = contract(low, pair_mat[...], 1, 0)
    key = raw[:, :HD]
    key_raw[...] = key
    key = key * root(key) * key_gain[1:2, :]
    pairs[:, :HD] = rotate(key, cosine[...], sine[...]).astype(BF)
    pairs[:, HD:] = raw[:, HD:].astype(BF)


def query_kernel(first_low, query_gain, query_mat, cosine, sine, query_raw, queries):
    rows = first_low.shape[0]
    raw = contract(first_low[...], query_mat[...], 1, 0)
    query_raw[...] = raw
    for h in range(H):
        head = raw[:, h * HD : (h + 1) * HD]
        head = rotate(head * root(head) * query_gain[0:1, :], cosine[...], sine[...])
        queries[h * rows : (h + 1) * rows, :] = (head * HD ** (-0.5)).astype(BF)


def attend_kernel(blocks, q, q_place, q_start, k_near, v_near, k_far, v_far, near, far, heads, mass):
    step = pl.program_id(0)
    middle = pl.num_programs(0) // 2

    @pl.when(step == 0)
    def _():
        heads[...] = jnp.zeros_like(heads)
        mass[...] = jnp.zeros_like(mass)

    def section(k, v, probs):
        scores = contract(k[...], q[...], 1, 1)
        rows = k.shape[0]
        block = 64
        place, start = q_place[...], q_start[...]
        total = jnp.zeros_like(mass)
        for i in range(rows // block):
            first = blocks[step * (rows // block) + i] * block
            keys = first + lax.broadcasted_iota(jnp.int32, (block, scores.shape[1]), 0)
            allowed = (keys <= place) & (keys >= start)
            weights = jnp.where(allowed, jnp.exp(scores[i * block : (i + 1) * block]), 0.0)
            probs[i * block : (i + 1) * block, :] = weights.astype(BF)
            total = total + jnp.sum(weights, axis=0, keepdims=True)
        mass[...] += total
        heads[...] += contract(v[...], probs[...], 0, 0)

    @pl.when(step < middle)
    def _():
        section(k_near, v_near, near)

    @pl.when(step >= middle)
    def _():
        section(k_far, v_far, far)


def halves_of(shape, steps, column=0):
    half = steps // 2
    return [
        pl.BlockSpec(shape, lambda i, *s: (jnp.minimum(i, half - 1), column)),
        pl.BlockSpec(shape, lambda i, *s: (jnp.maximum(i - half, 0), column)),
    ]


def attend(blocks, queries, q_place, q_start, near, far):
    head_rows = queries.shape[0]
    keys = near.shape[0]
    steps = 2 * keys // KEY_BLOCK
    key_blocks, value_blocks = [halves_of((KEY_BLOCK, HD), steps, c) for c in (0, 1)]
    return pl.pallas_call(
        attend_kernel,
        grid_spec=pltpu.PrefetchScalarGridSpec(
            num_scalar_prefetch=1,
            grid=(steps,),
            in_specs=[
                pl.BlockSpec((head_rows, HD), lambda i, b: (0, 0)),
                pl.BlockSpec((1, head_rows), lambda i, b: (0, 0)),
                pl.BlockSpec((1, head_rows), lambda i, b: (0, 0)),
                key_blocks[0],
                value_blocks[0],
                key_blocks[1],
                value_blocks[1],
            ],
            out_specs=[
                *halves_of((KEY_BLOCK, head_rows), steps),
                pl.BlockSpec((HD, head_rows), lambda i, b: (0, 0)),
                pl.BlockSpec((1, head_rows), lambda i, b: (0, 0)),
            ],
        ),
        out_shape=[
            jax.ShapeDtypeStruct((keys, head_rows), BF),
            jax.ShapeDtypeStruct((keys, head_rows), BF),
            jax.ShapeDtypeStruct((HD, head_rows), F32),
            jax.ShapeDtypeStruct((1, head_rows), F32),
        ],
        compiler_params=pltpu.CompilerParams(vmem_limit_bytes=VMEM_LIMIT),
        cost_estimate=pl.CostEstimate(
            flops=8 * keys * head_rows * HD,
            bytes_accessed=2 * keys * (head_rows + 2 * HD) * 2,
            transcendentals=2 * keys * head_rows,
        ),
        name="attend",
    )(blocks, queries, q_place, q_start, near, near, far, far)


def turned_line(column):
    return jnp.broadcast_to(column, (column.shape[0], 128)).T[0:1, :]


def after_attend_kernel(weighted, mass, out_mat, tokens, gains, heads, heads_low, attn_raw, hidden, second_low):
    rows = tokens.shape[0]
    heads[...] = (weighted[...] * (1.0 / mass[...])).T
    for h in range(H):
        heads_low[:, h * HD : (h + 1) * HD] = heads[h * rows : (h + 1) * rows, :].astype(BF)
    raw = contract(heads_low[...], out_mat[...], 1, 0)
    attn_raw[...] = raw
    total = tokens[...].astype(F32) + raw * root(raw) * gains[1:2, :]
    hidden[...] = total
    second_low[...] = (total * root(total) * gains[2:3, :]).astype(BF)


def after_ffn_kernel(part, other, hidden, cotangent, gains, block_out, d_ffn_low, d_gain):
    raw = part[...] + other[...].astype(F32)
    block_out[...] = (hidden[...] + raw * root(raw) * gains[3:4, :]).astype(BF)
    d_ffn, d_gain[...] = rms_back(raw, gains[3:4, :], cotangent[...].astype(F32))
    d_ffn_low[...] = d_ffn.astype(BF)


def before_attend_back_kernel(
    part, other, hidden, cotangent, gains, attn_raw, out_mat, heads,
    d_hidden, d_attn_low, d_heads, dots, d_gain_ffn_in, d_gain_attn_out,
):
    rows = part.shape[0]
    d_second = part[...] + other[...].astype(F32)
    extra, d_gain_ffn_in[...] = rms_back(hidden[...], gains[2:3, :], d_second)
    total = cotangent[...].astype(F32) + extra
    d_hidden[...] = total
    d_attn, d_gain_attn_out[...] = rms_back(attn_raw[...], gains[1:2, :], total)
    low = d_attn.astype(BF)
    d_attn_low[...] = low
    for h in range(H):
        at = pl.ds(h * rows, rows)
        head = contract(low, out_mat[h * HD : (h + 1) * HD, :], 1, 1).astype(BF)
        d_heads[at, :] = head
        dots[:, at] = turned_line(
            jnp.sum(head.astype(F32) * heads[at, :], axis=1, keepdims=True)
        )


def attend_back_kernel(
    q, d_heads, mass, dots, near, far, k_near, v_near, k_far, v_far, d_queries, d_near, d_far
):
    step = pl.program_id(0)
    middle = pl.num_programs(0) // 2

    @pl.when(step == 0)
    def _():
        d_queries[...] = jnp.zeros_like(d_queries)

    def section(probs, k, v, out):
        d_probs = contract(v[...], d_heads[...], 1, 1)
        chance = probs[...].astype(F32) * (1.0 / mass[...])
        d_scores = (chance * (d_probs - dots[...])).astype(BF)
        out[:, :HD] = contract(d_scores, q[...], 1, 0).astype(BF)
        out[:, HD:] = contract(chance.astype(BF), d_heads[...], 1, 0).astype(BF)
        d_queries[...] += contract(k[...], d_scores, 0, 0)

    @pl.when(step < middle)
    def _():
        section(near, k_near, v_near, d_near)

    @pl.when(step >= middle)
    def _():
        section(far, k_far, v_far, d_far)


def attend_back(queries, d_heads, mass, dots, probs, pairs):
    head_rows = queries.shape[0]
    keys = pairs[0].shape[0]
    steps = 2 * keys // KEY_BLOCK
    whole = pl.BlockSpec((head_rows, HD), lambda i: (0, 0))
    line = pl.BlockSpec((1, head_rows), lambda i: (0, 0))
    key_blocks, value_blocks = [halves_of((KEY_BLOCK, HD), steps, c) for c in (0, 1)]
    return pl.pallas_call(
        attend_back_kernel,
        grid=(steps,),
        in_specs=[
            whole,
            whole,
            line,
            line,
            *halves_of((KEY_BLOCK, head_rows), steps),
            key_blocks[0],
            value_blocks[0],
            key_blocks[1],
            value_blocks[1],
        ],
        out_specs=[
            pl.BlockSpec((HD, head_rows), lambda i: (0, 0)),
            *halves_of((KEY_BLOCK, 2 * HD), steps),
        ],
        out_shape=[
            jax.ShapeDtypeStruct((HD, head_rows), F32),
            jax.ShapeDtypeStruct((keys, 2 * HD), BF),
            jax.ShapeDtypeStruct((keys, 2 * HD), BF),
        ],
        compiler_params=pltpu.CompilerParams(vmem_limit_bytes=VMEM_LIMIT),
        cost_estimate=pl.CostEstimate(
            flops=16 * keys * head_rows * HD,
            bytes_accessed=2 * keys * (head_rows + 4 * HD) * 2,
            transcendentals=0,
        ),
        name="attend_back",
    )(queries, d_heads, mass, dots, *probs, pairs[0], pairs[0], pairs[1], pairs[1])


def spread_rows(product, mine, size, keep, send, first):
    step = keep.shape[0] // 2
    width = product.shape[1]
    for offset in range(4):
        rows = product[pl.ds(pl.multiple_of((mine ^ offset) * size, 32), size), :]
        out = send if offset % 2 else keep
        begin = offset // 2 * step + first
        out[begin : begin + size, :width] = rows.astype(out.dtype)


def query_back_kernel(
    mine, d_queries, query_raw, gains, cosine, sine, query_mat, first_low, heads_low, d_attn_low,
    keep, send, d_first, d_gain, product, out_product, query_low,
):
    rows = first_low.shape[0]
    gain = gains[0:1, :]
    d_gain[...] = jnp.zeros_like(d_gain)
    for h in range(H):
        columns = pl.ds(h * HD, HD)
        head = d_queries[:, h * rows : (h + 1) * rows].T * HD ** (-0.5)
        head = rotate(head, cosine[...], -sine[...])
        d_raw, d_head_gain = rms_back(query_raw[:, columns], gain, head)
        d_gain[...] += d_head_gain
        query_low[:, columns] = d_raw.astype(BF)
    d_first[...] = contract(query_low[...], query_mat[...], 1, 1)
    model, inner = product.shape[0] // 4, out_product.shape[0] // 4
    keep[...] = jnp.zeros_like(keep)
    send[...] = jnp.zeros_like(send)
    product[...] = contract(first_low[...], query_low[...], 0, 0)
    spread_rows(product, mine[0], model, keep, send, 0)
    out_product[...] = contract(heads_low[...], d_attn_low[...], 0, 0)
    spread_rows(out_product, mine[0], inner, keep, send, model)


def key_back_kernel(
    mine, sums, *refs
):
    terms, refs = refs[:-19], refs[-19:]
    (
        key_raw, gains, head_gains, cosine, sine, pair_mat, first_low, d_first_query, tokens, d_hidden,
        d_gain_attn_out, d_gain_ffn_in, d_gain_ffn_out, d_gain_query,
        grad_tokens, keep, send, product, gain_lines,
    ) = refs
    total = sums[...]
    for term in terms:
        total = total + term[...].astype(F32)
    d_key = rotate(total[:, :HD], cosine[...], -sine[...])
    d_raw, d_gain_key = rms_back(key_raw[...], head_gains[1:2, :], d_key)
    low = jnp.concatenate([d_raw, total[:, HD:]], axis=1).astype(BF)
    d_first = d_first_query[...] + contract(low, pair_mat[...], 1, 1)
    extra, d_gain_attn_in = rms_back(tokens[...].astype(F32), gains[0:1, :], d_first)
    grad_tokens[...] = d_hidden[...] + extra
    product[:, : 2 * HD] = contract(first_low[...], low, 0, 0)
    gain_lines[...] = jnp.zeros_like(gain_lines)
    for i, line in enumerate(
        (d_gain_attn_in, d_gain_attn_out[...], d_gain_ffn_in[...], d_gain_ffn_out[...])
    ):
        gain_lines[i : i + 1, :] = line
    size, head_size = product.shape[0] // 4, HD // 4
    for i, line in enumerate((d_gain_query[...], d_gain_key)):
        pieces = []
        for r in range(4):
            pieces += [line[:, r * head_size : (r + 1) * head_size], jnp.zeros((1, size - head_size), F32)]
        gain_lines[4 + i : 5 + i, :] = jnp.concatenate(pieces, axis=1)
    product[:, 2 * HD :] = gain_lines[...].T
    keep[...] = jnp.zeros_like(keep)
    send[...] = jnp.zeros_like(send)
    spread_rows(product, mine[0], size, keep, send, 0)


def left_of(owner, part):
    return pl.multiple_of(owner * part - part % 128 * (owner % 2), 128)


def carve_kernel(part, place, w, own, core, near, corner):
    wide, step = own.shape[2], pl.program_id(0)
    mine, low, high = place[0], place[1], place[2]
    for offset, out in enumerate((own, core)):
        out[...] = w[:, :, pl.ds(left_of(mine ^ offset, part), wide)]

    @pl.when(step // (pl.num_programs(0) // 2) == low)
    def _():
        for offset, out in ((2, near), (3, corner)):
            out[...] = w[pl.ds(high, 1), :, pl.ds(left_of(mine ^ offset, part), wide)]


def carve(w, place, part, wide):
    rows, step = w.shape[1], 48
    half = rows // 2 // step

    def quarter(i, p):
        return (0, jnp.clip(i - half * p[1], 0, half - 1), 0)

    return pl.pallas_call(
        functools.partial(carve_kernel, part),
        grid_spec=pltpu.PrefetchScalarGridSpec(
            num_scalar_prefetch=1,
            grid=(rows // step,),
            in_specs=[pl.BlockSpec((2, step, w.shape[2]), lambda i, p: (0, i, 0))],
            out_specs=[pl.BlockSpec((2, step, wide), lambda i, p: (0, i, 0))] * 2
            + [pl.BlockSpec((1, step, wide), quarter)] * 2,
        ),
        out_shape=[jax.ShapeDtypeStruct((2, rows, wide), BF)] * 2
        + [jax.ShapeDtypeStruct((1, rows // 2, wide), BF)] * 2,
        compiler_params=pltpu.CompilerParams(vmem_limit_bytes=VMEM_LIMIT),
        name="carve",
    )(place, w)


def walk(shape, first, count, scalars, dim=0):
    def place(i, *unused):
        return tuple(jnp.clip(i - first, 0, count - 1) if d == dim else 0 for d in range(len(shape)))

    return pl.BlockSpec(shape, place)


def settle_kernel(counts, places, *refs):
    out, sources = refs[-1], refs[:-1]
    step, first = pl.program_id(0), 0
    for source, count in zip(sources, counts):

        @pl.when((step >= first) & (step < first + count))
        def _(source=source):
            out[...] = source[...]

        first += count


def settle(places, rows, *sources):
    counts = [source.shape[0] // rows for source in sources]
    width = sources[0].shape[1]
    starts = [sum(counts[:i]) for i in range(len(counts))]
    return pl.pallas_call(
        functools.partial(settle_kernel, counts),
        grid_spec=pltpu.PrefetchScalarGridSpec(
            num_scalar_prefetch=1,
            grid=(sum(counts),),
            in_specs=[walk((rows, width), f, c, 1) for f, c in zip(starts, counts)],
            out_specs=pl.BlockSpec((rows, width), lambda i, p: (p[i], 0)),
        ),
        out_shape=jax.ShapeDtypeStruct((sum(counts) * rows, width), sources[0].dtype),
        compiler_params=pltpu.CompilerParams(vmem_limit_bytes=VMEM_LIMIT),
        name="settle",
    )(places, *sources)


def lay_kernel(sides, rows, *refs):
    out, sources = refs[-1], refs[:-1]
    step = pl.program_id(0)
    width = out.shape[3]
    for i, source in enumerate([sources[0]] * 4 + [sources[1]] * 4 + list(sources[2:])):

        @pl.when(step == i)
        def _(source=source):
            for block in range(out.shape[1]):
                out[0, block] = source[0, :, block * width : (block + 1) * width]


def lay(sides, rows, own, core, quarters):
    half, wide = own.shape[1] // 2, own.shape[2]
    shape = (1, half, wide)

    def run(first):
        def place(i, s, r):
            j = jnp.clip(i - first, 0, 3)
            return (j // 2, j % 2, 0)

        return pl.BlockSpec(shape, place)

    still = pl.BlockSpec(shape, lambda i, s, r: (0, 0, 0))
    return pl.pallas_call(
        lay_kernel,
        grid_spec=pltpu.PrefetchScalarGridSpec(
            num_scalar_prefetch=2,
            grid=(16,),
            in_specs=[run(0), run(4)] + [still] * 8,
            out_specs=pl.BlockSpec(
                (1, wide // 256, half, 256), lambda i, s, r: (s[i], 0, r[i], 0)
            ),
        ),
        out_shape=jax.ShapeDtypeStruct((2, wide // 256, 8 * half, 256), BF),
        compiler_params=pltpu.CompilerParams(vmem_limit_bytes=VMEM_LIMIT),
        name="lay",
    )(sides, rows, own, core, *quarters)


def contract(left, right, left_dim, right_dim):
    return lax.dot_general(
        left, right, (((left_dim,), (right_dim,)), ((), ())), preferred_element_type=F32
    )


def gelu_and_slope(x):
    scale = math.sqrt(2.0 / math.pi)
    square = x * x
    turn = jnp.tanh(x * (scale + (scale * 0.044715) * square))
    share = 0.5 + 0.5 * turn
    slope = share + (0.5 * x) * (1.0 - turn * turn) * (scale + (3 * scale * 0.044715) * square)
    return x * share, slope


def ffn_factors_kernel(second, w_gate, w_up, act, value, factor):
    rows, slab = second.shape[0], 256

    def products(r):
        at = pl.ds(r * slab, slab)
        return contract(second[at, :], w_gate[0, 0], 1, 0), contract(second[at, :], w_up[0, 0], 1, 0)

    ahead = products(0)
    for r in range(rows // slab):
        at = pl.ds(r * slab, slab)
        gate, upper = ahead
        if r + 1 < rows // slab:
            ahead = products(r + 1)
        gelu, slope = gelu_and_slope(gate)
        act[at, :] = (gelu * upper).astype(BF)
        value[at, :] = gelu.astype(BF)
        factor[at, :] = (upper * slope).astype(BF)


def ffn_factors(second_all, in_mat, first, last):
    tokens, model = second_all.shape
    slab, width = min(2048, tokens), 256
    columns = (last - first) * width
    return pl.pallas_call(
        ffn_factors_kernel,
        grid=(last - first, tokens // slab),
        in_specs=[
            pl.BlockSpec((slab, model), lambda j, t: (t, 0)),
            pl.BlockSpec((1, 1, model, width), lambda j, t: (0, j + first, 0, 0)),
            pl.BlockSpec((1, 1, model, width), lambda j, t: (1, j + first, 0, 0)),
        ],
        out_specs=[pl.BlockSpec((slab, width), lambda j, t: (t, j))] * 3,
        out_shape=[jax.ShapeDtypeStruct((tokens, columns), BF)] * 3,
        compiler_params=pltpu.CompilerParams(vmem_limit_bytes=VMEM_ALL),
        cost_estimate=pl.CostEstimate(
            flops=4 * tokens * model * columns,
            bytes_accessed=2 * tokens * model * (last - first) + 6 * tokens * columns,
            transcendentals=tokens * columns,
        ),
        name="ffn_factors",
    )(second_all, in_mat, in_mat)


def ffn_gradients_kernel(part, first, blocks, mine, second, d_ffn, act, value, factor, w_down, *rest):
    outs, down_rows, d_both, both_sum, down_sum, sem = rest[-9:-5], *rest[-5:]
    step = pl.program_id(1)
    rows, slab = second.shape[0], 256
    width = act.shape[1]

    def products(r):
        return contract(d_ffn[pl.ds(r * slab, slab), :], w_down[...], 1, 1)

    ahead = products(0)
    for r in range(rows // slab):
        at = pl.ds(r * slab, slab)
        d_act = ahead
        if r + 1 < rows // slab:
            ahead = products(r + 1)
        d_both[at, :width] = (d_act * factor[at, :].astype(F32)).astype(BF)
        d_both[at, width:] = (d_act * value[at, :].astype(F32)).astype(BF)
    grad_both = contract(second[...], d_both[...], 0, 0)
    grad_down = contract(act[...], d_ffn[...], 0, 0)

    @pl.when(step == 0)
    def _():
        both_sum[...] = grad_both
        down_sum[...] = grad_down

    @pl.when(step > 0)
    def _():
        both_sum[...] += grad_both
        down_sum[...] += grad_down

    @pl.when(step == pl.num_programs(1) - 1)
    def _():
        block = first + pl.program_id(0)
        odd = mine[0] % 2
        extra = blocks * width - part
        begins = (block == 0) & (odd == 1)
        ends = (block == blocks - 1) & (odd == 0)

        def put(source, at, size):
            copy = pltpu.make_async_copy(
                down_sum.at[pl.ds(source, size), :], down_rows.at[pl.ds(at, size), :], sem
            )
            copy.start()
            copy.wait()

        @pl.when(begins)
        def _():
            put(extra, 0, width - extra)

        @pl.when(ends)
        def _():
            put(0, (blocks - 1) * width, width - extra)

        @pl.when(jnp.logical_not(begins | ends))
        def _():
            put(0, pl.multiple_of(block * width - odd * extra, 64), width)

        quarter = second.shape[1] // 4
        for offset, out in enumerate(outs):
            at = pl.ds(pl.multiple_of((mine[0] ^ offset) * quarter, 32), quarter)
            out[0] = both_sum[at, :width].astype(BF)
            out[1] = both_sum[at, width:].astype(BF)


def ffn_gradients(mine, second_all, d_ffn_all, factors, down_mat, part, first, last, down_rows):
    tokens, model = second_all.shape
    slab, width = min(2048, tokens), 256
    columns = (last - first) * width
    tall = pl.BlockSpec((slab, model), lambda j, t, m: (t, 0))
    tile = pl.BlockSpec((slab, width), lambda j, t, m: (t, j))
    anywhere = pl.BlockSpec(memory_space=pl.ANY)
    earlier = [] if down_rows is None else [down_rows]
    return pl.pallas_call(
        functools.partial(ffn_gradients_kernel, part, first, down_mat.shape[0] // width),
        grid_spec=pltpu.PrefetchScalarGridSpec(
            num_scalar_prefetch=1,
            grid=(last - first, tokens // slab),
            in_specs=[
                tall,
                tall,
                tile,
                tile,
                tile,
                pl.BlockSpec((width, model), lambda j, t, m: (j + first, 0)),
            ]
            + [anywhere] * len(earlier),
            out_specs=[pl.BlockSpec((2, model // 4, width), lambda j, t, m: (0, 0, j))] * 4
            + [anywhere],
            scratch_shapes=[
                pltpu.VMEM((slab, 2 * width), BF),
                pltpu.VMEM((model, 2 * width), F32),
                pltpu.VMEM((width, model), F32),
                pltpu.SemaphoreType.DMA,
            ],
        ),
        out_shape=[jax.ShapeDtypeStruct((2, model // 4, columns), BF)] * 4
        + [jax.ShapeDtypeStruct((part, model), F32)],
        input_output_aliases={7: 4} if earlier else {},
        compiler_params=pltpu.CompilerParams(vmem_limit_bytes=VMEM_ALL),
        cost_estimate=pl.CostEstimate(
            flops=8 * tokens * model * columns,
            bytes_accessed=4 * tokens * model * (last - first) + 6 * tokens * columns,
            transcendentals=0,
        ),
        name="ffn_gradients",
    )(mine[None], second_all, d_ffn_all, *factors, down_mat, *earlier)


def ffn_forward_kernel(near, far, w_gate, w_up, w_down, gate, up, keep, send, act, total):
    step, half = pl.program_id(0), near.shape[0]

    @pl.when(step == 0)
    def _():
        total[...] = jnp.zeros_like(total)

    def products(rows):
        return contract(rows[...], w_gate[0, 0], 1, 0), contract(rows[...], w_up[0, 0], 1, 0)

    ahead = products(near)
    for i in range(2):
        at = pl.ds(i * half, half)
        left, right = ahead
        if i == 0:
            ahead = products(far)
        gate[at, :], up[at, :] = left, right
        act[at, :] = (gelu_and_slope(left)[0] * right).astype(BF)
    total[...] += contract(act[...], w_down[...], 1, 0)

    @pl.when(step == pl.num_programs(0) - 1)
    def _():
        keep[...], send[...] = total[:half, :], total[half:, :].astype(BF)


def ffn_backward_kernel(near, far, gate, up, w_gate, w_up, w_down, keep, send, d_gate, d_up, total):
    step, half = pl.program_id(0), near.shape[0]

    @pl.when(step == 0)
    def _():
        total[...] = jnp.zeros_like(total)

    ahead = contract(near[...], w_down[...], 1, 1)
    for i in range(2):
        at = pl.ds(i * half, half)
        d_act = ahead
        if i == 0:
            ahead = contract(far[...], w_down[...], 1, 1)
        value, slope = gelu_and_slope(gate[at, :])
        d_gate[at, :] = (d_act * up[at, :] * slope).astype(BF)
        d_up[at, :] = (d_act * value).astype(BF)
    total[...] += contract(d_gate[...], w_gate[0, 0], 1, 1) + contract(d_up[...], w_up[0, 0], 1, 1)

    @pl.when(step == pl.num_programs(0) - 1)
    def _():
        keep[...], send[...] = total[:half, :], total[half:, :].astype(BF)


def ffn_group(kernel, near, far, in_mat, down_mat, *kept):
    half, model = near.shape
    wide, width = down_mat.shape[0], 256
    rows = pl.BlockSpec((half, model), lambda j: (0, 0))
    column = pl.BlockSpec((2 * half, width), lambda j: (0, j))
    forward = not kept
    shape = jax.ShapeDtypeStruct((2 * half, wide), F32)
    return pl.pallas_call(
        kernel,
        grid=(wide // width,),
        in_specs=[rows, rows]
        + [column] * len(kept)
        + [
            pl.BlockSpec((1, 1, model, width), lambda j: (0, j, 0, 0)),
            pl.BlockSpec((1, 1, model, width), lambda j: (1, j, 0, 0)),
            pl.BlockSpec((width, model), lambda j: (j, 0)),
        ],
        out_specs=[column] * (2 * forward) + [rows, rows],
        out_shape=[shape] * (2 * forward)
        + [jax.ShapeDtypeStruct((half, model), F32), jax.ShapeDtypeStruct((half, model), BF)],
        scratch_shapes=[pltpu.VMEM((2 * half, width), BF)] * (1 if forward else 2)
        + [pltpu.VMEM((2 * half, model), F32)],
        compiler_params=pltpu.CompilerParams(vmem_limit_bytes=VMEM_ALL),
        cost_estimate=pl.CostEstimate(
            flops=12 * half * model * wide,
            bytes_accessed=6 * model * wide + 16 * half * wide,
            transcendentals=2 * half * wide,
        ),
        name="ffn_forward" if forward else "ffn_backward",
    )(near, far, *kept, in_mat, in_mat, down_mat)


def unfold_kernel(part, mine, *refs):
    out, sources = refs[-1], refs[:-1]
    ranges = len(sources) // 4
    extra = part % 128
    for m in range(4):

        @pl.when(mine[0] == m)
        def _(m=m):
            for side in range(2):
                rows = [
                    jnp.concatenate(
                        [sources[r * 4 + (m ^ owner)][side] for r in range(ranges)], axis=1
                    ).astype(F32)
                    for owner in range(4)
                ]
                wide = rows[0].shape[1]
                cut = wide - 128
                left = lax.broadcasted_iota(jnp.int32, (rows[0].shape[0], 128), 1) < extra
                pieces = []
                for even, odd in (rows[:2], rows[2:]):
                    shared = jnp.where(left, even[:, cut:], odd[:, :128])
                    pieces += [even[:, :cut], shared, odd[:, 128:]]
                out[:, side, :] = jnp.concatenate(pieces, axis=1)


def unfold(mine, part, ranges):
    sources = [piece for pieces in ranges for piece in pieces]
    rows, step = sources[0].shape[1], 16
    return pl.pallas_call(
        functools.partial(unfold_kernel, part),
        grid_spec=pltpu.PrefetchScalarGridSpec(
            num_scalar_prefetch=1,
            grid=(rows // step,),
            in_specs=[
                pl.BlockSpec((2, step, s.shape[2]), lambda i, m: (0, i, 0)) for s in sources
            ],
            out_specs=pl.BlockSpec((step, 2, 4 * part), lambda i, m: (i, 0, 0)),
        ),
        out_shape=jax.ShapeDtypeStruct((rows, 2, 4 * part), F32),
        compiler_params=pltpu.CompilerParams(vmem_limit_bytes=VMEM_LIMIT),
        name="unfold",
    )(mine[None], *sources)


def pick(table, index):
    hit = index[:, None] == jnp.arange(table.shape[0], dtype=jnp.int32)[None, :]
    return jnp.sum(jnp.where(hit, table[None, :], 0), axis=1)


def body(
    tokens,
    cotangent,
    block_table,
    sequence_ids,
    w_query,
    w_key,
    w_value,
    w_out,
    w_in,
    w_down,
    gain_attn_in,
    gain_attn_out,
    gain_ffn_in,
    gain_ffn_out,
    gain_query,
    gain_key,
):
    rows = tokens.shape[0]
    block = rows // 2
    model, part = w_in.shape[0] * 4, w_down.shape[0]
    mine = lax.axis_index("fsdp")
    me = lax.axis_index("ctx") * 4 + mine

    gains = (gain_attn_in, gain_attn_out, gain_ffn_in, gain_ffn_out, gain_query, gain_key)
    sizes = [g.shape[0] for g in gains]
    pair_flow = Flow(gather_rows(jnp.concatenate([w_key, w_value], axis=1), mine))
    packed = jnp.concatenate(gains).astype(F32)[None]
    gains_flow = Flow(iter_once([swap(packed, o) for o in (1, 2, 3)]))

    wide = -(-part // 256) * 256
    quarter = model // 4
    boundary = jnp.sum((sequence_ids == 0).astype(jnp.int32))
    everyone = me ^ jnp.array(wide_offsets(), jnp.int32)
    blocks = pick(block_table, jnp.stack([2 * everyone, 2 * everyone + 1], axis=1).reshape(-1))
    place = (blocks[:2, None] * block + jnp.arange(block, dtype=jnp.int32)[None, :]).reshape(-1)
    start = jnp.where(place >= boundary, boundary, 0)
    position = place - start
    inverse_angle = 1000000.0 ** (-jnp.arange(HD // 2, dtype=F32) / (HD // 2))
    angles = position.astype(F32)[:, None] * inverse_angle[None, :]
    cosine, sine = jnp.cos(angles), jnp.sin(angles)
    q_place, q_start = jnp.tile(place, H)[None], jnp.tile(start, H)[None]

    low_bit, high_bit = lax.axis_index("ctx") % 2, lax.axis_index("ctx") // 2 % 2
    own, to_core, to_x, to_corner = carve(
        jnp.swapaxes(w_in, 0, 1), jnp.stack([mine, low_bit, high_bit]), part, wide
    )
    own, to_core, to_x, to_corner = pace((own, to_core, to_x, to_corner), pair_flow)
    columns_flow = Flow(exchange_columns((to_x, to_corner)))

    cosine, sine, q_place, q_start, w_query = pace(
        (cosine, sine, q_place, q_start, w_query), gains_flow, pair_flow
    )
    query_flow = Flow(gather_rows(w_query, mine))
    model_gains, head_gains = kernel_call(
        gains_kernel,
        [((8, model), F32), ((8, HD), F32)],
        packed,
        *gains_flow.result,
        scalars=(mine[None],),
        name="gains",
    )
    pair_mat = pair_flow.result
    first_low, key_raw, pair_rows = kernel_call(
        key_kernel,
        [((rows, model), BF), ((rows, HD), F32), ((rows, 2 * HD), BF)],
        tokens,
        model_gains,
        head_gains,
        pair_mat,
        cosine,
        sine,
        name="keys",
    )
    pairs_flow = Flow(gather_wide(pair_rows))
    pace((), pairs_flow, columns_flow)
    to_core, w_out, w_down = pace(
        (to_core, w_out, w_down), pairs_flow, query_flow, columns_flow
    )
    out_flow = Flow(gather_rows(w_out, mine))
    from_core = swap(to_core, 1)
    query_mat = finish(query_flow)
    query_raw, queries = kernel_call(
        query_kernel,
        [((rows, H * HD), F32), ((H * rows, HD), BF)],
        first_low,
        head_gains,
        query_mat,
        cosine,
        sine,
        name="queries",
    )
    down_mat = lax.dynamic_update_slice_in_dim(
        jnp.zeros((wide, model), BF), w_down, part % 128 * (mine % 2), 0
    )
    queries, down_mat = pace((queries, down_mat), pairs_flow, columns_flow)
    pairs = finish(pairs_flow)
    *probs, weighted, mass = attend(blocks, queries, q_place, q_start, *pairs)
    weighted, mass = pace((weighted, mass), out_flow)
    out_mat = finish(out_flow)
    heads, heads_low, attn_raw, hidden, second_low = kernel_call(
        after_attend_kernel,
        [
            ((H * rows, HD), F32),
            ((rows, H * HD), BF),
            ((rows, model), F32),
            ((rows, model), F32),
            ((rows, model), BF),
        ],
        weighted,
        mass,
        out_mat,
        tokens,
        model_gains,
        name="after_attend",
    )

    group_flow = Flow(gather_group(second_low))
    second_all = lax.all_gather(second_low, AXES, axis=0, tiled=True)
    sides, halves = [], []
    for offset in (0, 1):
        sides += [0, 0, 1, 1]
        halves += [(mine ^ offset) * 2 + bit for bit in (0, 1, 0, 1)]
    for offset in (2, 3):
        sides += [high_bit, high_bit, 1 - high_bit, 1 - high_bit]
        halves += [(mine ^ offset) * 2 + bit for bit in (low_bit, 1 - low_bit) * 2]
    pace((), group_flow, columns_flow)
    from_x, from_corner = finish(columns_flow)
    in_mat = lay(
        jnp.stack([jnp.asarray(s, jnp.int32) for s in sides]),
        jnp.stack(halves),
        own,
        from_core,
        (*from_x, *from_corner),
    )
    gate, upper, keep, send = ffn_group(ffn_forward_kernel, *finish(group_flow), in_mat, down_mat)
    block_out, d_ffn_low, d_gain_ffn_out = kernel_call(
        after_ffn_kernel,
        [((rows, model), BF), ((rows, model), BF), ((1, model), F32)],
        *finish(Flow(scatter_group(keep, send))),
        hidden,
        cotangent,
        model_gains,
        name="after_ffn",
    )
    group_flow = Flow(gather_group(d_ffn_low))
    d_ffn_all = lax.all_gather(d_ffn_low, AXES, axis=0, tiled=True)
    keep, send = ffn_group(
        ffn_backward_kernel, *finish(group_flow), in_mat, down_mat, gate, upper
    )
    d_hidden, d_attn_low, d_heads, dots, d_gain_ffn_in, d_gain_attn_out = kernel_call(
        before_attend_back_kernel,
        [
            ((rows, model), F32),
            ((rows, model), BF),
            ((H * rows, HD), BF),
            ((1, H * rows), F32),
            ((1, model), F32),
            ((1, model), F32),
        ],
        *finish(Flow(scatter_group(keep, send))),
        hidden,
        cotangent,
        model_gains,
        attn_raw,
        out_mat,
        heads,
        name="before_attend_back",
    )

    d_queries, *d_pairs = attend_back(queries, d_heads, mass, dots, probs, pairs)
    sums_flow = Flow(scatter_wide(*d_pairs))
    early_rows = -(-(quarter + H * HD // 4) // 128) * 128
    tail_rows = -(-quarter // 128) * 128
    keep, send, d_first_query, d_gain_query = kernel_call(
        query_back_kernel,
        [
            ((2 * early_rows, model), F32),
            ((2 * early_rows, model), BF),
            ((rows, model), F32),
            ((1, HD), F32),
        ],
        d_queries,
        query_raw,
        head_gains,
        cosine,
        sine,
        query_mat,
        first_low,
        heads_low,
        d_attn_low,
        scalars=(mine[None],),
        scratch=[((model, H * HD), F32), ((H * HD, model), F32), ((rows, H * HD), BF)],
        name="query_back",
    )
    blocks_of_columns = wide // 256
    cuts = [0] + [blocks_of_columns - 2 * i for i in (3, 2, 1, 0)]
    factors = []

    def factors_step(index, values, *flows):
        values, second = values
        factors.append(ffn_factors(second, in_mat, cuts[index], cuts[index + 1]))
        (values, second), factors[-1] = pace(((values, second), factors[-1]), *flows)
        return values, second

    keep, send, d_first_query, second_all = pace(
        (keep, send, d_first_query, second_all), sums_flow
    )
    early_flow = Flow(scatter_group(keep, send))
    d_first_query, second_all = factors_step(0, (d_first_query, second_all), sums_flow, early_flow)
    d_first_query, second_all = factors_step(1, (d_first_query, second_all), sums_flow)
    d_first_query, second_all = factors_step(2, (d_first_query, second_all), sums_flow, early_flow)
    grad_tokens, keep, send = kernel_call(
        key_back_kernel,
        [
            ((rows, model), F32),
            ((2 * tail_rows, 2 * HD + 128), F32),
            ((2 * tail_rows, 2 * HD + 128), BF),
        ],
        *sums_flow.result,
        key_raw,
        model_gains,
        head_gains,
        cosine,
        sine,
        pair_mat,
        first_low,
        d_first_query,
        tokens,
        d_hidden,
        d_gain_attn_out,
        d_gain_ffn_in,
        d_gain_ffn_out,
        d_gain_query,
        scalars=(mine[None],),
        scratch=[((model, 2 * HD + 128), F32), ((128, model), F32)],
        name="key_back",
    )
    tail_flow = Flow(scatter_group(keep, send))

    def total(flow):
        near, far = flow.result
        return near + far.astype(F32)

    early_flow = Flow(sum_over_ctx(total(early_flow)))
    grad_tokens, second_all = factors_step(3, (grad_tokens, second_all), tail_flow, early_flow)
    both = pace((second_all, d_ffn_all))
    ranges, grad_down = [], None

    def columns_step(*flows):
        nonlocal both, grad_down
        i = len(ranges)
        *pieces, grad_down = ffn_gradients(
            mine, *both, factors[i], down_mat, part, cuts[i], cuts[i + 1], grad_down
        )
        both, grad_down, ranges[:] = pace((both, grad_down, list(ranges)), *flows)
        ranges.append([pieces[0]] + [swap(pieces[o], o) for o in (1, 2, 3)])

    columns_step(tail_flow, early_flow)
    tail_flow = Flow(sum_over_ctx(total(tail_flow)))
    columns_step(tail_flow, early_flow)
    columns_step(tail_flow, early_flow)
    columns_step(tail_flow)
    finish(tail_flow)
    early, tail = early_flow.result, tail_flow.result
    grad_query = early[:quarter, : H * HD]
    grad_out = early[quarter : quarter + w_out.shape[0]]
    grad_key, grad_value = tail[:quarter, :HD], tail[:quarter, HD : 2 * HD]
    gain_grads = [tail[:size, 2 * HD + i] for i, size in enumerate(sizes)]
    grad_in = unfold(mine, part, ranges)

    return (
        block_out,
        grad_tokens,
        grad_query,
        grad_key,
        grad_value,
        grad_out,
        grad_in,
        grad_down,
        *gain_grads,
    )


def solution(mesh):
    in_specs = (
        P(AXES, None),
        P(AXES, None),
        P(),
        P(),
        P("fsdp", None),
        P("fsdp", None),
        P("fsdp", None),
        P("fsdp", None),
        P("fsdp", None, None),
        P("fsdp", None),
        P("fsdp"),
        P("fsdp"),
        P("fsdp"),
        P("fsdp"),
        P("fsdp"),
        P("fsdp"),
    )
    out_specs = (
        P(AXES, None),
        P(AXES, None),
        P("fsdp", None),
        P("fsdp", None),
        P("fsdp", None),
        P("fsdp", None),
        P("fsdp", None, None),
        P("fsdp", None),
        P("fsdp"),
        P("fsdp"),
        P("fsdp"),
        P("fsdp"),
        P("fsdp"),
        P("fsdp"),
    )
    return jax.shard_map(body, mesh=mesh, in_specs=in_specs, out_specs=out_specs, check_vma=False)
```

time: 756 us -> 605 us (0.80)
  waiting for transfers between devices: 236 us -> 126 us
  Pallas kernels: 175 us -> 259 us
  matrix products: 42.9 us -> 0 us
  starting transfers between devices: 109 us -> 69.5 us
  local copies, waits for them, and re-layouts: 121 us -> 91.5 us
  other arithmetic: 58.8 us -> 34.5 us
  between operations: 2.78 us -> 15.9 us
    ppermute x92 -> x74, waiting for transfers between devices: 236 us -> 126 us  [swap(): return lax.ppermute(value, AXES, [(i, i ^ offset) for i in range(count)])]
    pallas_call x4 -> x22, Pallas kernels: 149 us -> 232 us  [the longest x4 113 us: ffn_gradients(): pl.pallas_call(functools.partial(ffn_gradients_kernel, part, first, down_...]
    dot_general x15 -> x0, matrix products: 42.9 us -> none  [the longest x6 22.3 us: dot_columns(): lax.dot_general(left, right, (((1,), (1,)), ((), ())), preferred_element_...]
    ppermute x92 -> x74, starting transfers between devices: 109 us -> 69.4 us  [swap(): return lax.ppermute(value, AXES, [(i, i ^ offset) for i in range(count)])]
    concatenate x15 -> x3, other arithmetic: 22.5 us -> 0.11 us  [join(): return jnp.concatenate(parts, axis=0)]
    unnamed x192 -> x271, local copies, waits for them, and re-layouts: 49.8 us -> 71.1 us
    concatenate x7 -> x5, local copies, waits for them, and re-layouts: 17.9 us -> 1.79 us  [join(): return jnp.concatenate(parts, axis=0)]
  transfers between devices with their start and end apart: 92 -> 76, of which waited for: 35 -> 25; matrix products, arithmetic and copies ran while one was open for 27% -> 10% of each run, Pallas kernels for 11% -> 41%
where the time goes in v2:
time: 605 us; the launch traced here: 596 us
  Pallas kernels  259 us (43%)
  waiting for transfers between devices  126 us (21%)
  local copies, waits for them, and re-layouts  91.5 us (15%)
  starting transfers between devices  69.5 us (11%)
  other arithmetic  34.5 us (6%)
  between operations  15.9 us (3%)
    ppermute x74, waiting for transfers between devices, swap(): return lax.ppermute(value, AXES, [(i, i ^ offset) for i in range(count)])  126 us
    pallas_call x4, Pallas kernels, ffn_gradients(): pl.pallas_call(functools.partial(ffn_gradients_kernel, part, first, down_...  113 us
    unnamed x271, local copies, waits for them, and re-layouts  71.1 us
    ppermute x74, starting transfers between devices, swap(): return lax.ppermute(value, AXES, [(i, i ^ offset) for i in range(count)])  69.4 us
    pallas_call x4, Pallas kernels, ffn_factors(): pl.pallas_call(ffn_factors_kernel, grid=(last - first, tokens // slab), i...  66 us
    pallas_call x2, Pallas kernels, ffn_group(): pl.pallas_call(kernel, grid=(wide // width,), in_specs=[rows, rows] + [co...  30.9 us
  transfers between devices with their start and end apart: 76, of which 25 were waited for; matrix products, arithmetic and copies ran while one was open for 10% of the time, Pallas kernels for 41%

profile of v2, /device:TPU:1, one launch (start us, length us, event | category | flops | bytes accessed | tf_op | source)
XLA Modules:
  0.0 595.9 jit_solution(11963587309780251015)
XLA Ops:
  18.7 7.3 %copy.44 = bf16[288,2,6912]{2,0,1:T(8,128)(2,1)} copy(bf16[288,2,6912]{2,1,0:T(2,128)(2,1)} %param.28) | data formatting | bytes 15925248 | tf_op args[8]
  39.7 3.4 collective-permute-start.7
  43.5 4.1 collective-permute-done.8.refs_2_
  48.1 11.4 %collective-permute-done.9.refs_6_ = bf16[1,144,1792]{2,1,0:T(8,128)(2,1)S(1)} collective-permute-done((bf16[1,144,1792]{2,1,0:T(8,128)(2,1)S(1)}, bf16[1,144,1792]{2,1,0:T(8,128)(2,1)S(1)}, u32[]{:S(2)}, u32[]{:S(2)}) %collective-permute-start.9) | collective-permute-done | bytes 516128 | tf_op jit(solution)/shard_map/ppermute | solution.py:73
  63.3 8.0 %collective-permute-done.12 = bf16[288,1024]{1,0:T(8,128)(2,1)S(1)} collective-permute-done((bf16[288,1024]{1,0:T(8,128)(2,1)S(1)}, bf16[288,1024]{1,0:T(8,128)(2,1)S(1)}, u32[]{:S(2)}, u32[]{:S(2)}) %collective-permute-start.12) | collective-permute-done | bytes 589856 | tf_op jit(solution)/shard_map/ppermute | solution.py:73
  74.1 8.4 %collective-permute-done.11 = bf16[512,512]{1,0:T(8,128)(2,1)S(1)} collective-permute-done((bf16[512,512]{1,0:T(8,128)(2,1)S(1)}, bf16[512,512]{1,0:T(8,128)(2,1)S(1)}, u32[]{:S(2)}, u32[]{:S(2)}) %collective-permute-start.11) | collective-permute-done | bytes 524320 | tf_op jit(solution)/shard_map/ppermute | solution.py:73
  100.0 3.9 collective-permute-done.16
  108.6 7.2 %attend.1 = (bf16[2048,512]{1,0:T(8,128)(2,1)S(1)}, bf16[2048,512]{1,0:T(8,128)(2,1)S(1)}, f32[256,512]{1,0:T(8,128)S(1)}, f32[1,512]{1,0:T(1,128)S(1)}) custom-call(s32[64]{0:T(128)S(1)} %copy-done.102, bf16[512,256]{1,0:T(8,128)(2,1)S(1)} %get-tuple-element.246.q, s32[1,512]{1,0:T(1,128)S(1)} %bitcast.25, s32[1,512]{1,0:T(1,128)S(1)} %bitcast.24, ...), custom_call_target="tpu_custom_call" | custom-call | flops 2147483648 | bytes 8388608 | tf_op jit(solution)/shard_map/attend/pallas_call | solution.py:272
  135.5 10.6 %collective-permute-done.23.refs_3_ = bf16[1,144,1792]{2,1,0:T(8,128)(2,1)S(1)} collective-permute-done((bf16[1,144,1792]{2,1,0:T(8,128)(2,1)}, bf16[1,144,1792]{2,1,0:T(8,128)(2,1)S(1)}, u32[]{:S(2)}, u32[]{:S(2)}) %collective-permute-start.23) | collective-permute-done | bytes 516128 | tf_op jit(solution)/shard_map/ppermute | solution.py:73
  146.9 10.3 %collective-permute-done.24.refs_5_ = bf16[1,144,1792]{2,1,0:T(8,128)(2,1)S(1)} collective-permute-done((bf16[1,144,1792]{2,1,0:T(8,128)(2,1)}, bf16[1,144,1792]{2,1,0:T(8,128)(2,1)S(1)}, u32[]{:S(2)}, u32[]{:S(2)}) %collective-permute-start.24) | collective-permute-done | bytes 516128 | tf_op jit(solution)/shard_map/ppermute | solution.py:73
  171.9 6.5 %lay.1.w_gate.w_up = bf16[2,7,1152,256]{3,2,1,0:T(8,128)(2,1)S(1)} custom-call(s32[16]{0:T(128)S(1)} %stack.74.sides, s32[16]{0:T(128)S(1)} %stack.83.rows, bf16[2,288,1792]{2,1,0:T(8,128)(2,1)S(1)} %copy-done.23, bf16[2,288,1792]{2,1,0:T(8,128)(2,1)} %collective-permute-done.27.refs_1_, bf16[1,144,1792]{2,1,0:T(8,128)(2,1)S(1)} %copy-done.57, ...), custom_call_target="tpu_custom_call" | custom-call | tf_op jit(solution)/shard_map/lay/pallas_call | solution.py:589
  181.8 15.4 %ffn_forward.1 = (f32[512,1792]{1,0:T(8,128)}, f32[512,1792]{1,0:T(8,128)}, f32[256,1152]{1,0:T(8,128)}, bf16[256,1152]{1,0:T(8,128)(2,1)}) custom-call(bf16[256,1152]{1,0:T(8,128)(2,1)} %constant_dynamic-update-slice_fusion.18.near, bf16[256,1152]{1,0:T(8,128)(2,1)} %collective-permute-done.26.far, bf16[2,7,1152,256]{3,2,1,0:T(8,128)(2,1)} %copy-done, ...), custom_call_target="tpu_custom_call" | custom-call | flops 6341787648 | bytes 19726336 | tf_op jit(solution)/shard_map/ffn_forward/pallas_call | solution.py:826
  201.0 8.6 %collective-permute-done.29.other = bf16[128,1152]{1,0:T(8,128)(2,1)S(1)} collective-permute-done((bf16[128,1152]{1,0:T(8,128)(2,1)S(1)}, bf16[128,1152]{1,0:T(8,128)(2,1)S(1)}, u32[]{:S(2)}, u32[]{:S(2)}) %collective-permute-start.29) | collective-permute-done | bytes 294944 | tf_op jit(solution)/shard_map/ppermute | solution.py:73
  212.7 6.8 %collective-permute-done.30 = bf16[128,1152]{1,0:T(8,128)(2,1)S(1)} collective-permute-done((bf16[128,1152]{1,0:T(8,128)(2,1)}, bf16[128,1152]{1,0:T(8,128)(2,1)S(1)}, u32[]{:S(2)}, u32[]{:S(2)}) %collective-permute-start.30) | collective-permute-done | bytes 294944 | tf_op jit(solution)/shard_map/ppermute | solution.py:73
  223.8 15.5 %ffn_backward.1 = (f32[256,1152]{1,0:T(8,128)}, bf16[256,1152]{1,0:T(8,128)(2,1)}) custom-call(bf16[256,1152]{1,0:T(8,128)(2,1)} %copy-done.114, bf16[256,1152]{1,0:T(8,128)(2,1)} %copy-done.122, f32[512,1792]{1,0:T(8,128)} %get-tuple-element.273.gate, f32[512,1792]{1,0:T(8,128)} %get-tuple-element.274.up, bf16[2,7,1152,256]{3,2,1,0:T(8,128)(2,1)} %copy-done, ...), custom_call_target="tpu_custom_call" | custom-call | flops 6341787648 | bytes 19726336 | tf_op jit(solution)/shard_map/ffn_backward/pallas_call | solution.py:826
  243.0 14.8 %collective-permute-done.33.other = bf16[128,1152]{1,0:T(8,128)(2,1)S(1)} collective-permute-done((bf16[128,1152]{1,0:T(8,128)(2,1)S(1)}, bf16[128,1152]{1,0:T(8,128)(2,1)S(1)}, u32[]{:S(2)}, u32[]{:S(2)}) %collective-permute-start.33) | collective-permute-done | bytes 294944 | tf_op jit(solution)/shard_map/ppermute | solution.py:73
  266.1 6.9 %attend_back.1 = (f32[256,512]{1,0:T(8,128)S(1)}, bf16[2048,512]{1,0:T(8,128)(2,1)S(1)}, bf16[2048,512]{1,0:T(8,128)(2,1)S(1)}) custom-call(bf16[512,256]{1,0:T(8,128)(2,1)S(1)} %copy-done.80, bf16[512,256]{1,0:T(8,128)(2,1)S(1)} %get-tuple-element.279.d_heads, f32[1,512]{1,0:T(1,128)S(1)} %copy-done.98, f32[1,512]{1,0:T(1,128)S(1)} %get-tuple-element.280.dots, ...), custom_call_target="tpu_custom_call" | custom-call | flops 4294967296 | bytes 12582912 | tf_op jit(solution)/shard_map/attend_back/pallas_call | solution.py:386
  284.0 5.0 convert_add_fusion
  290.5 11.6 %ffn_factors.4 = (bf16[4096,256]{1,0:T(8,128)(2,1)}, bf16[4096,256]{1,0:T(8,128)(2,1)}, bf16[4096,256]{1,0:T(8,128)(2,1)}) custom-call(bf16[4096,1152]{1,0:T(8,128)(2,1)} %all-gather.3.cloned.1.call-done.second, bf16[2,7,1152,256]{3,2,1,0:T(8,128)(2,1)} %copy-done, bf16[2,7,1152,256]{3,2,1,0:T(8,128)(2,1)} %copy-done), custom_call_target="tpu_custom_call" | custom-call | flops 4831838208 | bytes 15728640 | tf_op jit(solution)/shard_map/ffn_factors/pallas_call | solution.py:643
  305.2 3.6 add_convert_fusion
  309.0 18.1 %ffn_factors.5 = (bf16[4096,512]{1,0:T(8,128)(2,1)}, bf16[4096,512]{1,0:T(8,128)(2,1)}, bf16[4096,512]{1,0:T(8,128)(2,1)}) custom-call(bf16[4096,1152]{1,0:T(8,128)(2,1)} %all-gather.3.cloned.1.call-done.second, bf16[2,7,1152,256]{3,2,1,0:T(8,128)(2,1)} %copy-done, bf16[2,7,1152,256]{3,2,1,0:T(8,128)(2,1)} %copy-done), custom_call_target="tpu_custom_call" | custom-call | flops 9663676416 | bytes 31457280 | tf_op jit(solution)/shard_map/ffn_factors/pallas_call | solution.py:643
  330.2 3.6 collective-permute-start.42
  334.3 18.1 %ffn_factors.6 = (bf16[4096,512]{1,0:T(8,128)(2,1)}, bf16[4096,512]{1,0:T(8,128)(2,1)}, bf16[4096,512]{1,0:T(8,128)(2,1)}) custom-call(bf16[4096,1152]{1,0:T(8,128)(2,1)} %all-gather.3.cloned.1.call-done.second, bf16[2,7,1152,256]{3,2,1,0:T(8,128)(2,1)} %copy-done, bf16[2,7,1152,256]{3,2,1,0:T(8,128)(2,1)} %copy-done), custom_call_target="tpu_custom_call" | custom-call | flops 9663676416 | bytes 31457280 | tf_op jit(solution)/shard_map/ffn_factors/pallas_call | solution.py:643
  370.5 18.2 %ffn_factors.7 = (bf16[4096,512]{1,0:T(8,128)(2,1)}, bf16[4096,512]{1,0:T(8,128)(2,1)}, bf16[4096,512]{1,0:T(8,128)(2,1)}) custom-call(bf16[4096,1152]{1,0:T(8,128)(2,1)} %all-gather.3.cloned.1.call-done.second, bf16[2,7,1152,256]{3,2,1,0:T(8,128)(2,1)} %copy-done, bf16[2,7,1152,256]{3,2,1,0:T(8,128)(2,1)} %copy-done), custom_call_target="tpu_custom_call" | custom-call | flops 9663676416 | bytes 31457280 | tf_op jit(solution)/shard_map/ffn_factors/pallas_call | solution.py:643
  399.2 19.8 %ffn_gradients.4 = (bf16[2,288,256]{2,1,0:T(8,128)(2,1)}, bf16[2,288,256]{2,1,0:T(8,128)(2,1)}, bf16[2,288,256]{2,1,0:T(8,128)(2,1)}, bf16[2,288,256]{2,1,0:T(8,128)(2,1)}, f32[1728,1152]{1,0:T(8,128)}) custom-call(s32[1]{0:T(128)} %bitcast.2.mine, bf16[4096,1152]{1,0:T(8,128)(2,1)} %all-gather.3.cloned.1.call-done.second, ...), custom_call_target="tpu_custom_call" | custom-call | flops 9663676416 | bytes 25165824 | tf_op jit(solution)/shard_map/ffn_gradients/pallas_call | solution.py:735
  430.1 31.2 %ffn_gradients.5 = (bf16[2,288,512]{2,1,0:T(8,128)(2,1)}, bf16[2,288,512]{2,1,0:T(8,128)(2,1)}, bf16[2,288,512]{2,1,0:T(8,128)(2,1)}, bf16[2,288,512]{2,1,0:T(8,128)(2,1)}, f32[1728,1152]{1,0:T(8,128)}) custom-call(s32[1]{0:T(128)} %bitcast.2.mine, bf16[4096,1152]{1,0:T(8,128)(2,1)} %all-gather.3.cloned.1.call-done.second, ...), custom_call_target="tpu_custom_call", output_to_operand_aliasing={{4}: (7, {})} | custom-call | flops 19327352832 | bytes 50331648 | tf_op jit(solution)/shard_map/ffn_gradients/pallas_call | solution.py:735
  475.5 31.1 %ffn_gradients.6 = (bf16[2,288,512]{2,1,0:T(8,128)(2,1)}, bf16[2,288,512]{2,1,0:T(8,128)(2,1)}, bf16[2,288,512]{2,1,0:T(8,128)(2,1)}, bf16[2,288,512]{2,1,0:T(8,128)(2,1)}, f32[1728,1152]{1,0:T(8,128)}) custom-call(s32[1]{0:T(128)} %bitcast.2.mine, bf16[4096,1152]{1,0:T(8,128)(2,1)} %all-gather.3.cloned.1.call-done.second, ...), custom_call_target="tpu_custom_call", output_to_operand_aliasing={{4}: (7, {})} | custom-call | flops 19327352832 | bytes 50331648 | tf_op jit(solution)/shard_map/ffn_gradients/pallas_call | solution.py:735
  513.8 31.3 %ffn_gradients.7 = (bf16[2,288,512]{2,1,0:T(8,128)(2,1)}, bf16[2,288,512]{2,1,0:T(8,128)(2,1)}, bf16[2,288,512]{2,1,0:T(8,128)(2,1)}, bf16[2,288,512]{2,1,0:T(8,128)(2,1)}, f32[1728,1152]{1,0:T(8,128)}) custom-call(s32[1]{0:T(128)} %bitcast.2.mine, bf16[4096,1152]{1,0:T(8,128)(2,1)} %all-gather.3.cloned.1.call-done.second, ...), custom_call_target="tpu_custom_call", output_to_operand_aliasing={{4}: (7, {})} | custom-call | flops 19327352832 | bytes 50331648 | tf_op jit(solution)/shard_map/ffn_gradients/pallas_call | solution.py:735
  553.5 4.0 collective-permute-done.70
  560.3 4.1 collective-permute-done.72.refs_14_
  564.3 12.8 %collective-permute-done.73.refs_15_ = bf16[2,288,512]{2,1,0:T(8,128)(2,1)S(1)} collective-permute-done((bf16[2,288,512]{2,1,0:T(8,128)(2,1)S(1)}, bf16[2,288,512]{2,1,0:T(8,128)(2,1)S(1)}, u32[]{:S(2)}, u32[]{:S(2)}) %collective-permute-start.73) | collective-permute-done | bytes 589856 | tf_op jit(solution)/shard_map/ppermute | solution.py:73
  577.2 11.4 %unfold.1 = f32[288,2,6912]{2,1,0:T(2,128)} custom-call(s32[1]{0:T(128)} %bitcast.2.mine, bf16[2,288,256]{2,1,0:T(8,128)(2,1)S(1)} %copy-done.72, bf16[2,288,256]{2,1,0:T(8,128)(2,1)S(1)} %copy-done.74, bf16[2,288,256]{2,1,0:T(8,128)(2,1)S(1)} %copy-done.76, bf16[2,288,256]{2,1,0:T(8,128)(2,1)S(1)} %copy-done.78, bf16[2,288,512]{2,1,0:T(8,128)(2,1)S(1)} %copy-done.47, ...), custom_call_target="tpu_custom_call" | custom-call | tf_op jit(solution)/shard_map/unfold/pallas_call | solution.py:879
  (492 shorter events, 207.1 us)
Async XLA Ops:
  7.2 276.8 %all-gather.3.cloned.1.call-start = ((), (), s32[]{:S(2)}) async-start(), calls=%async_computation | async-start | bytes 9732096 | tf_op jit(solution)/shard_map/all_gather | solution.py:1018
  10.7 25.8 %collective-permute-start.2 = (f32[1,1280]{1,0:T(1,128)S(1)}, f32[1,1280]{1,0:T(1,128)S(1)}, u32[]{:S(2)}, u32[]{:S(2)}) collective-permute-start(f32[1,1280]{1,0:T(1,128)S(1)} %convert_element_type.134.refs_0_), channel_id=1, source_target_pairs={{0,3},{1,2},{2,1},{3,0},{4,7},{5,6},{6,5},{7,4},{8,11},{9,10},{10,... | collective-permute-start | bytes 15368 | tf_op jit(solution)/shard_map/ppermute | solution.py:73
  34.8 24.7 %collective-permute-start.9 = (bf16[1,144,1792]{2,1,0:T(8,128)(2,1)S(1)}, bf16[1,144,1792]{2,1,0:T(8,128)(2,1)S(1)}, u32[]{:S(2)}, u32[]{:S(2)}) collective-permute-start(bf16[1,144,1792]{2,1,0:T(8,128)(2,1)S(1)} %get-tuple-element.235), channel_id=1, source_target_pairs={{0,3},{1,2},{2,1},{3,0},{4,7},{5,6},{6,5},{7,4},{8,11},{9,10},{10,... | collective-permute-start | bytes 1548296 | tf_op jit(solution)/shard_map/ppermute | solution.py:73
  47.6 23.7 %collective-permute-start.12 = (bf16[288,1024]{1,0:T(8,128)(2,1)S(1)}, bf16[288,1024]{1,0:T(8,128)(2,1)S(1)}, u32[]{:S(2)}, u32[]{:S(2)}) collective-permute-start(bf16[288,1024]{1,0:T(8,128)(2,1)S(1)} %copy-done.120), channel_id=1, source_target_pairs={{0,2},{1,3},{2,0},{3,1},{4,6},{5,7},{6,4},{7,5},{8,10},{9,11},{10,... | collective-permute-start | bytes 1769480 | tf_op jit(solution)/shard_map/ppermute | solution.py:73
  130.2 258.6 %all-gather.5.cloned.1.call-start = ((), (), s32[]{:S(2)}) async-start(), calls=%async_computation.1 | async-start | bytes 9732096 | tf_op jit(solution)/shard_map/all_gather | solution.py:1046
  130.3 31.7 %collective-permute-start.27 = (bf16[2,288,1792]{2,1,0:T(8,128)(2,1)}, bf16[2,288,1792]{2,1,0:T(8,128)(2,1)}, u32[]{:S(2)}, u32[]{:S(2)}) collective-permute-start(bf16[2,288,1792]{2,1,0:T(8,128)(2,1)} %copy-done.108), channel_id=1, source_target_pairs={{0,1},{1,0},{2,3},{3,2},{4,5},{5,4},{6,7},{7,6},{8,9},{9,8},{10,11... | collective-permute-start | bytes 6193160 | tf_op jit(solution)/shard_map/ppermute | solution.py:73
  131.9 25.3 %collective-permute-start.24 = (bf16[1,144,1792]{2,1,0:T(8,128)(2,1)}, bf16[1,144,1792]{2,1,0:T(8,128)(2,1)S(1)}, u32[]{:S(2)}, u32[]{:S(2)}) collective-permute-start(bf16[1,144,1792]{2,1,0:T(8,128)(2,1)} %copy-done.60), channel_id=1, source_target_pairs={{0,4},{1,5},{2,6},{3,7},{4,0},{5,1},{6,2},{7,3},{8,12},{9,13},{10,... | collective-permute-start | bytes 1548296 | tf_op jit(solution)/shard_map/ppermute | solution.py:73
  132.2 25.9 %collective-permute-start.25 = (bf16[1,144,1792]{2,1,0:T(8,128)(2,1)}, bf16[1,144,1792]{2,1,0:T(8,128)(2,1)S(1)}, u32[]{:S(2)}, u32[]{:S(2)}) collective-permute-start(bf16[1,144,1792]{2,1,0:T(8,128)(2,1)} %copy-done.62), channel_id=1, source_target_pairs={{0,8},{1,9},{2,10},{3,11},{4,12},{5,13},{6,14},{7,15},{8,0},{9,1},... | collective-permute-start | bytes 1548296 | tf_op jit(solution)/shard_map/ppermute | solution.py:73
  133.5 25.4 %collective-permute-start.22 = (bf16[128,1152]{1,0:T(8,128)(2,1)}, bf16[128,1152]{1,0:T(8,128)(2,1)S(1)}, u32[]{:S(2)}, u32[]{:S(2)}) collective-permute-start(bf16[128,1152]{1,0:T(8,128)(2,1)} %copy-done.35), channel_id=1, source_target_pairs={{0,2},{1,3},{2,0},{3,1},{4,6},{5,7},{6,4},{7,5},{8,10},{9,11},{10,... | collective-permute-start | bytes 884744 | tf_op jit(solution)/shard_map/ppermute | solution.py:73
  303.6 23.5 %collective-permute-start.38 = (bf16[512,512]{1,0:T(8,128)(2,1)S(1)}, bf16[512,512]{1,0:T(8,128)(2,1)S(1)}, u32[]{:S(2)}, u32[]{:S(2)}) collective-permute-start(bf16[512,512]{1,0:T(8,128)(2,1)S(1)} %pad_maximum_fusion.2), channel_id=1, source_target_pairs={{0,4},{1,5},{2,6},{3,7},{4,0},{5,1},{6,2},{7,3},{8,12},{9,13},{10,... | collective-permute-start | bytes 1572872 | tf_op jit(solution)/shard_map/ppermute | solution.py:73
  303.8 23.3 %collective-permute-start.39 = (bf16[512,512]{1,0:T(8,128)(2,1)S(1)}, bf16[512,512]{1,0:T(8,128)(2,1)S(1)}, u32[]{:S(2)}, u32[]{:S(2)}) collective-permute-start(bf16[512,512]{1,0:T(8,128)(2,1)S(1)} %pad_maximum_fusion.3), channel_id=1, source_target_pairs={{0,2},{1,3},{2,0},{3,1},{4,6},{5,7},{6,4},{7,5},{8,10},{9,11},{10,... | collective-permute-start | bytes 1572872 | tf_op jit(solution)/shard_map/ppermute | solution.py:73
  308.9 45.5 %collective-permute-start.43 = (bf16[640,1152]{1,0:T(8,128)(2,1)}, bf16[640,1152]{1,0:T(8,128)(2,1)}, u32[]{:S(2)}, u32[]{:S(2)}) collective-permute-start(bf16[640,1152]{1,0:T(8,128)(2,1)} %add_convert_fusion), channel_id=1, source_target_pairs={{0,2},{1,3},{2,0},{3,1},{4,6},{5,7},{6,4},{7,5},{8,10},{9,11},{10,... | collective-permute-start | bytes 4423688 | tf_op jit(solution)/shard_map/ppermute | solution.py:73
  361.3 27.4 %collective-permute-start.44 = (bf16[768,640]{1,0:T(8,128)(2,1)}, bf16[768,640]{1,0:T(8,128)(2,1)S(1)}, u32[]{:S(2)}, u32[]{:S(2)}) collective-permute-start(bf16[768,640]{1,0:T(8,128)(2,1)} %get-tuple-element.330), channel_id=1, source_target_pairs={{0,1},{1,0},{2,3},{3,2},{4,5},{5,4},{6,7},{7,6},{8,9},{9,8},{10,11... | collective-permute-start | bytes 2949128 | tf_op jit(solution)/shard_map/ppermute | solution.py:73
  389.8 32.5 %collective-permute-start.46 = (bf16[384,640]{1,0:T(8,128)(2,1)}, bf16[384,640]{1,0:T(8,128)(2,1)}, u32[]{:S(2)}, u32[]{:S(2)}) collective-permute-start(bf16[384,640]{1,0:T(8,128)(2,1)} %add_convert_fusion.1), channel_id=1, source_target_pairs={{0,2},{1,3},{2,0},{3,1},{4,6},{5,7},{6,4},{7,5},{8,10},{9,11},{10,... | collective-permute-start | bytes 1474568 | tf_op jit(solution)/shard_map/ppermute | solution.py:73
  395.6 25.0 %collective-permute-start.49 = (bf16[80,1152]{1,0:T(8,128)(2,1)S(1)}, bf16[80,1152]{1,0:T(8,128)(2,1)S(1)}, u32[]{:S(2)}, u32[]{:S(2)}) collective-permute-start(bf16[80,1152]{1,0:T(8,128)(2,1)S(1)} %get-tuple-element.452), channel_id=1, source_target_pairs={{0,24},{1,25},{2,26},{3,27},{4,28},{5,29},{6,30},{7,31},{8,16},{9,... | collective-permute-start | bytes 552968 | tf_op jit(solution)/shard_map/ppermute | solution.py:73
  398.4 23.9 %collective-permute-start.47 = (bf16[80,1152]{1,0:T(8,128)(2,1)S(1)}, bf16[80,1152]{1,0:T(8,128)(2,1)S(1)}, u32[]{:S(2)}, u32[]{:S(2)}) collective-permute-start(bf16[80,1152]{1,0:T(8,128)(2,1)S(1)} %get-tuple-element.454), channel_id=1, source_target_pairs={{0,8},{1,9},{2,10},{3,11},{4,12},{5,13},{6,14},{7,15},{8,0},{9,1},... | collective-permute-start | bytes 552968 | tf_op jit(solution)/shard_map/ppermute | solution.py:73
  420.6 40.7 %collective-permute-start.52 = (bf16[2,288,256]{2,1,0:T(8,128)(2,1)}, bf16[2,288,256]{2,1,0:T(8,128)(2,1)S(1)}, u32[]{:S(2)}, u32[]{:S(2)}) collective-permute-start(bf16[2,288,256]{2,1,0:T(8,128)(2,1)} %get-tuple-element.356), channel_id=1, source_target_pairs={{0,3},{1,2},{2,1},{3,0},{4,7},{5,6},{6,5},{7,4},{8,11},{9,10},{10,... | collective-permute-start | bytes 884744 | tf_op jit(solution)/shard_map/ppermute | solution.py:73
  424.1 39.5 %collective-permute-start.55 = (bf16[80,1152]{1,0:T(8,128)(2,1)S(1)}, bf16[80,1152]{1,0:T(8,128)(2,1)}, u32[]{:S(2)}, u32[]{:S(2)}) collective-permute-start(bf16[80,1152]{1,0:T(8,128)(2,1)S(1)} %get-tuple-element.429), channel_id=1, source_target_pairs={{0,16},{1,17},{2,18},{3,19},{4,20},{5,21},{6,22},{7,23},{8,24},{9,... | collective-permute-start | bytes 552968 | tf_op jit(solution)/shard_map/ppermute | solution.py:73
  425.4 38.3 %collective-permute-start.54 = (bf16[80,1152]{1,0:T(8,128)(2,1)S(1)}, bf16[80,1152]{1,0:T(8,128)(2,1)}, u32[]{:S(2)}, u32[]{:S(2)}) collective-permute-start(bf16[80,1152]{1,0:T(8,128)(2,1)S(1)} %get-tuple-element.429), channel_id=1, source_target_pairs={{0,8},{1,9},{2,10},{3,11},{4,12},{5,13},{6,14},{7,15},{8,0},{9,1},... | collective-permute-start | bytes 552968 | tf_op jit(solution)/shard_map/ppermute | solution.py:73
  428.5 36.7 %collective-permute-start.56 = (bf16[80,1152]{1,0:T(8,128)(2,1)S(1)}, bf16[80,1152]{1,0:T(8,128)(2,1)}, u32[]{:S(2)}, u32[]{:S(2)}) collective-permute-start(bf16[80,1152]{1,0:T(8,128)(2,1)S(1)} %get-tuple-element.429), channel_id=1, source_target_pairs={{0,24},{1,25},{2,26},{3,27},{4,28},{5,29},{6,30},{7,31},{8,16},{9,... | collective-permute-start | bytes 552968 | tf_op jit(solution)/shard_map/ppermute | solution.py:73
  429.5 35.8 %collective-permute-start.53 = (bf16[192,640]{1,0:T(8,128)(2,1)S(1)}, bf16[192,640]{1,0:T(8,128)(2,1)S(1)}, u32[]{:S(2)}, u32[]{:S(2)}) collective-permute-start(bf16[192,640]{1,0:T(8,128)(2,1)S(1)} %dynamic-slice_convert_fusion.1), channel_id=1, source_target_pairs={{0,4},{1,5},{2,6},{3,7},{4,0},{5,1},{6,2},{7,3},{8,12},{9,13},{10,... | collective-permute-start | bytes 737288 | tf_op jit(solution)/shard_map/ppermute | solution.py:73
  462.1 45.9 %collective-permute-start.57 = (bf16[2,288,512]{2,1,0:T(8,128)(2,1)}, bf16[2,288,512]{2,1,0:T(8,128)(2,1)S(1)}, u32[]{:S(2)}, u32[]{:S(2)}) collective-permute-start(bf16[2,288,512]{2,1,0:T(8,128)(2,1)} %get-tuple-element.373), channel_id=1, source_target_pairs={{0,1},{1,0},{2,3},{3,2},{4,5},{5,4},{6,7},{7,6},{8,9},{9,8},{10,11... | collective-permute-start | bytes 1769480 | tf_op jit(solution)/shard_map/ppermute | solution.py:73
  463.6 44.5 %collective-permute-start.58 = (bf16[2,288,512]{2,1,0:T(8,128)(2,1)}, bf16[2,288,512]{2,1,0:T(8,128)(2,1)S(1)}, u32[]{:S(2)}, u32[]{:S(2)}) collective-permute-start(bf16[2,288,512]{2,1,0:T(8,128)(2,1)} %get-tuple-element.374), channel_id=1, source_target_pairs={{0,2},{1,3},{2,0},{3,1},{4,6},{5,7},{6,4},{7,5},{8,10},{9,11},{10,... | collective-permute-start | bytes 1769480 | tf_op jit(solution)/shard_map/ppermute | solution.py:73
  463.7 46.0 %collective-permute-start.59 = (bf16[2,288,512]{2,1,0:T(8,128)(2,1)}, bf16[2,288,512]{2,1,0:T(8,128)(2,1)S(1)}, u32[]{:S(2)}, u32[]{:S(2)}) collective-permute-start(bf16[2,288,512]{2,1,0:T(8,128)(2,1)} %get-tuple-element.375), channel_id=1, source_target_pairs={{0,3},{1,2},{2,1},{3,0},{4,7},{5,6},{6,5},{7,4},{8,11},{9,10},{10,... | collective-permute-start | bytes 1769480 | tf_op jit(solution)/shard_map/ppermute | solution.py:73
  473.8 32.7 %collective-permute-start.60 = (bf16[48,640]{1,0:T(8,128)(2,1)S(1)}, bf16[48,640]{1,0:T(8,128)(2,1)S(1)}, u32[]{:S(2)}, u32[]{:S(2)}) collective-permute-start(bf16[48,640]{1,0:T(8,128)(2,1)S(1)} %get-tuple-element.462), channel_id=1, source_target_pairs={{0,8},{1,9},{2,10},{3,11},{4,12},{5,13},{6,14},{7,15},{8,0},{9,1},... | collective-permute-start | bytes 184328 | tf_op jit(solution)/shard_map/ppermute | solution.py:73
  474.6 35.1 %collective-permute-start.63 = (bf16[320,1152]{1,0:T(8,128)(2,1)}, bf16[320,1152]{1,0:T(8,128)(2,1)}, u32[]{:S(2)}, u32[]{:S(2)}) collective-permute-start(bf16[320,1152]{1,0:T(8,128)(2,1)} %constant_dynamic-update-slice_fusion.26), channel_id=1, source_target_pairs={{0,4},{1,5},{2,6},{3,7},{4,0},{5,1},{6,2},{7,3},{8,12},{9,13},{10,... | collective-permute-start | bytes 2211848 | tf_op jit(solution)/shard_map/ppermute | solution.py:73
  506.6 40.2 %collective-permute-start.64 = (bf16[2,288,512]{2,1,0:T(8,128)(2,1)}, bf16[2,288,512]{2,1,0:T(8,128)(2,1)S(1)}, u32[]{:S(2)}, u32[]{:S(2)}) collective-permute-start(bf16[2,288,512]{2,1,0:T(8,128)(2,1)} %get-tuple-element.397), channel_id=1, source_target_pairs={{0,1},{1,0},{2,3},{3,2},{4,5},{5,4},{6,7},{7,6},{8,9},{9,8},{10,11... | collective-permute-start | bytes 1769480 | tf_op jit(solution)/shard_map/ppermute | solution.py:73
  508.0 40.5 %collective-permute-start.65 = (bf16[2,288,512]{2,1,0:T(8,128)(2,1)}, bf16[2,288,512]{2,1,0:T(8,128)(2,1)S(1)}, u32[]{:S(2)}, u32[]{:S(2)}) collective-permute-start(bf16[2,288,512]{2,1,0:T(8,128)(2,1)} %get-tuple-element.398), channel_id=1, source_target_pairs={{0,2},{1,3},{2,0},{3,1},{4,6},{5,7},{6,4},{7,5},{8,10},{9,11},{10,... | collective-permute-start | bytes 1769480 | tf_op jit(solution)/shard_map/ppermute | solution.py:73
  508.1 41.3 %collective-permute-start.66 = (bf16[2,288,512]{2,1,0:T(8,128)(2,1)}, bf16[2,288,512]{2,1,0:T(8,128)(2,1)S(1)}, u32[]{:S(2)}, u32[]{:S(2)}) collective-permute-start(bf16[2,288,512]{2,1,0:T(8,128)(2,1)} %get-tuple-element.399), channel_id=1, source_target_pairs={{0,3},{1,2},{2,1},{3,0},{4,7},{5,6},{6,5},{7,4},{8,11},{9,10},{10,... | collective-permute-start | bytes 1769480 | tf_op jit(solution)/shard_map/ppermute | solution.py:73
  510.6 38.9 %collective-permute-start.68 = (bf16[48,640]{1,0:T(8,128)(2,1)S(1)}, bf16[48,640]{1,0:T(8,128)(2,1)S(1)}, u32[]{:S(2)}, u32[]{:S(2)}) collective-permute-start(bf16[48,640]{1,0:T(8,128)(2,1)S(1)} %get-tuple-element.427), channel_id=1, source_target_pairs={{0,16},{1,17},{2,18},{3,19},{4,20},{5,21},{6,22},{7,23},{8,24},{9,... | collective-permute-start | bytes 184328 | tf_op jit(solution)/shard_map/ppermute | solution.py:73
  512.1 39.0 %collective-permute-start.67 = (bf16[48,640]{1,0:T(8,128)(2,1)S(1)}, bf16[48,640]{1,0:T(8,128)(2,1)S(1)}, u32[]{:S(2)}, u32[]{:S(2)}) collective-permute-start(bf16[48,640]{1,0:T(8,128)(2,1)S(1)} %get-tuple-element.427), channel_id=1, source_target_pairs={{0,8},{1,9},{2,10},{3,11},{4,12},{5,13},{6,14},{7,15},{8,0},{9,1},... | collective-permute-start | bytes 184328 | tf_op jit(solution)/shard_map/ppermute | solution.py:73
  549.5 27.6 %collective-permute-start.73 = (bf16[2,288,512]{2,1,0:T(8,128)(2,1)S(1)}, bf16[2,288,512]{2,1,0:T(8,128)(2,1)S(1)}, u32[]{:S(2)}, u32[]{:S(2)}) collective-permute-start(bf16[2,288,512]{2,1,0:T(8,128)(2,1)S(1)} %copy-done.125), channel_id=1, source_target_pairs={{0,3},{1,2},{2,1},{3,0},{4,7},{5,6},{6,5},{7,4},{8,11},{9,10},{10,... | collective-permute-start | bytes 1769480 | tf_op jit(solution)/shard_map/ppermute | solution.py:73
  (173 other events, 1599.0 us)
Sparse Core Ops, SparseCore 0:
  130.3 84.3 all-gather.2
  217.7 87.1 all-gather.4

commit v3 on v2

--- a/solution.py
+++ b/solution.py
@@ -154,18 +154,17 @@
 
 
 def gather_rows(value, me):
-    (other,) = yield [swap(value, 2)]
-    pair = join(value, other)
-    (other,) = yield [swap(pair, 1)]
+    pair, other = yield from gather_group(value)
     return settle(me ^ jnp.array([0, 2, 1, 3], jnp.int32), value.shape[0], pair, other)
 
 
-def exchange_columns(quarters):
+def exchange_columns(quarters, arrived):
     first, second = yield [swap(quarters[0], 2), swap(quarters[1], 3)]
     (first_z,) = yield [swap(first, 8)]
     second_z, second_y = yield [swap(second, 8), swap(second, 4)]
-    first_y, first_far, second_far = yield [swap(first, 4), swap(first_z, 4), swap(second_y, 8)]
-    return [(first, first_y, first_z, first_far), (second, second_y, second_z, second_far)]
+    first_far, second_far = yield [swap(first_z, 4), swap(second_y, 8)]
+    arrived += [first, first_z, first_far, second, second_y, second_z, second_far]
+    return (yield [swap(first, 4)])
 
 
 def kernel_call(kernel, out_shape, *operands, scalars=(), scratch=(), name):
@@ -181,22 +180,36 @@
     )(*scalars, *operands)
 
 
-def gains_kernel(mine, *refs):
-    sources, (wide, narrow) = refs[:4], refs[4:]
-    part, head_part = wide.shape[1] // 4, narrow.shape[1] // 4
+def pack_kernel(w_key, w_value, *refs):
+    gains, out = refs[:-1], refs[-1]
+    rows, width = w_key.shape[0], out.shape[1]
+    out[:rows, : w_key.shape[1]] = w_key[...]
+    out[:rows, w_key.shape[1] :] = w_value[...]
+    lines = [
+        jnp.concatenate([g[...].astype(F32), jnp.zeros((1, width - g.shape[1]), F32)], axis=1)
+        for g in gains
+    ]
+    lines.append(jnp.zeros((out.shape[0] - rows - len(lines), width), F32))
+    out[rows:, :] = jnp.concatenate(lines, axis=0).astype(BF)
+
+
+def unpack_kernel(mine, pair, other, pair_mat, wide, narrow):
+    size, head_part = wide.shape[1] // 4, narrow.shape[1] // 4
+    block = pair.shape[0] // 2
     for m in range(4):
 
         @pl.when(mine[0] == m)
         def _(m=m):
-            owners = [sources[m ^ r][...] for r in range(4)]
+            lines = []
+            for r in range(4):
+                source, first = (pair, other)[(m ^ r) % 2], (m ^ r) // 2 * block
+                pair_mat[r * size : (r + 1) * size, :] = source[first : first + size, :]
+                lines.append(source[first + size : first + block, :].astype(F32))
             for i in range(4):
-                wide[i : i + 1, :] = jnp.concatenate(
-                    [o[:, i * part : (i + 1) * part] for o in owners], axis=1
-                )
+                wide[i : i + 1, :] = jnp.concatenate([l[i : i + 1, :size] for l in lines], axis=1)
             for i in range(2):
-                first = 4 * part + i * head_part
                 narrow[i : i + 1, :] = jnp.concatenate(
-                    [o[:, first : first + head_part] for o in owners], axis=1
+                    [l[4 + i : 5 + i, :head_part] for l in lines], axis=1
                 )
 
 
@@ -490,38 +503,52 @@
     return pl.multiple_of(owner * part - part % 128 * (owner % 2), 128)
 
 
-def carve_kernel(part, place, w, own, core, near, corner):
-    wide, step = own.shape[2], pl.program_id(0)
-    mine, low, high = place[0], place[1], place[2]
+def carve_kernel(part, mine, w, own, core):
     for offset, out in enumerate((own, core)):
-        out[...] = w[:, :, pl.ds(left_of(mine ^ offset, part), wide)]
-
-    @pl.when(step // (pl.num_programs(0) // 2) == low)
-    def _():
-        for offset, out in ((2, near), (3, corner)):
-            out[...] = w[pl.ds(high, 1), :, pl.ds(left_of(mine ^ offset, part), wide)]
-
-
-def carve(w, place, part, wide):
+        out[...] = w[:, :, pl.ds(left_of(mine[0] ^ offset, part), out.shape[2])]
+
+
+def carve(w, mine, part, wide):
     rows, step = w.shape[1], 48
-    half = rows // 2 // step
-
-    def quarter(i, p):
-        return (0, jnp.clip(i - half * p[1], 0, half - 1), 0)
-
     return pl.pallas_call(
         functools.partial(carve_kernel, part),
         grid_spec=pltpu.PrefetchScalarGridSpec(
             num_scalar_prefetch=1,
             grid=(rows // step,),
             in_specs=[pl.BlockSpec((2, step, w.shape[2]), lambda i, p: (0, i, 0))],
-            out_specs=[pl.BlockSpec((2, step, wide), lambda i, p: (0, i, 0))] * 2
-            + [pl.BlockSpec((1, step, wide), quarter)] * 2,
+            out_specs=[pl.BlockSpec((2, step, wide), lambda i, p: (0, i, 0))] * 2,
         ),
-        out_shape=[jax.ShapeDtypeStruct((2, rows, wide), BF)] * 2
-        + [jax.ShapeDtypeStruct((1, rows // 2, wide), BF)] * 2,
+        out_shape=[jax.ShapeDtypeStruct((2, rows, wide), BF)] * 2,
         compiler_params=pltpu.CompilerParams(vmem_limit_bytes=VMEM_LIMIT),
         name="carve",
+    )(mine[None], w)
+
+
+def carve_quarters_kernel(part, place, w, near, corner):
+    mine, side = place[0], place[2]
+    for offset, out in ((2, near), (3, corner)):
+        at = pl.ds(left_of(mine ^ offset, part), out.shape[2])
+        for s in range(2):
+
+            @pl.when(side == s)
+            def _(s=s):
+                out[0] = w[:, s, at]
+
+
+def carve_quarters(w, place, part, wide):
+    rows, step = w.shape[0], 48
+    half = rows // 2 // step
+    return pl.pallas_call(
+        functools.partial(carve_quarters_kernel, part),
+        grid_spec=pltpu.PrefetchScalarGridSpec(
+            num_scalar_prefetch=1,
+            grid=(half,),
+            in_specs=[pl.BlockSpec((step, 2, w.shape[2]), lambda i, p: (i + half * p[1], 0, 0))],
+            out_specs=[pl.BlockSpec((1, step, wide), lambda i, p: (0, i, 0))] * 2,
+        ),
+        out_shape=[jax.ShapeDtypeStruct((1, rows // 2, wide), BF)] * 2,
+        compiler_params=pltpu.CompilerParams(vmem_limit_bytes=VMEM_ALL),
+        name="carve_quarters",
     )(place, w)
 
 
@@ -562,44 +589,49 @@
     )(places, *sources)
 
 
-def lay_kernel(sides, rows, *refs):
-    out, sources = refs[-1], refs[:-1]
-    step = pl.program_id(0)
+def lay_kernel(counts, sides, rows, *refs):
+    out, sources = refs[-1], refs[: len(counts)]
+    step, first = pl.program_id(0), 0
     width = out.shape[3]
-    for i, source in enumerate([sources[0]] * 4 + [sources[1]] * 4 + list(sources[2:])):
-
-        @pl.when(step == i)
+    for source, count in zip(sources, counts):
+
+        @pl.when((step >= first) & (step < first + count))
         def _(source=source):
             for block in range(out.shape[1]):
                 out[0, block] = source[0, :, block * width : (block + 1) * width]
 
-
-def lay(sides, rows, own, core, quarters):
-    half, wide = own.shape[1] // 2, own.shape[2]
-    shape = (1, half, wide)
-
-    def run(first):
+        first += count
+
+
+def lay(places, sources, laid=None):
+    half, wide = sources[-1].shape[1], sources[-1].shape[2]
+    counts = [source.shape[0] * source.shape[1] // half for source in sources]
+
+    def run(first, count):
         def place(i, s, r):
-            j = jnp.clip(i - first, 0, 3)
+            j = jnp.clip(i - first, 0, count - 1)
             return (j // 2, j % 2, 0)
 
-        return pl.BlockSpec(shape, place)
-
-    still = pl.BlockSpec(shape, lambda i, s, r: (0, 0, 0))
+        return pl.BlockSpec((1, half, wide), place)
+
+    base = [] if laid is None else [laid]
+    sides, rows = [jnp.stack([jnp.asarray(p[i], jnp.int32) for p in places]) for i in (0, 1)]
     return pl.pallas_call(
-        lay_kernel,
+        functools.partial(lay_kernel, counts),
         grid_spec=pltpu.PrefetchScalarGridSpec(
             num_scalar_prefetch=2,
-            grid=(16,),
-            in_specs=[run(0), run(4)] + [still] * 8,
+            grid=(sum(counts),),
+            in_specs=[run(sum(counts[:i]), count) for i, count in enumerate(counts)]
+            + [pl.BlockSpec(memory_space=pl.ANY)] * len(base),
             out_specs=pl.BlockSpec(
                 (1, wide // 256, half, 256), lambda i, s, r: (s[i], 0, r[i], 0)
             ),
         ),
         out_shape=jax.ShapeDtypeStruct((2, wide // 256, 8 * half, 256), BF),
-        compiler_params=pltpu.CompilerParams(vmem_limit_bytes=VMEM_LIMIT),
+        input_output_aliases={2 + len(sources): 0} if base else {},
+        compiler_params=pltpu.CompilerParams(vmem_limit_bytes=VMEM_ALL),
         name="lay",
-    )(sides, rows, own, core, *quarters)
+    )(sides, rows, *sources, *base)
 
 
 def contract(left, right, left_dim, right_dim):
@@ -610,73 +642,36 @@
 
 def gelu_and_slope(x):
     scale = math.sqrt(2.0 / math.pi)
-    square = x * x
-    turn = jnp.tanh(x * (scale + (scale * 0.044715) * square))
-    share = 0.5 + 0.5 * turn
-    slope = share + (0.5 * x) * (1.0 - turn * turn) * (scale + (3 * scale * 0.044715) * square)
-    return x * share, slope
-
-
-def ffn_factors_kernel(second, w_gate, w_up, act, value, factor):
+    cubic = (scale * 0.044715) * (x * x * x)
+    inner = scale * x + cubic
+    share = 0.5 + 0.5 * jnp.tanh(inner)
+    return x * share, share + share * (1.0 - share) * (2.0 * inner + 4.0 * cubic)
+
+
+def ffn_gradients_kernel(part, first, blocks, mine, second, d_ffn, w_gate, w_up, w_down, *rest):
+    outs, down_rows, act, d_both, both_sum, down_sum, sem = rest[-10:-6], *rest[-6:]
+    step = pl.program_id(1)
     rows, slab = second.shape[0], 256
+    width = act.shape[1]
 
     def products(r):
         at = pl.ds(r * slab, slab)
-        return contract(second[at, :], w_gate[0, 0], 1, 0), contract(second[at, :], w_up[0, 0], 1, 0)
+        return (
+            contract(second[at, :], w_gate[0, 0], 1, 0),
+            contract(second[at, :], w_up[0, 0], 1, 0),
+            contract(d_ffn[at, :], w_down[...], 1, 1),
+        )
 
     ahead = products(0)
     for r in range(rows // slab):
         at = pl.ds(r * slab, slab)
-        gate, upper = ahead
+        gate, upper, d_act = ahead
         if r + 1 < rows // slab:
             ahead = products(r + 1)
-        gelu, slope = gelu_and_slope(gate)
-        act[at, :] = (gelu * upper).astype(BF)
-        value[at, :] = gelu.astype(BF)
-        factor[at, :] = (upper * slope).astype(BF)
-
-
-def ffn_factors(second_all, in_mat, first, last):
-    tokens, model = second_all.shape
-    slab, width = min(2048, tokens), 256
-    columns = (last - first) * width
-    return pl.pallas_call(
-        ffn_factors_kernel,
-        grid=(last - first, tokens // slab),
-        in_specs=[
-            pl.BlockSpec((slab, model), lambda j, t: (t, 0)),
-            pl.BlockSpec((1, 1, model, width), lambda j, t: (0, j + first, 0, 0)),
-            pl.BlockSpec((1, 1, model, width), lambda j, t: (1, j + first, 0, 0)),
-        ],
-        out_specs=[pl.BlockSpec((slab, width), lambda j, t: (t, j))] * 3,
-        out_shape=[jax.ShapeDtypeStruct((tokens, columns), BF)] * 3,
-        compiler_params=pltpu.CompilerParams(vmem_limit_bytes=VMEM_ALL),
-        cost_estimate=pl.CostEstimate(
-            flops=4 * tokens * model * columns,
-            bytes_accessed=2 * tokens * model * (last - first) + 6 * tokens * columns,
-            transcendentals=tokens * columns,
-        ),
-        name="ffn_factors",
-    )(second_all, in_mat, in_mat)
-
-
-def ffn_gradients_kernel(part, first, blocks, mine, second, d_ffn, act, value, factor, w_down, *rest):
-    outs, down_rows, d_both, both_sum, down_sum, sem = rest[-9:-5], *rest[-5:]
-    step = pl.program_id(1)
-    rows, slab = second.shape[0], 256
-    width = act.shape[1]
-
-    def products(r):
-        return contract(d_ffn[pl.ds(r * slab, slab), :], w_down[...], 1, 1)
-
-    ahead = products(0)
-    for r in range(rows // slab):
-        at = pl.ds(r * slab, slab)
-        d_act = ahead
-        if r + 1 < rows // slab:
-            ahead = products(r + 1)
-        d_both[at, :width] = (d_act * factor[at, :].astype(F32)).astype(BF)
-        d_both[at, width:] = (d_act * value[at, :].astype(F32)).astype(BF)
+        value, slope = gelu_and_slope(gate)
+        act[at, :] = (value * upper).astype(BF)
+        d_both[at, :width] = (d_act * upper * slope).astype(BF)
+        d_both[at, width:] = (d_act * value).astype(BF)
     grad_both = contract(second[...], d_both[...], 0, 0)
     grad_down = contract(act[...], d_ffn[...], 0, 0)
 
@@ -724,12 +719,11 @@
             out[1] = both_sum[at, width:].astype(BF)
 
 
-def ffn_gradients(mine, second_all, d_ffn_all, factors, down_mat, part, first, last, down_rows):
+def ffn_gradients(mine, second_all, d_ffn_all, in_mat, down_mat, part, first, last, down_rows):
     tokens, model = second_all.shape
     slab, width = min(2048, tokens), 256
     columns = (last - first) * width
     tall = pl.BlockSpec((slab, model), lambda j, t, m: (t, 0))
-    tile = pl.BlockSpec((slab, width), lambda j, t, m: (t, j))
     anywhere = pl.BlockSpec(memory_space=pl.ANY)
     earlier = [] if down_rows is None else [down_rows]
     return pl.pallas_call(
@@ -740,15 +734,15 @@
             in_specs=[
                 tall,
                 tall,
-                tile,
-                tile,
-                tile,
+                pl.BlockSpec((1, 1, model, width), lambda j, t, m: (0, j + first, 0, 0)),
+                pl.BlockSpec((1, 1, model, width), lambda j, t, m: (1, j + first, 0, 0)),
                 pl.BlockSpec((width, model), lambda j, t, m: (j + first, 0)),
             ]
             + [anywhere] * len(earlier),
             out_specs=[pl.BlockSpec((2, model // 4, width), lambda j, t, m: (0, 0, j))] * 4
             + [anywhere],
             scratch_shapes=[
+                pltpu.VMEM((slab, width), BF),
                 pltpu.VMEM((slab, 2 * width), BF),
                 pltpu.VMEM((model, 2 * width), F32),
                 pltpu.VMEM((width, model), F32),
@@ -757,15 +751,15 @@
         ),
         out_shape=[jax.ShapeDtypeStruct((2, model // 4, columns), BF)] * 4
         + [jax.ShapeDtypeStruct((part, model), F32)],
-        input_output_aliases={7: 4} if earlier else {},
+        input_output_aliases={6: 4} if earlier else {},
         compiler_params=pltpu.CompilerParams(vmem_limit_bytes=VMEM_ALL),
         cost_estimate=pl.CostEstimate(
-            flops=8 * tokens * model * columns,
-            bytes_accessed=4 * tokens * model * (last - first) + 6 * tokens * columns,
-            transcendentals=0,
+            flops=12 * tokens * model * columns,
+            bytes_accessed=4 * tokens * model * (last - first),
+            transcendentals=tokens * columns,
         ),
         name="ffn_gradients",
-    )(mine[None], second_all, d_ffn_all, *factors, down_mat, *earlier)
+    )(mine[None], second_all, d_ffn_all, in_mat, in_mat, down_mat, *earlier)
 
 
 def ffn_forward_kernel(near, far, w_gate, w_up, w_down, gate, up, keep, send, act, total):
@@ -923,9 +917,15 @@
 
     gains = (gain_attn_in, gain_attn_out, gain_ffn_in, gain_ffn_out, gain_query, gain_key)
     sizes = [g.shape[0] for g in gains]
-    pair_flow = Flow(gather_rows(jnp.concatenate([w_key, w_value], axis=1), mine))
-    packed = jnp.concatenate(gains).astype(F32)[None]
-    gains_flow = Flow(iter_once([swap(packed, o) for o in (1, 2, 3)]))
+    (packed,) = kernel_call(
+        pack_kernel,
+        [((w_key.shape[0] + 16, 2 * HD), BF)],
+        w_key,
+        w_value,
+        *[g[None] for g in gains],
+        name="pack",
+    )
+    packed_flow = Flow(gather_group(packed))
 
     wide = -(-part // 256) * 256
     quarter = model // 4
@@ -941,25 +941,18 @@
     q_place, q_start = jnp.tile(place, H)[None], jnp.tile(start, H)[None]
 
     low_bit, high_bit = lax.axis_index("ctx") % 2, lax.axis_index("ctx") // 2 % 2
-    own, to_core, to_x, to_corner = carve(
-        jnp.swapaxes(w_in, 0, 1), jnp.stack([mine, low_bit, high_bit]), part, wide
-    )
-    own, to_core, to_x, to_corner = pace((own, to_core, to_x, to_corner), pair_flow)
-    columns_flow = Flow(exchange_columns((to_x, to_corner)))
-
-    cosine, sine, q_place, q_start, w_query = pace(
-        (cosine, sine, q_place, q_start, w_query), gains_flow, pair_flow
-    )
-    query_flow = Flow(gather_rows(w_query, mine))
-    model_gains, head_gains = kernel_call(
-        gains_kernel,
-        [((8, model), F32), ((8, HD), F32)],
-        packed,
-        *gains_flow.result,
+    quarters = carve_quarters(w_in, jnp.stack([mine, low_bit, high_bit]), part, wide)
+    quarters = pace(quarters, packed_flow)
+    arrived = []
+    columns_flow = Flow(exchange_columns(quarters, arrived))
+    cosine, sine, q_place, q_start = pace((cosine, sine, q_place, q_start), packed_flow)
+    pair_mat, model_gains, head_gains = kernel_call(
+        unpack_kernel,
+        [((model, 2 * HD), BF), ((8, model), F32), ((8, HD), F32)],
+        *packed_flow.result,
         scalars=(mine[None],),
-        name="gains",
-    )
-    pair_mat = pair_flow.result
+        name="unpack",
+    )
     first_low, key_raw, pair_rows = kernel_call(
         key_kernel,
         [((rows, model), BF), ((rows, HD), F32), ((rows, 2 * HD), BF)],
@@ -972,12 +965,14 @@
         name="keys",
     )
     pairs_flow = Flow(gather_wide(pair_rows))
-    pace((), pairs_flow, columns_flow)
-    to_core, w_out, w_down = pace(
-        (to_core, w_out, w_down), pairs_flow, query_flow, columns_flow
-    )
+    own, to_core = carve(jnp.swapaxes(w_in, 0, 1), mine, part, wide)
+    own, to_core, w_query = pace((own, to_core, w_query), pairs_flow, columns_flow)
+    core_flow = Flow(iter_once([swap(to_core, 1)]))
+    query_flow = Flow(gather_rows(w_query, mine))
+    w_out, w_down = pace((w_out, w_down), pairs_flow, columns_flow, core_flow)
+    w_out, w_down = pace((w_out, w_down), pairs_flow, columns_flow, query_flow)
     out_flow = Flow(gather_rows(w_out, mine))
-    from_core = swap(to_core, 1)
+    pairs = finish(pairs_flow)
     query_mat = finish(query_flow)
     query_raw, queries = kernel_call(
         query_kernel,
@@ -992,10 +987,8 @@
     down_mat = lax.dynamic_update_slice_in_dim(
         jnp.zeros((wide, model), BF), w_down, part % 128 * (mine % 2), 0
     )
-    queries, down_mat = pace((queries, down_mat), pairs_flow, columns_flow)
-    pairs = finish(pairs_flow)
     *probs, weighted, mass = attend(blocks, queries, q_place, q_start, *pairs)
-    weighted, mass = pace((weighted, mass), out_flow)
+    weighted, mass = pace((weighted, mass), out_flow, columns_flow)
     out_mat = finish(out_flow)
     heads, heads_low, attn_raw, hidden, second_low = kernel_call(
         after_attend_kernel,
@@ -1016,22 +1009,18 @@
 
     group_flow = Flow(gather_group(second_low))
     second_all = lax.all_gather(second_low, AXES, axis=0, tiled=True)
-    sides, halves = [], []
-    for offset in (0, 1):
-        sides += [0, 0, 1, 1]
-        halves += [(mine ^ offset) * 2 + bit for bit in (0, 1, 0, 1)]
+    places = [
+        (side, (mine ^ offset) * 2 + bit) for offset in (0, 1) for side in (0, 1) for bit in (0, 1)
+    ]
     for offset in (2, 3):
-        sides += [high_bit, high_bit, 1 - high_bit, 1 - high_bit]
-        halves += [(mine ^ offset) * 2 + bit for bit in (low_bit, 1 - low_bit) * 2]
-    pace((), group_flow, columns_flow)
-    from_x, from_corner = finish(columns_flow)
-    in_mat = lay(
-        jnp.stack([jnp.asarray(s, jnp.int32) for s in sides]),
-        jnp.stack(halves),
-        own,
-        from_core,
-        (*from_x, *from_corner),
-    )
+        places += [
+            (side, (mine ^ offset) * 2 + bit)
+            for side in (high_bit, 1 - high_bit)
+            for bit in (low_bit, 1 - low_bit)
+        ]
+    laid = lay(places[:9] + places[10:], (own, *core_flow.result, *arrived))
+    (laid,) = pace((laid,), group_flow, columns_flow)
+    in_mat = lay(places[9:10], columns_flow.result, laid)
     gate, upper, keep, send = ffn_group(ffn_forward_kernel, *finish(group_flow), in_mat, down_mat)
     block_out, d_ffn_low, d_gain_ffn_out = kernel_call(
         after_ffn_kernel,
@@ -1069,8 +1058,7 @@
 
     d_queries, *d_pairs = attend_back(queries, d_heads, mass, dots, probs, pairs)
     sums_flow = Flow(scatter_wide(*d_pairs))
-    early_rows = -(-(quarter + H * HD // 4) // 128) * 128
-    tail_rows = -(-quarter // 128) * 128
+    early_rows = quarter + H * HD // 4
     keep, send, d_first_query, d_gain_query = kernel_call(
         query_back_kernel,
         [
@@ -1092,29 +1080,17 @@
         scratch=[((model, H * HD), F32), ((H * HD, model), F32), ((rows, H * HD), BF)],
         name="query_back",
     )
-    blocks_of_columns = wide // 256
-    cuts = [0] + [blocks_of_columns - 2 * i for i in (3, 2, 1, 0)]
-    factors = []
-
-    def factors_step(index, values, *flows):
-        values, second = values
-        factors.append(ffn_factors(second, in_mat, cuts[index], cuts[index + 1]))
-        (values, second), factors[-1] = pace(((values, second), factors[-1]), *flows)
-        return values, second
-
-    keep, send, d_first_query, second_all = pace(
-        (keep, send, d_first_query, second_all), sums_flow
-    )
+    keep, send, d_first_query = pace((keep, send, d_first_query), sums_flow)
+    pace((), sums_flow)
+    pace((), sums_flow)
     early_flow = Flow(scatter_group(keep, send))
-    d_first_query, second_all = factors_step(0, (d_first_query, second_all), sums_flow, early_flow)
-    d_first_query, second_all = factors_step(1, (d_first_query, second_all), sums_flow)
-    d_first_query, second_all = factors_step(2, (d_first_query, second_all), sums_flow, early_flow)
+    pace((), sums_flow, early_flow)
     grad_tokens, keep, send = kernel_call(
         key_back_kernel,
         [
             ((rows, model), F32),
-            ((2 * tail_rows, 2 * HD + 128), F32),
-            ((2 * tail_rows, 2 * HD + 128), BF),
+            ((2 * quarter, 2 * HD + 128), F32),
+            ((2 * quarter, 2 * HD + 128), BF),
         ],
         *sums_flow.result,
         key_raw,
@@ -1137,33 +1113,39 @@
     )
     tail_flow = Flow(scatter_group(keep, send))
 
-    def total(flow):
-        near, far = flow.result
-        return near + far.astype(F32)
-
-    early_flow = Flow(sum_over_ctx(total(early_flow)))
-    grad_tokens, second_all = factors_step(3, (grad_tokens, second_all), tail_flow, early_flow)
-    both = pace((second_all, d_ffn_all))
+    count = wide // 256
+    unit = count // 7
+    cuts = [0, 2 * unit, 4 * unit, 5 * unit, 6 * unit, count]
     ranges, grad_down = [], None
+    both = (second_all, d_ffn_all)
 
     def columns_step(*flows):
         nonlocal both, grad_down
         i = len(ranges)
         *pieces, grad_down = ffn_gradients(
-            mine, *both, factors[i], down_mat, part, cuts[i], cuts[i + 1], grad_down
+            mine, *both, in_mat, down_mat, part, cuts[i], cuts[i + 1], grad_down
         )
-        both, grad_down, ranges[:] = pace((both, grad_down, list(ranges)), *flows)
+        over_x = [sent[2:] for sent in ranges]
+        both, grad_down, over_x = pace((both, grad_down, over_x), *flows)
+        for sent, arrays in zip(ranges, over_x):
+            sent[2:] = arrays
         ranges.append([pieces[0]] + [swap(pieces[o], o) for o in (1, 2, 3)])
 
+    def total(flow):
+        near, far = flow.result
+        return near + far.astype(F32)
+
+    pace((), tail_flow)
     columns_step(tail_flow, early_flow)
-    tail_flow = Flow(sum_over_ctx(total(tail_flow)))
-    columns_step(tail_flow, early_flow)
-    columns_step(tail_flow, early_flow)
-    columns_step(tail_flow)
-    finish(tail_flow)
-    early, tail = early_flow.result, tail_flow.result
+    early, tail = total(early_flow), total(tail_flow)
+    tail = jnp.pad(tail, ((0, 0), (0, model - tail.shape[1])))
+    spare = -(early.shape[0] + tail.shape[0]) % 128
+    rest_flow = Flow(sum_over_ctx(join(early, tail, jnp.zeros((spare, model), F32))))
+    for _ in range(4):
+        columns_step(rest_flow)
+    early, tail = rest_flow.result[:early_rows], rest_flow.result[early_rows:]
     grad_query = early[:quarter, : H * HD]
-    grad_out = early[quarter : quarter + w_out.shape[0]]
+    grad_out = early[quarter:]
     grad_key, grad_value = tail[:quarter, :HD], tail[:quarter, HD : 2 * HD]
     gain_grads = [tail[:size, 2 * HD + i] for i, size in enumerate(sizes)]
     grad_in = unfold(mine, part, ranges)

time: 605 us -> 551 us (0.911)
  local copies, waits for them, and re-layouts: 91.5 us -> 52.5 us
  Pallas kernels: 259 us -> 248 us
  other arithmetic: 34.5 us -> 27.9 us
    pallas_call x5 -> x3, Pallas kernels: 72.5 us -> 19.4 us  [the longest x2 13.5 us: lay(): pl.pallas_call(functools.partial(lay_kernel, counts), grid_spec=pltpu.Pre...]
    pallas_call x4 -> x5, Pallas kernels: 113 us -> 157 us  [ffn_gradients(): pl.pallas_call(functools.partial(ffn_gradients_kernel, part, first, down_...]
    unnamed x271 -> x142, local copies, waits for them, and re-layouts: 71.1 us -> 31.8 us
    ppermute x74 -> x66, waiting for transfers between devices: 126 us -> 119 us  [swap(): return lax.ppermute(value, AXES, [(i, i ^ offset) for i in range(count)])]
    ppermute x74 -> x66, starting transfers between devices: 69.4 us -> 72.5 us  [swap(): return lax.ppermute(value, AXES, [(i, i ^ offset) for i in range(count)])]
  transfers between devices with their start and end apart: 76 -> 68, of which waited for: 25 -> 25; matrix products, arithmetic and copies ran while one was open for 10% -> 9% of each run, Pallas kernels for 41% -> 43%
where the time goes in v3:
time: 551 us; the launch traced here: 541 us
  Pallas kernels  248 us (45%)
  waiting for transfers between devices  125 us (23%)
  starting transfers between devices  72.8 us (13%)
  local copies, waits for them, and re-layouts  52.5 us (10%)
  other arithmetic  27.9 us (5%)
  between operations  15.4 us (3%)
    pallas_call x5, Pallas kernels, ffn_gradients(): pl.pallas_call(functools.partial(ffn_gradients_kernel, part, first, down_...  157 us
    ppermute x66, waiting for transfers between devices, swap(): return lax.ppermute(value, AXES, [(i, i ^ offset) for i in range(count)])  119 us
    ppermute x66, starting transfers between devices, swap(): return lax.ppermute(value, AXES, [(i, i ^ offset) for i in range(count)])  72.5 us
    unnamed x142, local copies, waits for them, and re-layouts  31.8 us
    pallas_call x2, Pallas kernels, ffn_group(): pl.pallas_call(kernel, grid=(wide // width,), in_specs=[rows, rows] + [co...  30 us
    pallas_call x2, Pallas kernels, lay(): pl.pallas_call(functools.partial(lay_kernel, counts), grid_spec=pltpu.Pre...  13.5 us
    pallas_call x1, Pallas kernels, unfold(): pl.pallas_call(functools.partial(unfold_kernel, part), grid_spec=pltpu.Pr...  13.1 us
    pallas_call x9, Pallas kernels, kernel_call(): pl.pallas_call(kernel, out_shape=[jax.ShapeDtypeStruct(shape, dtype) for...  11.1 us
  transfers between devices with their start and end apart: 68, of which 25 were waited for; matrix products, arithmetic and copies ran while one was open for 9% of the time, Pallas kernels for 43%

profile of v3, /device:TPU:1, one launch (start us, length us, event | category | flops | bytes accessed | tf_op | source)
XLA Modules:
  0.0 541.2 jit_solution(3811414681511722395)
XLA Ops:
  17.7 5.9 %carve_quarters.1 = (bf16[1,144,1792]{2,1,0:T(8,128)(2,1)}, bf16[1,144,1792]{2,1,0:T(8,128)(2,1)}) custom-call(s32[3]{0:T(128)} %pad_add_fusion.1.place, bf16[288,2,6912]{2,1,0:T(2,128)(2,1)} %w.1), custom_call_target="tpu_custom_call" | custom-call | tf_op jit(solution)/shard_map/carve_quarters/pallas_call | solution.py:541
  33.7 4.0 copy.45
  40.3 9.9 %collective-permute-done.6.refs_5_ = bf16[1,144,1792]{2,1,0:T(8,128)(2,1)} collective-permute-done((bf16[1,144,1792]{2,1,0:T(8,128)(2,1)}, bf16[1,144,1792]{2,1,0:T(8,128)(2,1)}, u32[]{:S(2)}, u32[]{:S(2)}) %collective-permute-start.6) | collective-permute-done | bytes 516128 | tf_op jit(solution)/shard_map/ppermute | solution.py:73
  58.3 10.3 %collective-permute-done.9.refs_3_ = bf16[1,144,1792]{2,1,0:T(8,128)(2,1)S(1)} collective-permute-done((bf16[1,144,1792]{2,1,0:T(8,128)(2,1)}, bf16[1,144,1792]{2,1,0:T(8,128)(2,1)S(1)}, u32[]{:S(2)}, u32[]{:S(2)}) %collective-permute-start.9) | collective-permute-done | bytes 516128 | tf_op jit(solution)/shard_map/ppermute | solution.py:73
  72.1 8.6 %collective-permute-done.13.refs_7_ = bf16[1,144,1792]{2,1,0:T(8,128)(2,1)S(1)} collective-permute-done((bf16[1,144,1792]{2,1,0:T(8,128)(2,1)}, bf16[1,144,1792]{2,1,0:T(8,128)(2,1)S(1)}, u32[]{:S(2)}, u32[]{:S(2)}) %collective-permute-start.13) | collective-permute-done | bytes 516128 | tf_op jit(solution)/shard_map/ppermute | solution.py:73
  82.1 5.6 %collective-permute-done.11 = bf16[256,512]{1,0:T(8,128)(2,1)S(1)} collective-permute-done((bf16[256,512]{1,0:T(8,128)(2,1)S(1)}, bf16[256,512]{1,0:T(8,128)(2,1)S(1)}, u32[]{:S(2)}, u32[]{:S(2)}) %collective-permute-start.11) | collective-permute-done | bytes 262176 | tf_op jit(solution)/shard_map/ppermute | solution.py:73
  91.2 4.3 collective-permute-done.16.refs_1_
  97.8 7.2 %attend.1 = (bf16[2048,512]{1,0:T(8,128)(2,1)S(1)}, bf16[2048,512]{1,0:T(8,128)(2,1)S(1)}, f32[256,512]{1,0:T(8,128)S(1)}, f32[1,512]{1,0:T(1,128)S(1)}) custom-call(s32[64]{0:T(128)S(1)} %select_reduce_fusion.blocks, bf16[512,256]{1,0:T(8,128)(2,1)S(1)} %get-tuple-element.204.q, s32[1,512]{1,0:T(1,128)S(1)} %bitcast.25, s32[1,512]{1,0:T(1,128)S(1)} %bitcast.24, ...), custom_call_target="tpu_custom_call" | custom-call | flops 2147483648 | bytes 8388608 | tf_op jit(solution)/shard_map/attend/pallas_call | solution.py:285
  119.1 11.7 %lay.2.refs_1_ = bf16[2,7,1152,256]{3,2,1,0:T(8,128)(2,1)} custom-call(s32[15]{0:T(128)} %stack.74.sides, s32[15]{0:T(128)} %stack.83.rows, bf16[2,288,1792]{2,1,0:T(8,128)(2,1)} %copy-done.14, bf16[2,288,1792]{2,1,0:T(8,128)(2,1)} %copy-done.49, bf16[1,144,1792]{2,1,0:T(8,128)(2,1)} %collective-permute-done.5.refs_2_, bf16[1,144,1792]{2,1,0:T(8,128)(2,1)} %copy-done.55, ...), custom_call_target="tpu_custom_call" | custom-call | tf_op jit(solution)/shard_map/lay/pallas_call | solution.py:619
  140.6 14.6 %ffn_forward.1 = (f32[512,1792]{1,0:T(8,128)}, f32[512,1792]{1,0:T(8,128)}, f32[256,1152]{1,0:T(8,128)}, bf16[256,1152]{1,0:T(8,128)(2,1)}) custom-call(bf16[256,1152]{1,0:T(8,128)(2,1)} %constant_dynamic-update-slice_fusion.16.near, bf16[256,1152]{1,0:T(8,128)(2,1)} %collective-permute-done.24.far, bf16[2,7,1152,256]{3,2,1,0:T(8,128)(2,1)} %lay.3.w_gate.w_up, ...), custom_call_target="tpu_custom_call" | custom-call | flops 6341787648 | bytes 19726336 | tf_op jit(solution)/shard_map/ffn_forward/pallas_call | solution.py:820
  160.9 7.2 %collective-permute-done.26.other = bf16[128,1152]{1,0:T(8,128)(2,1)S(1)} collective-permute-done((bf16[128,1152]{1,0:T(8,128)(2,1)S(1)}, bf16[128,1152]{1,0:T(8,128)(2,1)S(1)}, u32[]{:S(2)}, u32[]{:S(2)}) %collective-permute-start.26) | collective-permute-done | bytes 294944 | tf_op jit(solution)/shard_map/ppermute | solution.py:73
  173.0 12.2 %collective-permute-done.27 = bf16[128,1152]{1,0:T(8,128)(2,1)S(1)} collective-permute-done((bf16[128,1152]{1,0:T(8,128)(2,1)}, bf16[128,1152]{1,0:T(8,128)(2,1)S(1)}, u32[]{:S(2)}, u32[]{:S(2)}) %collective-permute-start.27) | collective-permute-done | bytes 294944 | tf_op jit(solution)/shard_map/ppermute | solution.py:73
  185.2 3.2 collective-permute-start.28
  191.0 15.4 %ffn_backward.1 = (f32[256,1152]{1,0:T(8,128)}, bf16[256,1152]{1,0:T(8,128)(2,1)}) custom-call(bf16[256,1152]{1,0:T(8,128)(2,1)} %copy-done.50, bf16[256,1152]{1,0:T(8,128)(2,1)} %copy-done.54, f32[512,1792]{1,0:T(8,128)} %get-tuple-element.232.gate, f32[512,1792]{1,0:T(8,128)} %get-tuple-element.233.up, bf16[2,7,1152,256]{3,2,1,0:T(8,128)(2,1)} %lay.3.w_gate.w_up, ...), custom_call_target="tpu_custom_call" | custom-call | flops 6341787648 | bytes 19726336 | tf_op jit(solution)/shard_map/ffn_backward/pallas_call | solution.py:820
  211.8 7.1 %collective-permute-done.30.other = bf16[128,1152]{1,0:T(8,128)(2,1)S(1)} collective-permute-done((bf16[128,1152]{1,0:T(8,128)(2,1)S(1)}, bf16[128,1152]{1,0:T(8,128)(2,1)S(1)}, u32[]{:S(2)}, u32[]{:S(2)}) %collective-permute-start.30) | collective-permute-done | bytes 294944 | tf_op jit(solution)/shard_map/ppermute | solution.py:73
  226.5 7.1 %attend_back.1 = (f32[256,512]{1,0:T(8,128)S(1)}, bf16[2048,512]{1,0:T(8,128)(2,1)S(1)}, bf16[2048,512]{1,0:T(8,128)(2,1)S(1)}) custom-call(bf16[512,256]{1,0:T(8,128)(2,1)S(1)} %copy-done.33, bf16[512,256]{1,0:T(8,128)(2,1)S(1)} %get-tuple-element.238.d_heads, f32[1,512]{1,0:T(1,128)S(1)} %get-tuple-element.215.mass, f32[1,512]{1,0:T(1,128)S(1)} %get-tuple-element.239.dots, ...), custom_call_target="tpu_custom_call" | custom-call | flops 4294967296 | bytes 12582912 | tf_op jit(solution)/shard_map/attend_back/pallas_call | solution.py:399
  243.7 7.1 %collective-permute-done.32 = bf16[256,512]{1,0:T(8,128)(2,1)S(1)} collective-permute-done((bf16[256,512]{1,0:T(8,128)(2,1)S(1)}, bf16[256,512]{1,0:T(8,128)(2,1)S(1)}, u32[]{:S(2)}, u32[]{:S(2)}) %collective-permute-start.32) | collective-permute-done | bytes 262176 | tf_op jit(solution)/shard_map/ppermute | solution.py:73
  252.7 12.1 %collective-permute-done.35 = bf16[512,512]{1,0:T(8,128)(2,1)S(1)} collective-permute-done((bf16[512,512]{1,0:T(8,128)(2,1)S(1)}, bf16[512,512]{1,0:T(8,128)(2,1)S(1)}, u32[]{:S(2)}, u32[]{:S(2)}) %collective-permute-start.35) | collective-permute-done | bytes 524320 | tf_op jit(solution)/shard_map/ppermute | solution.py:73
  269.0 9.9 %collective-permute-done.36.refs_0_ = bf16[128,512]{1,0:T(8,128)(2,1)S(1)} collective-permute-done((bf16[128,512]{1,0:T(8,128)(2,1)S(1)}, bf16[128,512]{1,0:T(8,128)(2,1)S(1)}, u32[]{:S(2)}, u32[]{:S(2)}) %collective-permute-start.36) | collective-permute-done | bytes 131104 | tf_op jit(solution)/shard_map/ppermute | solution.py:73
  278.9 5.2 collective-permute-done.38.refs_2_
  286.1 6.6 %collective-permute-start.40 = (bf16[576,640]{1,0:T(8,128)(2,1)}, bf16[576,640]{1,0:T(8,128)(2,1)S(1)}, u32[]{:S(2)}, u32[]{:S(2)}) collective-permute-start(bf16[576,640]{1,0:T(8,128)(2,1)} %get-tuple-element.272), channel_id=1, source_target_pairs={{0,1},{1,0},{2,3},{3,2},{4,5},{5,4},{6,7},{7,6},{8,9},{9,8},{10,11... | collective-permute-start | bytes 2211848 | tf_op jit(solution)/shard_map/ppermute | solution.py:73
  292.8 3.4 add_convert_fusion
  298.4 5.4 all-gather.5.cloned.1.call-done.d_ffn
  303.8 42.7 %ffn_gradients.5 = (bf16[2,288,512]{2,1,0:T(8,128)(2,1)}, bf16[2,288,512]{2,1,0:T(8,128)(2,1)}, bf16[2,288,512]{2,1,0:T(8,128)(2,1)}, bf16[2,288,512]{2,1,0:T(8,128)(2,1)}, f32[1728,1152]{1,0:T(8,128)}) custom-call(s32[1]{0:T(128)} %bitcast.2.mine, bf16[4096,1152]{1,0:T(8,128)(2,1)} %all-gather.3.cloned.1.call-done.second, ...), custom_call_target="tpu_custom_call" | custom-call | flops 28991029248 | bytes 37748736 | tf_op jit(solution)/shard_map/ffn_gradients/pallas_call | solution.py:729
  358.4 42.5 %ffn_gradients.6 = (bf16[2,288,512]{2,1,0:T(8,128)(2,1)}, bf16[2,288,512]{2,1,0:T(8,128)(2,1)}, bf16[2,288,512]{2,1,0:T(8,128)(2,1)}, bf16[2,288,512]{2,1,0:T(8,128)(2,1)}, f32[1728,1152]{1,0:T(8,128)}) custom-call(s32[1]{0:T(128)} %bitcast.2.mine, bf16[4096,1152]{1,0:T(8,128)(2,1)} %all-gather.3.cloned.1.call-done.second, ...), custom_call_target="tpu_custom_call", output_to_operand_aliasing={{4}: (6, {})} | custom-call | flops 28991029248 | bytes 37748736 | tf_op jit(solution)/shard_map/ffn_gradients/pallas_call | solution.py:729
  403.5 3.5 fusion.7
  407.8 4.2 collective-permute-start.48
  414.2 23.9 %ffn_gradients.7 = (bf16[2,288,256]{2,1,0:T(8,128)(2,1)}, bf16[2,288,256]{2,1,0:T(8,128)(2,1)}, bf16[2,288,256]{2,1,0:T(8,128)(2,1)}, bf16[2,288,256]{2,1,0:T(8,128)(2,1)}, f32[1728,1152]{1,0:T(8,128)}) custom-call(s32[1]{0:T(128)} %bitcast.2.mine, bf16[4096,1152]{1,0:T(8,128)(2,1)} %all-gather.3.cloned.1.call-done.second, ...), custom_call_target="tpu_custom_call", output_to_operand_aliasing={{4}: (6, {})} | custom-call | flops 14495514624 | bytes 18874368 | tf_op jit(solution)/shard_map/ffn_gradients/pallas_call | solution.py:729
  446.5 23.9 %ffn_gradients.8 = (bf16[2,288,256]{2,1,0:T(8,128)(2,1)}, bf16[2,288,256]{2,1,0:T(8,128)(2,1)}, bf16[2,288,256]{2,1,0:T(8,128)(2,1)}, bf16[2,288,256]{2,1,0:T(8,128)(2,1)}, f32[1728,1152]{1,0:T(8,128)}) custom-call(s32[1]{0:T(128)} %bitcast.2.mine, bf16[4096,1152]{1,0:T(8,128)(2,1)} %all-gather.3.cloned.1.call-done.second, ...), custom_call_target="tpu_custom_call", output_to_operand_aliasing={{4}: (6, {})} | custom-call | flops 14495514624 | bytes 18874368 | tf_op jit(solution)/shard_map/ffn_gradients/pallas_call | solution.py:729
  478.4 24.0 %ffn_gradients.9 = (bf16[2,288,256]{2,1,0:T(8,128)(2,1)}, bf16[2,288,256]{2,1,0:T(8,128)(2,1)}, bf16[2,288,256]{2,1,0:T(8,128)(2,1)}, bf16[2,288,256]{2,1,0:T(8,128)(2,1)}, f32[1728,1152]{1,0:T(8,128)}) custom-call(s32[1]{0:T(128)} %bitcast.2.mine, bf16[4096,1152]{1,0:T(8,128)(2,1)} %all-gather.3.cloned.1.call-done.second, ...), custom_call_target="tpu_custom_call", output_to_operand_aliasing={{4}: (6, {})} | custom-call | flops 14495514624 | bytes 18874368 | tf_op jit(solution)/shard_map/ffn_gradients/pallas_call | solution.py:729
  514.4 6.4 %collective-permute-done.65.refs_19_ = bf16[2,288,256]{2,1,0:T(8,128)(2,1)S(1)} collective-permute-done((bf16[2,288,256]{2,1,0:T(8,128)(2,1)S(1)}, bf16[2,288,256]{2,1,0:T(8,128)(2,1)S(1)}, u32[]{:S(2)}, u32[]{:S(2)}) %collective-permute-start.65) | collective-permute-done | bytes 294944 | tf_op jit(solution)/shard_map/ppermute | solution.py:73
  520.8 13.1 %unfold.1 = f32[288,2,6912]{2,1,0:T(2,128)} custom-call(s32[1]{0:T(128)} %bitcast.2.mine, bf16[2,288,512]{2,1,0:T(8,128)(2,1)S(1)} %copy-done.23, bf16[2,288,512]{2,1,0:T(8,128)(2,1)S(1)} %collective-permute-done.59.refs_1_, bf16[2,288,512]{2,1,0:T(8,128)(2,1)S(1)} %collective-permute-done.43.refs_2_, ...), custom_call_target="tpu_custom_call" | custom-call | tf_op jit(solution)/shard_map/unfold/pallas_call | solution.py:873
  (338 shorter events, 157.8 us)
Async XLA Ops:
  7.2 291.2 %all-gather.3.cloned.1.call-start = ((), (), s32[]{:S(2)}) async-start(), calls=%async_computation | async-start | bytes 9732096 | tf_op jit(solution)/shard_map/all_gather | solution.py:1011
  25.8 24.4 %collective-permute-start.6 = (bf16[1,144,1792]{2,1,0:T(8,128)(2,1)}, bf16[1,144,1792]{2,1,0:T(8,128)(2,1)}, u32[]{:S(2)}, u32[]{:S(2)}) collective-permute-start(bf16[1,144,1792]{2,1,0:T(8,128)(2,1)} %get-tuple-element.191), channel_id=1, source_target_pairs={{0,3},{1,2},{2,1},{3,0},{4,7},{5,6},{6,5},{7,4},{8,11},{9,10},{10,... | collective-permute-start | bytes 1548296 | tf_op jit(solution)/shard_map/ppermute | solution.py:73
  30.0 20.2 %collective-permute-start.2 = (bf16[128,512]{1,0:T(8,128)(2,1)}, bf16[128,512]{1,0:T(8,128)(2,1)}, u32[]{:S(2)}, u32[]{:S(2)}) collective-permute-start(bf16[128,512]{1,0:T(8,128)(2,1)} %get-tuple-element.189), channel_id=1, source_target_pairs={{0,8},{1,9},{2,10},{3,11},{4,12},{5,13},{6,14},{7,15},{8,0},{9,1},... | collective-permute-start | bytes 393224 | tf_op jit(solution)/shard_map/ppermute | solution.py:73
  31.3 18.9 %collective-permute-start.3 = (bf16[128,512]{1,0:T(8,128)(2,1)}, bf16[128,512]{1,0:T(8,128)(2,1)}, u32[]{:S(2)}, u32[]{:S(2)}) collective-permute-start(bf16[128,512]{1,0:T(8,128)(2,1)} %get-tuple-element.189), channel_id=1, source_target_pairs={{0,16},{1,17},{2,18},{3,19},{4,20},{5,21},{6,22},{7,23},{8,24},{9,... | collective-permute-start | bytes 393224 | tf_op jit(solution)/shard_map/ppermute | solution.py:73
  33.6 16.6 %collective-permute-start.4 = (bf16[128,512]{1,0:T(8,128)(2,1)}, bf16[128,512]{1,0:T(8,128)(2,1)}, u32[]{:S(2)}, u32[]{:S(2)}) collective-permute-start(bf16[128,512]{1,0:T(8,128)(2,1)} %get-tuple-element.189), channel_id=1, source_target_pairs={{0,24},{1,25},{2,26},{3,27},{4,28},{5,29},{6,30},{7,31},{8,16},{9,... | collective-permute-start | bytes 393224 | tf_op jit(solution)/shard_map/ppermute | solution.py:73
  50.2 19.9 %collective-permute-start.10 = (bf16[2,288,1792]{2,1,0:T(8,128)(2,1)S(1)}, bf16[2,288,1792]{2,1,0:T(8,128)(2,1)S(1)}, u32[]{:S(2)}, u32[]{:S(2)}) collective-permute-start(bf16[2,288,1792]{2,1,0:T(8,128)(2,1)S(1)} %get-tuple-element.197), channel_id=1, source_target_pairs={{0,1},{1,0},{2,3},{3,2},{4,5},{5,4},{6,7},{7,6},{8,9},{9,8},{10,11... | collective-permute-start | bytes 6193160 | tf_op jit(solution)/shard_map/ppermute | solution.py:73
  57.3 24.8 %collective-permute-start.15 = (bf16[288,1024]{1,0:T(8,128)(2,1)S(1)}, bf16[288,1024]{1,0:T(8,128)(2,1)S(1)}, u32[]{:S(2)}, u32[]{:S(2)}) collective-permute-start(bf16[288,1024]{1,0:T(8,128)(2,1)S(1)} %copy-done.52), channel_id=1, source_target_pairs={{0,2},{1,3},{2,0},{3,1},{4,6},{5,7},{6,4},{7,5},{8,10},{9,11},{10,... | collective-permute-start | bytes 1769480 | tf_op jit(solution)/shard_map/ppermute | solution.py:73
  70.1 17.6 %collective-permute-start.11 = (bf16[256,512]{1,0:T(8,128)(2,1)S(1)}, bf16[256,512]{1,0:T(8,128)(2,1)S(1)}, u32[]{:S(2)}, u32[]{:S(2)}) collective-permute-start(bf16[256,512]{1,0:T(8,128)(2,1)S(1)} %slice.141), channel_id=1, source_target_pairs={{0,2},{1,3},{2,0},{3,1},{4,6},{5,7},{6,4},{7,5},{8,10},{9,11},{10,... | collective-permute-start | bytes 786440 | tf_op jit(solution)/shard_map/ppermute | solution.py:73
  70.6 17.1 %collective-permute-start.12 = (bf16[256,512]{1,0:T(8,128)(2,1)S(1)}, bf16[256,512]{1,0:T(8,128)(2,1)S(1)}, u32[]{:S(2)}, u32[]{:S(2)}) collective-permute-start(bf16[256,512]{1,0:T(8,128)(2,1)S(1)} %slice.142), channel_id=1, source_target_pairs={{0,4},{1,5},{2,6},{3,7},{4,0},{5,1},{6,2},{7,3},{8,12},{9,13},{10,... | collective-permute-start | bytes 786440 | tf_op jit(solution)/shard_map/ppermute | solution.py:73
  90.1 16.4 %collective-permute-start.19 = (bf16[1,144,1792]{2,1,0:T(8,128)(2,1)S(1)}, bf16[1,144,1792]{2,1,0:T(8,128)(2,1)S(1)}, u32[]{:S(2)}, u32[]{:S(2)}) collective-permute-start(bf16[1,144,1792]{2,1,0:T(8,128)(2,1)S(1)} %collective-permute-done.9.refs_3_), channel_id=1, source_target_pairs={{0,4},{1,5},{2,6},{3,7},{4,0},{5,1},{6,2},{7,3},{8,12},{9,13},{10,... | collective-permute-start | bytes 1548296 | tf_op jit(solution)/shard_map/ppermute | solution.py:73
  116.6 187.2 %all-gather.5.cloned.1.call-start = ((), (), s32[]{:S(2)}) async-start(), calls=%async_computation.1 | async-start | bytes 9732096 | tf_op jit(solution)/shard_map/all_gather | solution.py:1035
  239.7 44.4 %collective-permute-start.39 = (bf16[1088,1152]{1,0:T(8,128)(2,1)S(1)}, bf16[1088,1152]{1,0:T(8,128)(2,1)S(1)}, u32[]{:S(2)}, u32[]{:S(2)}) collective-permute-start(bf16[1088,1152]{1,0:T(8,128)(2,1)S(1)} %get-tuple-element.256), channel_id=1, source_target_pairs={{0,1},{1,0},{2,3},{3,2},{4,5},{5,4},{6,7},{7,6},{8,9},{9,8},{10,11... | collective-permute-start | bytes 7520264 | tf_op jit(solution)/shard_map/ppermute | solution.py:73
  296.1 50.4 %collective-permute-start.42 = (bf16[544,1152]{1,0:T(8,128)(2,1)}, bf16[544,1152]{1,0:T(8,128)(2,1)S(1)}, u32[]{:S(2)}, u32[]{:S(2)}) collective-permute-start(bf16[544,1152]{1,0:T(8,128)(2,1)} %add_convert_fusion), channel_id=1, source_target_pairs={{0,2},{1,3},{2,0},{3,1},{4,6},{5,7},{6,4},{7,5},{8,10},{9,11},{10,... | collective-permute-start | bytes 3760136 | tf_op jit(solution)/shard_map/ppermute | solution.py:73
  298.0 48.4 %collective-permute-start.41 = (bf16[288,640]{1,0:T(8,128)(2,1)}, bf16[288,640]{1,0:T(8,128)(2,1)}, u32[]{:S(2)}, u32[]{:S(2)}) collective-permute-start(bf16[288,640]{1,0:T(8,128)(2,1)} %add_convert_fusion.1), channel_id=1, source_target_pairs={{0,2},{1,3},{2,0},{3,1},{4,6},{5,7},{6,4},{7,5},{8,10},{9,11},{10,... | collective-permute-start | bytes 1105928 | tf_op jit(solution)/shard_map/ppermute | solution.py:73
  354.9 47.6 %collective-permute-start.45 = (bf16[448,1152]{1,0:T(8,128)(2,1)}, bf16[448,1152]{1,0:T(8,128)(2,1)S(1)}, u32[]{:S(2)}, u32[]{:S(2)}) collective-permute-start(bf16[448,1152]{1,0:T(8,128)(2,1)} %dynamic-slice_convert_fusion), channel_id=1, source_target_pairs={{0,4},{1,5},{2,6},{3,7},{4,0},{5,1},{6,2},{7,3},{8,12},{9,13},{10,... | collective-permute-start | bytes 3096584 | tf_op jit(solution)/shard_map/ppermute | solution.py:73
  356.1 46.4 %collective-permute-start.43 = (bf16[2,288,512]{2,1,0:T(8,128)(2,1)}, bf16[2,288,512]{2,1,0:T(8,128)(2,1)S(1)}, u32[]{:S(2)}, u32[]{:S(2)}) collective-permute-start(bf16[2,288,512]{2,1,0:T(8,128)(2,1)} %get-tuple-element.279), channel_id=1, source_target_pairs={{0,2},{1,3},{2,0},{3,1},{4,6},{5,7},{6,4},{7,5},{8,10},{9,11},{10,... | collective-permute-start | bytes 1769480 | tf_op jit(solution)/shard_map/ppermute | solution.py:73
  357.3 45.2 %collective-permute-start.44 = (bf16[2,288,512]{2,1,0:T(8,128)(2,1)S(1)}, bf16[2,288,512]{2,1,0:T(8,128)(2,1)S(1)}, u32[]{:S(2)}, u32[]{:S(2)}) collective-permute-start(bf16[2,288,512]{2,1,0:T(8,128)(2,1)S(1)} %copy-done.61), channel_id=1, source_target_pairs={{0,3},{1,2},{2,1},{3,0},{4,7},{5,6},{6,5},{7,4},{8,11},{9,10},{10,... | collective-permute-start | bytes 1769480 | tf_op jit(solution)/shard_map/ppermute | solution.py:73
  400.9 37.1 %collective-permute-start.46 = (bf16[2,288,512]{2,1,0:T(8,128)(2,1)}, bf16[2,288,512]{2,1,0:T(8,128)(2,1)S(1)}, u32[]{:S(2)}, u32[]{:S(2)}) collective-permute-start(bf16[2,288,512]{2,1,0:T(8,128)(2,1)} %get-tuple-element.288), channel_id=1, source_target_pairs={{0,2},{1,3},{2,0},{3,1},{4,6},{5,7},{6,4},{7,5},{8,10},{9,11},{10,... | collective-permute-start | bytes 1769480 | tf_op jit(solution)/shard_map/ppermute | solution.py:73
  402.2 36.6 %collective-permute-start.47 = (bf16[2,288,512]{2,1,0:T(8,128)(2,1)}, bf16[2,288,512]{2,1,0:T(8,128)(2,1)S(1)}, u32[]{:S(2)}, u32[]{:S(2)}) collective-permute-start(bf16[2,288,512]{2,1,0:T(8,128)(2,1)} %get-tuple-element.289), channel_id=1, source_target_pairs={{0,3},{1,2},{2,1},{3,0},{4,7},{5,6},{6,5},{7,4},{8,11},{9,10},{10,... | collective-permute-start | bytes 1769480 | tf_op jit(solution)/shard_map/ppermute | solution.py:73
  407.8 32.8 %collective-permute-start.48 = (bf16[112,1152]{1,0:T(8,128)(2,1)}, bf16[112,1152]{1,0:T(8,128)(2,1)}, u32[]{:S(2)}, u32[]{:S(2)}) collective-permute-start(bf16[112,1152]{1,0:T(8,128)(2,1)} %get-tuple-element.370), channel_id=1, source_target_pairs={{0,8},{1,9},{2,10},{3,11},{4,12},{5,13},{6,14},{7,15},{8,0},{9,1},... | collective-permute-start | bytes 774152 | tf_op jit(solution)/shard_map/ppermute | solution.py:73
  412.1 28.6 %collective-permute-start.49 = (bf16[112,1152]{1,0:T(8,128)(2,1)}, bf16[112,1152]{1,0:T(8,128)(2,1)}, u32[]{:S(2)}, u32[]{:S(2)}) collective-permute-start(bf16[112,1152]{1,0:T(8,128)(2,1)} %get-tuple-element.369), channel_id=1, source_target_pairs={{0,16},{1,17},{2,18},{3,19},{4,20},{5,21},{6,22},{7,23},{8,24},{9,... | collective-permute-start | bytes 774152 | tf_op jit(solution)/shard_map/ppermute | solution.py:73
  412.3 28.4 %collective-permute-start.50 = (bf16[112,1152]{1,0:T(8,128)(2,1)}, bf16[112,1152]{1,0:T(8,128)(2,1)}, u32[]{:S(2)}, u32[]{:S(2)}) collective-permute-start(bf16[112,1152]{1,0:T(8,128)(2,1)} %get-tuple-element.368), channel_id=1, source_target_pairs={{0,24},{1,25},{2,26},{3,27},{4,28},{5,29},{6,30},{7,31},{8,16},{9,... | collective-permute-start | bytes 774152 | tf_op jit(solution)/shard_map/ppermute | solution.py:73
  438.1 32.4 %collective-permute-start.51 = (bf16[2,288,256]{2,1,0:T(8,128)(2,1)}, bf16[2,288,256]{2,1,0:T(8,128)(2,1)S(1)}, u32[]{:S(2)}, u32[]{:S(2)}) collective-permute-start(bf16[2,288,256]{2,1,0:T(8,128)(2,1)} %get-tuple-element.301), channel_id=1, source_target_pairs={{0,2},{1,3},{2,0},{3,1},{4,6},{5,7},{6,4},{7,5},{8,10},{9,11},{10,... | collective-permute-start | bytes 884744 | tf_op jit(solution)/shard_map/ppermute | solution.py:73
  438.7 32.5 %collective-permute-start.52 = (bf16[2,288,256]{2,1,0:T(8,128)(2,1)}, bf16[2,288,256]{2,1,0:T(8,128)(2,1)S(1)}, u32[]{:S(2)}, u32[]{:S(2)}) collective-permute-start(bf16[2,288,256]{2,1,0:T(8,128)(2,1)} %get-tuple-element.302), channel_id=1, source_target_pairs={{0,3},{1,2},{2,1},{3,0},{4,7},{5,6},{6,5},{7,4},{8,11},{9,10},{10,... | collective-permute-start | bytes 884744 | tf_op jit(solution)/shard_map/ppermute | solution.py:73
  442.9 28.4 %collective-permute-start.53 = (bf16[112,1152]{1,0:T(8,128)(2,1)}, bf16[112,1152]{1,0:T(8,128)(2,1)}, u32[]{:S(2)}, u32[]{:S(2)}) collective-permute-start(bf16[112,1152]{1,0:T(8,128)(2,1)} %get-tuple-element.347), channel_id=1, source_target_pairs={{0,8},{1,9},{2,10},{3,11},{4,12},{5,13},{6,14},{7,15},{8,0},{9,1},... | collective-permute-start | bytes 774152 | tf_op jit(solution)/shard_map/ppermute | solution.py:73
  443.8 28.5 %collective-permute-start.54 = (bf16[112,1152]{1,0:T(8,128)(2,1)}, bf16[112,1152]{1,0:T(8,128)(2,1)}, u32[]{:S(2)}, u32[]{:S(2)}) collective-permute-start(bf16[112,1152]{1,0:T(8,128)(2,1)} %get-tuple-element.347), channel_id=1, source_target_pairs={{0,16},{1,17},{2,18},{3,19},{4,20},{5,21},{6,22},{7,23},{8,24},{9,... | collective-permute-start | bytes 774152 | tf_op jit(solution)/shard_map/ppermute | solution.py:73
  444.5 28.9 %collective-permute-start.55 = (bf16[112,1152]{1,0:T(8,128)(2,1)}, bf16[112,1152]{1,0:T(8,128)(2,1)}, u32[]{:S(2)}, u32[]{:S(2)}) collective-permute-start(bf16[112,1152]{1,0:T(8,128)(2,1)} %get-tuple-element.347), channel_id=1, source_target_pairs={{0,24},{1,25},{2,26},{3,27},{4,28},{5,29},{6,30},{7,31},{8,16},{9,... | collective-permute-start | bytes 774152 | tf_op jit(solution)/shard_map/ppermute | solution.py:73
  470.4 35.2 %collective-permute-start.60 = (bf16[2,288,512]{2,1,0:T(8,128)(2,1)}, bf16[2,288,512]{2,1,0:T(8,128)(2,1)S(1)}, u32[]{:S(2)}, u32[]{:S(2)}) collective-permute-start(bf16[2,288,512]{2,1,0:T(8,128)(2,1)} %get-tuple-element.324), channel_id=1, source_target_pairs={{0,1},{1,0},{2,3},{3,2},{4,5},{5,4},{6,7},{7,6},{8,9},{9,8},{10,11... | collective-permute-start | bytes 1769480 | tf_op jit(solution)/shard_map/ppermute | solution.py:73
  471.3 35.1 %collective-permute-start.59 = (bf16[2,288,512]{2,1,0:T(8,128)(2,1)}, bf16[2,288,512]{2,1,0:T(8,128)(2,1)S(1)}, u32[]{:S(2)}, u32[]{:S(2)}) collective-permute-start(bf16[2,288,512]{2,1,0:T(8,128)(2,1)} %get-tuple-element.320), channel_id=1, source_target_pairs={{0,1},{1,0},{2,3},{3,2},{4,5},{5,4},{6,7},{7,6},{8,9},{9,8},{10,11... | collective-permute-start | bytes 1769480 | tf_op jit(solution)/shard_map/ppermute | solution.py:73
  471.3 31.1 %collective-permute-start.56 = (bf16[2,288,256]{2,1,0:T(8,128)(2,1)}, bf16[2,288,256]{2,1,0:T(8,128)(2,1)}, u32[]{:S(2)}, u32[]{:S(2)}) collective-permute-start(bf16[2,288,256]{2,1,0:T(8,128)(2,1)} %get-tuple-element.316), channel_id=1, source_target_pairs={{0,2},{1,3},{2,0},{3,1},{4,6},{5,7},{6,4},{7,5},{8,10},{9,11},{10,... | collective-permute-start | bytes 884744 | tf_op jit(solution)/shard_map/ppermute | solution.py:73
  472.3 30.2 %collective-permute-start.57 = (bf16[2,288,256]{2,1,0:T(8,128)(2,1)}, bf16[2,288,256]{2,1,0:T(8,128)(2,1)}, u32[]{:S(2)}, u32[]{:S(2)}) collective-permute-start(bf16[2,288,256]{2,1,0:T(8,128)(2,1)} %get-tuple-element.317), channel_id=1, source_target_pairs={{0,3},{1,2},{2,1},{3,0},{4,7},{5,6},{6,5},{7,4},{8,11},{9,10},{10,... | collective-permute-start | bytes 884744 | tf_op jit(solution)/shard_map/ppermute | solution.py:73
  478.4 24.9 %collective-permute-start.58 = (bf16[448,1152]{1,0:T(8,128)(2,1)}, bf16[448,1152]{1,0:T(8,128)(2,1)}, u32[]{:S(2)}, u32[]{:S(2)}) collective-permute-start(bf16[448,1152]{1,0:T(8,128)(2,1)} %constant_dynamic-update-slice_fusion.20), channel_id=1, source_target_pairs={{0,4},{1,5},{2,6},{3,7},{4,0},{5,1},{6,2},{7,3},{8,12},{9,13},{10,... | collective-permute-start | bytes 3096584 | tf_op jit(solution)/shard_map/ppermute | solution.py:73
  (101 other events, 840.2 us)
Sparse Core Ops, SparseCore 0:
  116.7 90.0 all-gather.2
  210.2 93.5 all-gather.4

commit v4 on v3

--- a/solution.py
+++ b/solution.py
@@ -131,28 +131,6 @@
     return [line[:rows], *terms]
 
 
-def sum_over_ctx(value):
-    count, me = lax.axis_size("ctx"), lax.axis_index("ctx")
-    highs, low, high = count // 2, me % 2, me // 2
-    half, step = value.shape[0] // 2, value.shape[0] // count
-    (other,) = yield [swap(lax.dynamic_slice_in_dim(value, (1 - low) * half, half, 0).astype(BF), 4)]
-    line = lax.dynamic_slice_in_dim(value, low * half, half, 0) + other.astype(F32)
-    line_low = line.astype(BF)
-    terms = yield [
-        swap(lax.dynamic_slice_in_dim(line_low, (high ^ s) * step, step, 0), 8 * s)
-        for s in range(1, highs)
-    ]
-    total = lax.dynamic_slice_in_dim(line, high * step, step, 0)
-    total = (total + sum(term.astype(F32) for term in terms)).astype(BF)
-    pieces = yield [swap(total, 8 * s) for s in range(1, highs)]
-    line = line_low
-    for s, piece in enumerate([total, *pieces]):
-        line = lax.dynamic_update_slice_in_dim(line, piece, (high ^ s) * step, 0)
-    (other,) = yield [swap(line, 4)]
-    even, odd = jnp.where(low == 0, line, other), jnp.where(low == 0, other, line)
-    return join(even, odd).astype(F32)
-
-
 def gather_rows(value, me):
     pair, other = yield from gather_group(value)
     return settle(me ^ jnp.array([0, 2, 1, 3], jnp.int32), value.shape[0], pair, other)
@@ -165,6 +143,18 @@
     first_far, second_far = yield [swap(first_z, 4), swap(second_y, 8)]
     arrived += [first, first_z, first_far, second, second_y, second_z, second_far]
     return (yield [swap(first, 4)])
+
+
+def exchange_results(pieces, down):
+    others = yield [swap(pieces[o], o) for o in (1, 2, 3)]
+    mixed = join(*[piece.reshape(-1, piece.shape[2]) for piece in (pieces[0], *others)])
+    width = mixed.shape[1] // 2
+    first, second = [
+        jnp.concatenate([mixed[:, at], down[:, at].reshape(-1, down.shape[2])], axis=1)
+        for at in (slice(0, width), slice(width, 2 * width))
+    ]
+    first_y, second_z = yield [swap(first, 4), swap(second, 8)]
+    return [first, first_y, second, second_z]
 
 
 def kernel_call(kernel, out_shape, *operands, scalars=(), scratch=(), name):
@@ -648,8 +638,61 @@
     return x * share, share + share * (1.0 - share) * (2.0 * inner + 4.0 * cubic)
 
 
-def ffn_gradients_kernel(part, first, blocks, mine, second, d_ffn, w_gate, w_up, w_down, *rest):
-    outs, down_rows, act, d_both, both_sum, down_sum, sem = rest[-10:-6], *rest[-6:]
+def place_rows(part, blocks, mine, block, source, rows, sem):
+    width = source.shape[0]
+    odd = mine % 2
+    extra = blocks * width - part
+    begins = (block == 0) & (odd == 1)
+    ends = (block == blocks - 1) & (odd == 0)
+
+    def put(first, at, size):
+        copy = pltpu.make_async_copy(
+            source.at[pl.ds(first, size), :], rows.at[pl.ds(at, size), :], sem
+        )
+        copy.start()
+        copy.wait()
+
+    @pl.when(begins)
+    def _():
+        put(extra, 0, width - extra)
+
+    @pl.when(ends)
+    def _():
+        put(0, (blocks - 1) * width, width - extra)
+
+    @pl.when(jnp.logical_not(begins | ends))
+    def _():
+        put(0, pl.multiple_of(block * width - odd * extra, 64), width)
+
+
+def fill_rows_kernel(part, blocks, info, *refs):
+    sources, (rows, block, sem) = refs[:-4], refs[-3:]
+    for partner, source in enumerate(sources):
+        width = block.shape[0]
+        for tile in range(block.shape[1] // 128):
+            block[:, tile * 128 : (tile + 1) * 128] = source[
+                tile * width : (tile + 1) * width, width : width + 128
+            ].astype(F32)
+        place_rows(part, blocks, info[0], info[1 + partner], block, rows, sem)
+
+
+def fill_rows(info, part, blocks, sources, rows):
+    whole = pl.BlockSpec(memory_space=pltpu.VMEM)
+    anywhere = pl.BlockSpec(memory_space=pl.ANY)
+    return pl.pallas_call(
+        functools.partial(fill_rows_kernel, part, blocks),
+        in_specs=[pl.BlockSpec(memory_space=pltpu.SMEM)] + [whole] * len(sources) + [anywhere],
+        out_specs=anywhere,
+        out_shape=jax.ShapeDtypeStruct(rows.shape, rows.dtype),
+        scratch_shapes=[pltpu.VMEM((256, rows.shape[1]), F32), pltpu.SemaphoreType.DMA],
+        input_output_aliases={1 + len(sources): 0},
+        compiler_params=pltpu.CompilerParams(vmem_limit_bytes=VMEM_LIMIT),
+        name="fill_rows",
+    )(info, *sources, rows)
+
+
+def ffn_gradients_kernel(part, apart, blocks, info, second, d_ffn, w_gate, w_up, w_down, *rest):
+    outs, down_out, act, d_both, both_sum, down_sum, sem = rest[-10:-6], *rest[-6:]
     step = pl.program_id(1)
     rows, slab = second.shape[0], 256
     width = act.shape[1]
@@ -687,60 +730,45 @@
 
     @pl.when(step == pl.num_programs(1) - 1)
     def _():
-        block = first + pl.program_id(0)
-        odd = mine[0] % 2
-        extra = blocks * width - part
-        begins = (block == 0) & (odd == 1)
-        ends = (block == blocks - 1) & (odd == 0)
-
-        def put(source, at, size):
-            copy = pltpu.make_async_copy(
-                down_sum.at[pl.ds(source, size), :], down_rows.at[pl.ds(at, size), :], sem
-            )
-            copy.start()
-            copy.wait()
-
-        @pl.when(begins)
-        def _():
-            put(extra, 0, width - extra)
-
-        @pl.when(ends)
-        def _():
-            put(0, (blocks - 1) * width, width - extra)
-
-        @pl.when(jnp.logical_not(begins | ends))
-        def _():
-            put(0, pl.multiple_of(block * width - odd * extra, 64), width)
+        if apart:
+            for tile in range(down_out.shape[0]):
+                down_out[tile] = down_sum[:, tile * 128 : (tile + 1) * 128].astype(BF)
+        else:
+            place_rows(part, blocks, info[0], info[1 + pl.program_id(0)], down_sum, down_out, sem)
 
         quarter = second.shape[1] // 4
         for offset, out in enumerate(outs):
-            at = pl.ds(pl.multiple_of((mine[0] ^ offset) * quarter, 32), quarter)
+            at = pl.ds(pl.multiple_of((info[0] ^ offset) * quarter, 32), quarter)
             out[0] = both_sum[at, :width].astype(BF)
             out[1] = both_sum[at, width:].astype(BF)
 
 
-def ffn_gradients(mine, second_all, d_ffn_all, in_mat, down_mat, part, first, last, down_rows):
+def ffn_gradients(info, second_all, d_ffn_all, in_mat, down_mat, part, count, down_rows, apart):
     tokens, model = second_all.shape
     slab, width = min(2048, tokens), 256
-    columns = (last - first) * width
+    columns = count * width
     tall = pl.BlockSpec((slab, model), lambda j, t, m: (t, 0))
     anywhere = pl.BlockSpec(memory_space=pl.ANY)
     earlier = [] if down_rows is None else [down_rows]
     return pl.pallas_call(
-        functools.partial(ffn_gradients_kernel, part, first, down_mat.shape[0] // width),
+        functools.partial(ffn_gradients_kernel, part, apart, down_mat.shape[0] // width),
         grid_spec=pltpu.PrefetchScalarGridSpec(
             num_scalar_prefetch=1,
-            grid=(last - first, tokens // slab),
+            grid=(count, tokens // slab),
             in_specs=[
                 tall,
                 tall,
-                pl.BlockSpec((1, 1, model, width), lambda j, t, m: (0, j + first, 0, 0)),
-                pl.BlockSpec((1, 1, model, width), lambda j, t, m: (1, j + first, 0, 0)),
-                pl.BlockSpec((width, model), lambda j, t, m: (j + first, 0)),
+                pl.BlockSpec((1, 1, model, width), lambda j, t, m: (0, m[1 + j], 0, 0)),
+                pl.BlockSpec((1, 1, model, width), lambda j, t, m: (1, m[1 + j], 0, 0)),
+                pl.BlockSpec((width, model), lambda j, t, m: (m[1 + j], 0)),
             ]
             + [anywhere] * len(earlier),
             out_specs=[pl.BlockSpec((2, model // 4, width), lambda j, t, m: (0, 0, j))] * 4
-            + [anywhere],
+            + [
+                pl.BlockSpec((model // 128, width, 128), lambda j, t, m: (0, j, 0))
+                if apart
+                else anywhere
+            ],
             scratch_shapes=[
                 pltpu.VMEM((slab, width), BF),
                 pltpu.VMEM((slab, 2 * width), BF),
@@ -750,19 +778,23 @@
             ],
         ),
         out_shape=[jax.ShapeDtypeStruct((2, model // 4, columns), BF)] * 4
-        + [jax.ShapeDtypeStruct((part, model), F32)],
+        + [
+            jax.ShapeDtypeStruct((model // 128, columns, 128), BF)
+            if apart
+            else jax.ShapeDtypeStruct((part, model), F32)
+        ],
         input_output_aliases={6: 4} if earlier else {},
         compiler_params=pltpu.CompilerParams(vmem_limit_bytes=VMEM_ALL),
         cost_estimate=pl.CostEstimate(
             flops=12 * tokens * model * columns,
-            bytes_accessed=4 * tokens * model * (last - first),
+            bytes_accessed=4 * tokens * model * count,
             transcendentals=tokens * columns,
         ),
         name="ffn_gradients",
-    )(mine[None], second_all, d_ffn_all, in_mat, in_mat, down_mat, *earlier)
-
-
-def ffn_forward_kernel(near, far, w_gate, w_up, w_down, gate, up, keep, send, act, total):
+    )(info, second_all, d_ffn_all, in_mat, in_mat, down_mat, *earlier)
+
+
+def ffn_forward_kernel(near, far, w_gate, w_up, w_down, value, factor, keep, send, act, total):
     step, half = pl.program_id(0), near.shape[0]
 
     @pl.when(step == 0)
@@ -775,11 +807,13 @@
     ahead = products(near)
     for i in range(2):
         at = pl.ds(i * half, half)
-        left, right = ahead
+        gate, upper = ahead
         if i == 0:
             ahead = products(far)
-        gate[at, :], up[at, :] = left, right
-        act[at, :] = (gelu_and_slope(left)[0] * right).astype(BF)
+        gelu, slope = gelu_and_slope(gate)
+        act[at, :] = (gelu * upper).astype(BF)
+        value[at, :] = gelu.astype(BF)
+        factor[at, :] = (upper * slope).astype(BF)
     total[...] += contract(act[...], w_down[...], 1, 0)
 
     @pl.when(step == pl.num_programs(0) - 1)
@@ -787,22 +821,19 @@
         keep[...], send[...] = total[:half, :], total[half:, :].astype(BF)
 
 
-def ffn_backward_kernel(near, far, gate, up, w_gate, w_up, w_down, keep, send, d_gate, d_up, total):
+def ffn_backward_kernel(
+    near, far, value, factor, w_gate, w_up, w_down, keep, send, d_gate, d_up, total
+):
     step, half = pl.program_id(0), near.shape[0]
 
     @pl.when(step == 0)
     def _():
         total[...] = jnp.zeros_like(total)
 
-    ahead = contract(near[...], w_down[...], 1, 1)
-    for i in range(2):
-        at = pl.ds(i * half, half)
-        d_act = ahead
-        if i == 0:
-            ahead = contract(far[...], w_down[...], 1, 1)
-        value, slope = gelu_and_slope(gate[at, :])
-        d_gate[at, :] = (d_act * up[at, :] * slope).astype(BF)
-        d_up[at, :] = (d_act * value).astype(BF)
+    for rows, at in ((near, pl.ds(0, half)), (far, pl.ds(half, half))):
+        d_act = contract(rows[...], w_down[...], 1, 1)
+        d_gate[at, :] = (d_act * factor[at, :].astype(F32)).astype(BF)
+        d_up[at, :] = (d_act * value[at, :].astype(F32)).astype(BF)
     total[...] += contract(d_gate[...], w_gate[0, 0], 1, 1) + contract(d_up[...], w_up[0, 0], 1, 1)
 
     @pl.when(step == pl.num_programs(0) - 1)
@@ -816,7 +847,7 @@
     rows = pl.BlockSpec((half, model), lambda j: (0, 0))
     column = pl.BlockSpec((2 * half, width), lambda j: (0, j))
     forward = not kept
-    shape = jax.ShapeDtypeStruct((2 * half, wide), F32)
+    shape = jax.ShapeDtypeStruct((2 * half, wide), BF)
     return pl.pallas_call(
         kernel,
         grid=(wide // width,),
@@ -842,48 +873,51 @@
     )(near, far, *kept, in_mat, in_mat, down_mat)
 
 
-def unfold_kernel(part, mine, *refs):
-    out, sources = refs[-1], refs[:-1]
-    ranges = len(sources) // 4
-    extra = part % 128
-    for m in range(4):
-
-        @pl.when(mine[0] == m)
-        def _(m=m):
-            for side in range(2):
-                rows = [
-                    jnp.concatenate(
-                        [sources[r * 4 + (m ^ owner)][side] for r in range(ranges)], axis=1
-                    ).astype(F32)
-                    for owner in range(4)
-                ]
-                wide = rows[0].shape[1]
-                cut = wide - 128
-                left = lax.broadcasted_iota(jnp.int32, (rows[0].shape[0], 128), 1) < extra
-                pieces = []
-                for even, odd in (rows[:2], rows[2:]):
-                    shared = jnp.where(left, even[:, cut:], odd[:, :128])
-                    pieces += [even[:, :cut], shared, odd[:, 128:]]
-                out[:, side, :] = jnp.concatenate(pieces, axis=1)
-
-
-def unfold(mine, part, ranges):
+def unfold_kernel(part, info, *refs):
+    shared, sources, (out, wide) = refs[:4], refs[4:-2], refs[-2:]
+    mine, width = info[0], 256
+    for partner, source in enumerate(shared):
+        at = pl.ds(pl.multiple_of(info[1 + partner] * width, 128), width)
+        for offset in range(4):
+            wide[mine ^ offset, :, :, at] = source[offset, :, :, :width]
+    first = 4 * width
+    for r in range(0, len(sources), 4):
+        last = first + sources[r].shape[2]
+        for offset in range(4):
+            wide[mine ^ offset, :, :, first:last] = sources[r + offset][...]
+        first = last
+    cut = wide.shape[3] - 128
+    left = lax.broadcasted_iota(jnp.int32, (wide.shape[2], 128), 1) < part % 128
+    for side in range(2):
+        rows = [wide[owner, side].astype(F32) for owner in range(4)]
+        pieces = []
+        for even, odd in (rows[:2], rows[2:]):
+            shared_tile = jnp.where(left, even[:, cut:], odd[:, :128])
+            pieces += [even[:, :cut], shared_tile, odd[:, 128:]]
+        out[:, side, :] = jnp.concatenate(pieces, axis=1)
+
+
+def unfold(info, part, shared, ranges):
     sources = [piece for pieces in ranges for piece in pieces]
-    rows, step = sources[0].shape[1], 16
+    rows, step = sources[0].shape[1], 32
+    shared = [s.reshape(4, 2, rows, s.shape[1]) for s in shared]
+    columns = sum(pieces[0].shape[2] for pieces in ranges) + 4 * 256
     return pl.pallas_call(
         functools.partial(unfold_kernel, part),
         grid_spec=pltpu.PrefetchScalarGridSpec(
             num_scalar_prefetch=1,
             grid=(rows // step,),
             in_specs=[
-                pl.BlockSpec((2, step, s.shape[2]), lambda i, m: (0, i, 0)) for s in sources
-            ],
+                pl.BlockSpec((4, 2, step, s.shape[3]), lambda i, m: (0, 0, i, 0)) for s in shared
+            ]
+            + [pl.BlockSpec((2, step, s.shape[2]), lambda i, m: (0, i, 0)) for s in sources],
             out_specs=pl.BlockSpec((step, 2, 4 * part), lambda i, m: (i, 0, 0)),
+            scratch_shapes=[pltpu.VMEM((4, 2, step, columns), BF)],
         ),
         out_shape=jax.ShapeDtypeStruct((rows, 2, 4 * part), F32),
         compiler_params=pltpu.CompilerParams(vmem_limit_bytes=VMEM_LIMIT),
         name="unfold",
-    )(mine[None], *sources)
+    )(info, *shared, *sources)
 
 
 def pick(table, index):
@@ -966,11 +1000,16 @@
     )
     pairs_flow = Flow(gather_wide(pair_rows))
     own, to_core = carve(jnp.swapaxes(w_in, 0, 1), mine, part, wide)
-    own, to_core, w_query = pace((own, to_core, w_query), pairs_flow, columns_flow)
+    down_mat = lax.dynamic_update_slice_in_dim(
+        jnp.zeros((wide, model), BF), w_down, part % 128 * (mine % 2), 0
+    )
+    own, to_core, w_query, down_mat = pace(
+        (own, to_core, w_query, down_mat), pairs_flow, columns_flow
+    )
     core_flow = Flow(iter_once([swap(to_core, 1)]))
     query_flow = Flow(gather_rows(w_query, mine))
-    w_out, w_down = pace((w_out, w_down), pairs_flow, columns_flow, core_flow)
-    w_out, w_down = pace((w_out, w_down), pairs_flow, columns_flow, query_flow)
+    pace((), pairs_flow, columns_flow, core_flow)
+    (w_out,) = pace((w_out,), pairs_flow, columns_flow, query_flow)
     out_flow = Flow(gather_rows(w_out, mine))
     pairs = finish(pairs_flow)
     query_mat = finish(query_flow)
@@ -983,9 +1022,6 @@
         cosine,
         sine,
         name="queries",
-    )
-    down_mat = lax.dynamic_update_slice_in_dim(
-        jnp.zeros((wide, model), BF), w_down, part % 128 * (mine % 2), 0
     )
     *probs, weighted, mass = attend(blocks, queries, q_place, q_start, *pairs)
     weighted, mass = pace((weighted, mass), out_flow, columns_flow)
@@ -1021,7 +1057,7 @@
     laid = lay(places[:9] + places[10:], (own, *core_flow.result, *arrived))
     (laid,) = pace((laid,), group_flow, columns_flow)
     in_mat = lay(places[9:10], columns_flow.result, laid)
-    gate, upper, keep, send = ffn_group(ffn_forward_kernel, *finish(group_flow), in_mat, down_mat)
+    value, factor, keep, send = ffn_group(ffn_forward_kernel, *finish(group_flow), in_mat, down_mat)
     block_out, d_ffn_low, d_gain_ffn_out = kernel_call(
         after_ffn_kernel,
         [((rows, model), BF), ((rows, model), BF), ((1, model), F32)],
@@ -1034,7 +1070,7 @@
     group_flow = Flow(gather_group(d_ffn_low))
     d_ffn_all = lax.all_gather(d_ffn_low, AXES, axis=0, tiled=True)
     keep, send = ffn_group(
-        ffn_backward_kernel, *finish(group_flow), in_mat, down_mat, gate, upper
+        ffn_backward_kernel, *finish(group_flow), in_mat, down_mat, value, factor
     )
     d_hidden, d_attn_low, d_heads, dots, d_gain_ffn_in, d_gain_attn_out = kernel_call(
         before_attend_back_kernel,
@@ -1082,9 +1118,9 @@
     )
     keep, send, d_first_query = pace((keep, send, d_first_query), sums_flow)
     pace((), sums_flow)
-    pace((), sums_flow)
     early_flow = Flow(scatter_group(keep, send))
     pace((), sums_flow, early_flow)
+    pace((), sums_flow)
     grad_tokens, keep, send = kernel_call(
         key_back_kernel,
         [
@@ -1114,41 +1150,49 @@
     tail_flow = Flow(scatter_group(keep, send))
 
     count = wide // 256
-    unit = count // 7
-    cuts = [0, 2 * unit, 4 * unit, 5 * unit, 6 * unit, count]
+    block_info = jnp.stack([mine, low_bit, 1 - low_bit, 2 + high_bit, 3 - high_bit])
+
+    def total(flow):
+        near, far = flow.result
+        return near + far.astype(F32)
+
+    pace((), tail_flow)
+    both = (second_all, d_ffn_all)
+    *pieces, down = ffn_gradients(
+        block_info[jnp.array([0, 1, 3])], *both, in_mat, down_mat, part, 2, None, True
+    )
+    both, pieces, down = pace((both, pieces, down), tail_flow, early_flow)
+    early, tail = total(early_flow), total(tail_flow)
+    tail = jnp.pad(tail, ((0, 0), (0, model - tail.shape[1])))
+    rest = lax.psum(join(early, tail).astype(BF), "ctx")
+    shared_flow = Flow(exchange_results(pieces, down))
     ranges, grad_down = [], None
-    both = (second_all, d_ffn_all)
-
-    def columns_step(*flows):
-        nonlocal both, grad_down
-        i = len(ranges)
+    for first, last in ((4, 5), (5, count)):
         *pieces, grad_down = ffn_gradients(
-            mine, *both, in_mat, down_mat, part, cuts[i], cuts[i + 1], grad_down
+            jnp.stack([mine, *[jnp.int32(i) for i in range(first, last)]]),
+            *both,
+            in_mat,
+            down_mat,
+            part,
+            last - first,
+            grad_down,
+            False,
         )
         over_x = [sent[2:] for sent in ranges]
-        both, grad_down, over_x = pace((both, grad_down, over_x), *flows)
+        both, grad_down, over_x = pace((both, grad_down, over_x), shared_flow)
         for sent, arrays in zip(ranges, over_x):
             sent[2:] = arrays
         ranges.append([pieces[0]] + [swap(pieces[o], o) for o in (1, 2, 3)])
-
-    def total(flow):
-        near, far = flow.result
-        return near + far.astype(F32)
-
-    pace((), tail_flow)
-    columns_step(tail_flow, early_flow)
-    early, tail = total(early_flow), total(tail_flow)
-    tail = jnp.pad(tail, ((0, 0), (0, model - tail.shape[1])))
-    spare = -(early.shape[0] + tail.shape[0]) % 128
-    rest_flow = Flow(sum_over_ctx(join(early, tail, jnp.zeros((spare, model), F32))))
-    for _ in range(4):
-        columns_step(rest_flow)
-    early, tail = rest_flow.result[:early_rows], rest_flow.result[early_rows:]
+    shared = shared_flow.result
+    grad_down = fill_rows(block_info, part, count, shared, grad_down)
+    rest, grad_down = pace((rest, grad_down))
+    early, tail = rest[:early_rows], rest[early_rows:]
+    grad_in = unfold(block_info, part, shared, ranges)
+    early, tail = early.astype(F32), tail.astype(F32)
     grad_query = early[:quarter, : H * HD]
     grad_out = early[quarter:]
     grad_key, grad_value = tail[:quarter, :HD], tail[:quarter, HD : 2 * HD]
     gain_grads = [tail[:size, 2 * HD + i] for i, size in enumerate(sizes)]
-    grad_in = unfold(mine, part, ranges)
 
     return (
         block_out,

time: 551 us -> 490 us (0.89)
  Pallas kernels: 248 us -> 203 us
  starting transfers between devices: 72.8 us -> 55.5 us
    pallas_call x5 -> x4, Pallas kernels: 157 us -> 116 us  [the longest x3 110 us: ffn_gradients(): pl.pallas_call(functools.partial(ffn_gradients_kernel, part, apart, down_...]
    ppermute x66 -> x54, starting transfers between devices: 72.5 us -> 54.9 us  [swap(): return lax.ppermute(value, AXES, [(i, i ^ offset) for i in range(count)])]
    psum x0 -> x1, waiting for transfers between devices: none -> 9.61 us  [body(): rest = lax.psum(join(early, tail).astype(BF), 'ctx')]
    concatenate x0 -> x4, other arithmetic: none -> 7.46 us  [exchange_results(): jnp.concatenate([mixed[:, at], down[:, at].reshape(-1, down.shape[2])], a...]
    ppermute x66 -> x54, waiting for transfers between devices: 119 us -> 113 us  [swap(): return lax.ppermute(value, AXES, [(i, i ^ offset) for i in range(count)])]
    another operation x2 -> x6, other arithmetic: 0.44 us -> 6.43 us
    unnamed x142 -> x168, local copies, waits for them, and re-layouts: 31.8 us -> 33.8 us
  transfers between devices with their start and end apart: 68 -> 57, of which waited for: 25 -> 26; matrix products, arithmetic and copies ran while one was open for 9% -> 10% of each run, Pallas kernels for 43% -> 39%
where the time goes in v4:
time: 490 us; the launch traced here: 480 us
  Pallas kernels  203 us (41%)
  waiting for transfers between devices  126 us (26%)
  starting transfers between devices  55.5 us (11%)
  local copies, waits for them, and re-layouts  51.5 us (11%)
  other arithmetic  29.3 us (6%)
  between operations  15.1 us (3%)
    ppermute x54, waiting for transfers between devices, swap(): return lax.ppermute(value, AXES, [(i, i ^ offset) for i in range(count)])  113 us
    pallas_call x3, Pallas kernels, ffn_gradients(): pl.pallas_call(functools.partial(ffn_gradients_kernel, part, apart, down_...  110 us
    ppermute x54, starting transfers between devices, swap(): return lax.ppermute(value, AXES, [(i, i ^ offset) for i in range(count)])  54.9 us
    unnamed x168, local copies, waits for them, and re-layouts  33.8 us
    pallas_call x2, Pallas kernels, ffn_group(): pl.pallas_call(kernel, grid=(wide // width,), in_specs=[rows, rows] + [co...  28 us
    pallas_call x2, Pallas kernels, lay(): pl.pallas_call(functools.partial(lay_kernel, counts), grid_spec=pltpu.Pre...  13.5 us
    pallas_call x1, Pallas kernels, unfold(): pl.pallas_call(functools.partial(unfold_kernel, part), grid_spec=pltpu.Pr...  11 us
    pallas_call x9, Pallas kernels, kernel_call(): pl.pallas_call(kernel, out_shape=[jax.ShapeDtypeStruct(shape, dtype) for...  11 us
  transfers between devices with their start and end apart: 57, of which 26 were waited for; matrix products, arithmetic and copies ran while one was open for 10% of the time, Pallas kernels for 39%

profile of v4, /device:TPU:1, one launch (start us, length us, event | category | flops | bytes accessed | tf_op | source)
XLA Modules:
  0.0 480.5 jit_solution(4944722684344770417)
XLA Ops:
  17.7 5.9 %carve_quarters.1 = (bf16[1,144,1792]{2,1,0:T(8,128)(2,1)}, bf16[1,144,1792]{2,1,0:T(8,128)(2,1)}) custom-call(s32[3]{0:T(128)} %pad_add_fusion.1.place, bf16[288,2,6912]{2,1,0:T(2,128)(2,1)} %w.1), custom_call_target="tpu_custom_call" | custom-call | tf_op jit(solution)/shard_map/carve_quarters/pallas_call | solution.py:531
  30.4 3.3 collective-permute-start.4
  38.5 4.0 copy.44
  45.3 6.0 %collective-permute-done.6.refs_5_ = bf16[1,144,1792]{2,1,0:T(8,128)(2,1)} collective-permute-done((bf16[1,144,1792]{2,1,0:T(8,128)(2,1)}, bf16[1,144,1792]{2,1,0:T(8,128)(2,1)}, u32[]{:S(2)}, u32[]{:S(2)}) %collective-permute-start.6) | collective-permute-done | bytes 516128 | tf_op jit(solution)/shard_map/ppermute | solution.py:73
  59.4 9.5 %collective-permute-done.9.refs_3_ = bf16[1,144,1792]{2,1,0:T(8,128)(2,1)S(1)} collective-permute-done((bf16[1,144,1792]{2,1,0:T(8,128)(2,1)}, bf16[1,144,1792]{2,1,0:T(8,128)(2,1)S(1)}, u32[]{:S(2)}, u32[]{:S(2)}) %collective-permute-start.9) | collective-permute-done | bytes 516128 | tf_op jit(solution)/shard_map/ppermute | solution.py:73
  72.8 8.1 %collective-permute-done.14.refs_6_ = bf16[1,144,1792]{2,1,0:T(8,128)(2,1)S(1)} collective-permute-done((bf16[1,144,1792]{2,1,0:T(8,128)(2,1)}, bf16[1,144,1792]{2,1,0:T(8,128)(2,1)S(1)}, u32[]{:S(2)}, u32[]{:S(2)}) %collective-permute-start.14) | collective-permute-done | bytes 516128 | tf_op jit(solution)/shard_map/ppermute | solution.py:73
  81.9 4.6 collective-permute-done.12
  96.8 7.2 %attend.1 = (bf16[2048,512]{1,0:T(8,128)(2,1)S(1)}, bf16[2048,512]{1,0:T(8,128)(2,1)S(1)}, f32[256,512]{1,0:T(8,128)S(1)}, f32[1,512]{1,0:T(1,128)S(1)}) custom-call(s32[64]{0:T(128)S(1)} %select_reduce_fusion.blocks, bf16[512,256]{1,0:T(8,128)(2,1)S(1)} %get-tuple-element.169.q, s32[1,512]{1,0:T(1,128)S(1)} %bitcast.42, s32[1,512]{1,0:T(1,128)S(1)} %bitcast.41, ...), custom_call_target="tpu_custom_call" | custom-call | flops 2147483648 | bytes 8388608 | tf_op jit(solution)/shard_map/attend/pallas_call | solution.py:275
  120.2 11.7 %lay.2.refs_1_ = bf16[2,7,1152,256]{3,2,1,0:T(8,128)(2,1)} custom-call(s32[15]{0:T(128)} %stack.96.sides, s32[15]{0:T(128)} %stack.105.rows, bf16[2,288,1792]{2,1,0:T(8,128)(2,1)} %copy-done.16, bf16[2,288,1792]{2,1,0:T(8,128)(2,1)} %copy-done.62, bf16[1,144,1792]{2,1,0:T(8,128)(2,1)} %collective-permute-done.5.refs_2_, bf16[1,144,1792]{2,1,0:T(8,128)(2,1)} %copy-done.69, ...), custom_call_target="tpu_custom_call" | custom-call | tf_op jit(solution)/shard_map/lay/pallas_call | solution.py:609
  137.1 14.0 %ffn_forward.1 = (bf16[512,1792]{1,0:T(8,128)(2,1)}, bf16[512,1792]{1,0:T(8,128)(2,1)}, f32[256,1152]{1,0:T(8,128)}, bf16[256,1152]{1,0:T(8,128)(2,1)}) custom-call(bf16[256,1152]{1,0:T(8,128)(2,1)} %constant_dynamic-update-slice_fusion.16.near, bf16[256,1152]{1,0:T(8,128)(2,1)} %collective-permute-done.24.far, bf16[2,7,1152,256]{3,2,1,0:T(8,128)(2,1)} %lay.3.w_gate.w_up, ...), custom_call_target="tpu_custom_call" | custom-call | flops 6341787648 | bytes 19726336 | tf_op jit(solution)/shard_map/ffn_forward/pallas_call | solution.py:851
  155.7 7.3 %collective-permute-done.26.other = bf16[128,1152]{1,0:T(8,128)(2,1)S(1)} collective-permute-done((bf16[128,1152]{1,0:T(8,128)(2,1)S(1)}, bf16[128,1152]{1,0:T(8,128)(2,1)S(1)}, u32[]{:S(2)}, u32[]{:S(2)}) %collective-permute-start.26) | collective-permute-done | bytes 294944 | tf_op jit(solution)/shard_map/ppermute | solution.py:73
  167.0 10.5 %collective-permute-done.27 = bf16[128,1152]{1,0:T(8,128)(2,1)S(1)} collective-permute-done((bf16[128,1152]{1,0:T(8,128)(2,1)}, bf16[128,1152]{1,0:T(8,128)(2,1)S(1)}, u32[]{:S(2)}, u32[]{:S(2)}) %collective-permute-start.27) | collective-permute-done | bytes 294944 | tf_op jit(solution)/shard_map/ppermute | solution.py:73
  177.5 3.5 collective-permute-start.28
  183.5 14.0 %ffn_backward.1 = (f32[256,1152]{1,0:T(8,128)}, bf16[256,1152]{1,0:T(8,128)(2,1)}) custom-call(bf16[256,1152]{1,0:T(8,128)(2,1)} %copy-done.63, bf16[256,1152]{1,0:T(8,128)(2,1)} %copy-done.66, bf16[512,1792]{1,0:T(8,128)(2,1)} %get-tuple-element.197.value, bf16[512,1792]{1,0:T(8,128)(2,1)} %get-tuple-element.198.factor, ...), custom_call_target="tpu_custom_call" | custom-call | flops 6341787648 | bytes 19726336 | tf_op jit(solution)/shard_map/ffn_backward/pallas_call | solution.py:851
  203.1 7.2 %collective-permute-done.30.other = bf16[128,1152]{1,0:T(8,128)(2,1)S(1)} collective-permute-done((bf16[128,1152]{1,0:T(8,128)(2,1)S(1)}, bf16[128,1152]{1,0:T(8,128)(2,1)S(1)}, u32[]{:S(2)}, u32[]{:S(2)}) %collective-permute-start.30) | collective-permute-done | bytes 294944 | tf_op jit(solution)/shard_map/ppermute | solution.py:73
  218.1 6.9 %attend_back.1 = (f32[256,512]{1,0:T(8,128)S(1)}, bf16[2048,512]{1,0:T(8,128)(2,1)S(1)}, bf16[2048,512]{1,0:T(8,128)(2,1)S(1)}) custom-call(bf16[512,256]{1,0:T(8,128)(2,1)S(1)} %copy-done.40, bf16[512,256]{1,0:T(8,128)(2,1)S(1)} %get-tuple-element.203.d_heads, f32[1,512]{1,0:T(1,128)S(1)} %get-tuple-element.180.mass, f32[1,512]{1,0:T(1,128)S(1)} %get-tuple-element.204.dots, ...), custom_call_target="tpu_custom_call" | custom-call | flops 4294967296 | bytes 12582912 | tf_op jit(solution)/shard_map/attend_back/pallas_call | solution.py:389
  225.7 2.9 query_back.1
  233.3 8.9 %collective-permute-done.33 = bf16[256,512]{1,0:T(8,128)(2,1)S(1)} collective-permute-done((bf16[256,512]{1,0:T(8,128)(2,1)S(1)}, bf16[256,512]{1,0:T(8,128)(2,1)S(1)}, u32[]{:S(2)}, u32[]{:S(2)}) %collective-permute-start.33) | collective-permute-done | bytes 262176 | tf_op jit(solution)/shard_map/ppermute | solution.py:73
  247.6 9.8 %collective-permute-done.34 = bf16[512,512]{1,0:T(8,128)(2,1)S(1)} collective-permute-done((bf16[512,512]{1,0:T(8,128)(2,1)S(1)}, bf16[512,512]{1,0:T(8,128)(2,1)S(1)}, u32[]{:S(2)}, u32[]{:S(2)}) %collective-permute-start.34) | collective-permute-done | bytes 524320 | tf_op jit(solution)/shard_map/ppermute | solution.py:73
  260.3 3.2 collective-permute-start.39
  266.7 2.7 collective-permute-done.39.refs_2_
  269.3 19.0 %collective-permute-done.38.refs_1_ = bf16[128,512]{1,0:T(8,128)(2,1)S(1)} collective-permute-done((bf16[128,512]{1,0:T(8,128)(2,1)}, bf16[128,512]{1,0:T(8,128)(2,1)S(1)}, u32[]{:S(2)}, u32[]{:S(2)}) %collective-permute-start.38) | collective-permute-done | bytes 131104 | tf_op jit(solution)/shard_map/ppermute | solution.py:73
  294.3 3.0 add_convert_fusion.1
  299.7 3.5 all-gather.5.cloned.1.call-done.d_ffn
  303.2 41.6 %ffn_gradients.3 = (bf16[2,288,512]{2,1,0:T(8,128)(2,1)}, bf16[2,288,512]{2,1,0:T(8,128)(2,1)}, bf16[2,288,512]{2,1,0:T(8,128)(2,1)}, bf16[2,288,512]{2,1,0:T(8,128)(2,1)}, bf16[9,512,128]{2,1,0:T(8,128)(2,1)}) custom-call(s32[3]{0:T(128)} %gather_fusion, bf16[4096,1152]{1,0:T(8,128)(2,1)} %all-gather.3.cloned.1.call-done.second, ...), custom_call_target="tpu_custom_call" | custom-call | flops 28991029248 | bytes 37748736 | tf_op jit(solution)/shard_map/ffn_gradients/pallas_call | solution.py:753
  352.1 25.0 %ffn_gradients.4 = (bf16[2,288,256]{2,1,0:T(8,128)(2,1)}, bf16[2,288,256]{2,1,0:T(8,128)(2,1)}, bf16[2,288,256]{2,1,0:T(8,128)(2,1)}, bf16[2,288,256]{2,1,0:T(8,128)(2,1)}, f32[1728,1152]{1,0:T(8,128)}) custom-call(s32[2]{0:T(128)} %pad_add_fusion.2.info, bf16[4096,1152]{1,0:T(8,128)(2,1)} %all-gather.3.cloned.1.call-done.second, ...), custom_call_target="tpu_custom_call" | custom-call | flops 14495514624 | bytes 18874368 | tf_op jit(solution)/shard_map/ffn_gradients/pallas_call | solution.py:753
  383.3 43.4 %ffn_gradients.5 = (bf16[2,288,512]{2,1,0:T(8,128)(2,1)}, bf16[2,288,512]{2,1,0:T(8,128)(2,1)}, bf16[2,288,512]{2,1,0:T(8,128)(2,1)}, bf16[2,288,512]{2,1,0:T(8,128)(2,1)}, f32[1728,1152]{1,0:T(8,128)}) custom-call(s32[3]{0:T(128)} %pad_add_fusion.3.info, bf16[4096,1152]{1,0:T(8,128)(2,1)} %all-gather.3.cloned.1.call-done.second, ...), custom_call_target="tpu_custom_call", output_to_operand_aliasing={{4}: (6, {})} | custom-call | flops 28991029248 | bytes 37748736 | tf_op jit(solution)/shard_map/ffn_gradients/pallas_call | solution.py:753
  426.7 3.0 pad_maximum_fusion.3.refs_0_
  434.0 4.3 collective-permute-done.49.refs_3_
  438.4 6.3 %fill_rows.1 = f32[1728,1152]{1,0:T(8,128)} custom-call(s32[5]{0:T(128)S(1)} %stack.109.info, bf16[2304,384]{1,0:T(8,128)(2,1)} %pad_maximum_fusion.1.refs_0_, bf16[2304,384]{1,0:T(8,128)(2,1)S(1)} %collective-permute-done.48.refs_1_, bf16[2304,384]{1,0:T(8,128)(2,1)} %pad_maximum_fusion.2.refs_2_, ...), custom_call_target="tpu_custom_call", output_to_operand_aliasing={{}: (5, {})} | custom-call | tf_op jit(solution)/shard_map/fill_rows/pallas_call | solution.py:682
  444.7 9.6 %all-reduce.3.cloned.1.call-done = bf16[832,1152]{1,0:T(8,128)(2,1)} async-done(((bf16[832,1152]{1,0:T(8,128)(2,1)}), bf16[832,1152]{1,0:T(8,128)(2,1)}) %all-reduce.3.cloned.1.call-update) | async-done | bytes 1916944 | tf_op jit(solution)/shard_map/psum | solution.py:1167
  462.5 11.0 %unfold.1 = f32[288,2,6912]{2,1,0:T(2,128)} custom-call(s32[5]{0:T(128)S(1)} %stack.109.info, bf16[4,2,288,384]{3,2,1,0:T(8,128)(2,1)S(1)} %copy-done.6, bf16[4,2,288,384]{3,2,1,0:T(8,128)(2,1)S(1)} %bitcast.39, bf16[4,2,288,384]{3,2,1,0:T(8,128)(2,1)S(1)} %copy-done.7, bf16[4,2,288,384]{3,2,1,0:T(8,128)(2,1)S(1)} %bitcast.40, ...), custom_call_target="tpu_custom_call" | custom-call | tf_op jit(solution)/shard_map/unfold/pallas_call | solution.py:905
  (345 shorter events, 144.5 us)
Async XLA Ops:
  7.2 292.5 %all-gather.3.cloned.1.call-start = ((), (), s32[]{:S(2)}) async-start(), calls=%async_computation | async-start | bytes 9732096 | tf_op jit(solution)/shard_map/all_gather | solution.py:1047
  26.3 18.9 %collective-permute-start.5 = (bf16[1,144,1792]{2,1,0:T(8,128)(2,1)}, bf16[1,144,1792]{2,1,0:T(8,128)(2,1)}, u32[]{:S(2)}, u32[]{:S(2)}) collective-permute-start(bf16[1,144,1792]{2,1,0:T(8,128)(2,1)} %get-tuple-element.157), channel_id=1, source_target_pairs={{0,2},{1,3},{2,0},{3,1},{4,6},{5,7},{6,4},{7,5},{8,10},{9,11},{10,... | collective-permute-start | bytes 1548296 | tf_op jit(solution)/shard_map/ppermute | solution.py:73
  26.8 24.4 %collective-permute-start.6 = (bf16[1,144,1792]{2,1,0:T(8,128)(2,1)}, bf16[1,144,1792]{2,1,0:T(8,128)(2,1)}, u32[]{:S(2)}, u32[]{:S(2)}) collective-permute-start(bf16[1,144,1792]{2,1,0:T(8,128)(2,1)} %get-tuple-element.158), channel_id=1, source_target_pairs={{0,3},{1,2},{2,1},{3,0},{4,7},{5,6},{6,5},{7,4},{8,11},{9,10},{10,... | collective-permute-start | bytes 1548296 | tf_op jit(solution)/shard_map/ppermute | solution.py:73
  30.4 20.9 %collective-permute-start.4 = (bf16[128,512]{1,0:T(8,128)(2,1)}, bf16[128,512]{1,0:T(8,128)(2,1)}, u32[]{:S(2)}, u32[]{:S(2)}) collective-permute-start(bf16[128,512]{1,0:T(8,128)(2,1)} %get-tuple-element.156), channel_id=1, source_target_pairs={{0,24},{1,25},{2,26},{3,27},{4,28},{5,29},{6,30},{7,31},{8,16},{9,... | collective-permute-start | bytes 393224 | tf_op jit(solution)/shard_map/ppermute | solution.py:73
  33.7 17.6 %collective-permute-start.3 = (bf16[128,512]{1,0:T(8,128)(2,1)}, bf16[128,512]{1,0:T(8,128)(2,1)}, u32[]{:S(2)}, u32[]{:S(2)}) collective-permute-start(bf16[128,512]{1,0:T(8,128)(2,1)} %get-tuple-element.156), channel_id=1, source_target_pairs={{0,16},{1,17},{2,18},{3,19},{4,20},{5,21},{6,22},{7,23},{8,24},{9,... | collective-permute-start | bytes 393224 | tf_op jit(solution)/shard_map/ppermute | solution.py:73
  33.7 17.6 %collective-permute-start.2 = (bf16[128,512]{1,0:T(8,128)(2,1)}, bf16[128,512]{1,0:T(8,128)(2,1)}, u32[]{:S(2)}, u32[]{:S(2)}) collective-permute-start(bf16[128,512]{1,0:T(8,128)(2,1)} %get-tuple-element.156), channel_id=1, source_target_pairs={{0,8},{1,9},{2,10},{3,11},{4,12},{5,13},{6,14},{7,15},{8,0},{9,1},... | collective-permute-start | bytes 393224 | tf_op jit(solution)/shard_map/ppermute | solution.py:73
  51.2 20.1 %collective-permute-start.10 = (bf16[2,288,1792]{2,1,0:T(8,128)(2,1)S(1)}, bf16[2,288,1792]{2,1,0:T(8,128)(2,1)S(1)}, u32[]{:S(2)}, u32[]{:S(2)}) collective-permute-start(bf16[2,288,1792]{2,1,0:T(8,128)(2,1)S(1)} %get-tuple-element.164), channel_id=1, source_target_pairs={{0,1},{1,0},{2,3},{3,2},{4,5},{5,4},{6,7},{7,6},{8,9},{9,8},{10,11... | collective-permute-start | bytes 6193160 | tf_op jit(solution)/shard_map/ppermute | solution.py:73
  58.3 23.5 %collective-permute-start.15 = (bf16[288,1024]{1,0:T(8,128)(2,1)S(1)}, bf16[288,1024]{1,0:T(8,128)(2,1)S(1)}, u32[]{:S(2)}, u32[]{:S(2)}) collective-permute-start(bf16[288,1024]{1,0:T(8,128)(2,1)S(1)} %copy-done.67), channel_id=1, source_target_pairs={{0,2},{1,3},{2,0},{3,1},{4,6},{5,7},{6,4},{7,5},{8,10},{9,11},{10,... | collective-permute-start | bytes 1769480 | tf_op jit(solution)/shard_map/ppermute | solution.py:73
  71.4 15.1 %collective-permute-start.12 = (bf16[256,512]{1,0:T(8,128)(2,1)S(1)}, bf16[256,512]{1,0:T(8,128)(2,1)S(1)}, u32[]{:S(2)}, u32[]{:S(2)}) collective-permute-start(bf16[256,512]{1,0:T(8,128)(2,1)S(1)} %slice.148), channel_id=1, source_target_pairs={{0,4},{1,5},{2,6},{3,7},{4,0},{5,1},{6,2},{7,3},{8,12},{9,13},{10,... | collective-permute-start | bytes 786440 | tf_op jit(solution)/shard_map/ppermute | solution.py:73
  71.7 15.2 %collective-permute-start.11 = (bf16[256,512]{1,0:T(8,128)(2,1)S(1)}, bf16[256,512]{1,0:T(8,128)(2,1)S(1)}, u32[]{:S(2)}, u32[]{:S(2)}) collective-permute-start(bf16[256,512]{1,0:T(8,128)(2,1)S(1)} %slice.147), channel_id=1, source_target_pairs={{0,2},{1,3},{2,0},{3,1},{4,6},{5,7},{6,4},{7,5},{8,10},{9,11},{10,... | collective-permute-start | bytes 786440 | tf_op jit(solution)/shard_map/ppermute | solution.py:73
  89.1 16.2 %collective-permute-start.19 = (bf16[1,144,1792]{2,1,0:T(8,128)(2,1)S(1)}, bf16[1,144,1792]{2,1,0:T(8,128)(2,1)S(1)}, u32[]{:S(2)}, u32[]{:S(2)}) collective-permute-start(bf16[1,144,1792]{2,1,0:T(8,128)(2,1)S(1)} %collective-permute-done.9.refs_3_), channel_id=1, source_target_pairs={{0,4},{1,5},{2,6},{3,7},{4,0},{5,1},{6,2},{7,3},{8,12},{9,13},{10,... | collective-permute-start | bytes 1548296 | tf_op jit(solution)/shard_map/ppermute | solution.py:73
  90.4 14.9 %collective-permute-start.20 = (bf16[1,144,1792]{2,1,0:T(8,128)(2,1)S(1)}, bf16[1,144,1792]{2,1,0:T(8,128)(2,1)S(1)}, u32[]{:S(2)}, u32[]{:S(2)}) collective-permute-start(bf16[1,144,1792]{2,1,0:T(8,128)(2,1)S(1)} %collective-permute-done.14.refs_6_), channel_id=1, source_target_pairs={{0,8},{1,9},{2,10},{3,11},{4,12},{5,13},{6,14},{7,15},{8,0},{9,1},... | collective-permute-start | bytes 1548296 | tf_op jit(solution)/shard_map/ppermute | solution.py:73
  117.1 186.1 %all-gather.5.cloned.1.call-start = ((), (), s32[]{:S(2)}) async-start(), calls=%async_computation.1 | async-start | bytes 9732096 | tf_op jit(solution)/shard_map/all_gather | solution.py:1071
  117.6 15.9 %collective-permute-start.23 = (bf16[1,144,1792]{2,1,0:T(8,128)(2,1)}, bf16[1,144,1792]{2,1,0:T(8,128)(2,1)}, u32[]{:S(2)}, u32[]{:S(2)}) collective-permute-start(bf16[1,144,1792]{2,1,0:T(8,128)(2,1)} %collective-permute-done.5.refs_2_), channel_id=1, source_target_pairs={{0,4},{1,5},{2,6},{3,7},{4,0},{5,1},{6,2},{7,3},{8,12},{9,13},{10,... | collective-permute-start | bytes 1548296 | tf_op jit(solution)/shard_map/ppermute | solution.py:73
  117.9 15.6 %collective-permute-start.22 = (bf16[128,1152]{1,0:T(8,128)(2,1)}, bf16[128,1152]{1,0:T(8,128)(2,1)S(1)}, u32[]{:S(2)}, u32[]{:S(2)}) collective-permute-start(bf16[128,1152]{1,0:T(8,128)(2,1)} %get-tuple-element.182), channel_id=1, source_target_pairs={{0,2},{1,3},{2,0},{3,1},{4,6},{5,7},{6,4},{7,5},{8,10},{9,11},{10,... | collective-permute-start | bytes 884744 | tf_op jit(solution)/shard_map/ppermute | solution.py:73
  164.9 289.4 %all-reduce.3.cloned.1.call-start = ((), (), s32[]{:S(2)}) async-start(), calls=%async_computation.2 | async-start | bytes 3833856 | tf_op jit(solution)/shard_map/psum | solution.py:1167
  229.5 28.6 %collective-permute-start.36 = (bf16[1088,1152]{1,0:T(8,128)(2,1)S(1)}, bf16[1088,1152]{1,0:T(8,128)(2,1)S(1)}, u32[]{:S(2)}, u32[]{:S(2)}) collective-permute-start(bf16[1088,1152]{1,0:T(8,128)(2,1)S(1)} %get-tuple-element.219), channel_id=1, source_target_pairs={{0,1},{1,0},{2,3},{3,2},{4,5},{5,4},{6,7},{7,6},{8,9},{9,8},{10,11... | collective-permute-start | bytes 7520264 | tf_op jit(solution)/shard_map/ppermute | solution.py:73
  263.5 24.8 %collective-permute-start.38 = (bf16[128,512]{1,0:T(8,128)(2,1)}, bf16[128,512]{1,0:T(8,128)(2,1)S(1)}, u32[]{:S(2)}, u32[]{:S(2)}) collective-permute-start(bf16[128,512]{1,0:T(8,128)(2,1)} %get-tuple-element.301), channel_id=1, source_target_pairs={{0,16},{1,17},{2,18},{3,19},{4,20},{5,21},{6,22},{7,23},{8,24},{9,... | collective-permute-start | bytes 393224 | tf_op jit(solution)/shard_map/ppermute | solution.py:73
  263.5 24.8 %collective-permute-start.37 = (bf16[128,512]{1,0:T(8,128)(2,1)}, bf16[128,512]{1,0:T(8,128)(2,1)S(1)}, u32[]{:S(2)}, u32[]{:S(2)}) collective-permute-start(bf16[128,512]{1,0:T(8,128)(2,1)} %get-tuple-element.302), channel_id=1, source_target_pairs={{0,8},{1,9},{2,10},{3,11},{4,12},{5,13},{6,14},{7,15},{8,0},{9,1},... | collective-permute-start | bytes 393224 | tf_op jit(solution)/shard_map/ppermute | solution.py:73
  297.3 47.5 %collective-permute-start.42 = (bf16[544,1152]{1,0:T(8,128)(2,1)}, bf16[544,1152]{1,0:T(8,128)(2,1)S(1)}, u32[]{:S(2)}, u32[]{:S(2)}) collective-permute-start(bf16[544,1152]{1,0:T(8,128)(2,1)} %add_convert_fusion.1), channel_id=1, source_target_pairs={{0,2},{1,3},{2,0},{3,1},{4,6},{5,7},{6,4},{7,5},{8,10},{9,11},{10,... | collective-permute-start | bytes 3760136 | tf_op jit(solution)/shard_map/ppermute | solution.py:73
  298.2 46.6 %collective-permute-start.41 = (bf16[288,640]{1,0:T(8,128)(2,1)}, bf16[288,640]{1,0:T(8,128)(2,1)}, u32[]{:S(2)}, u32[]{:S(2)}) collective-permute-start(bf16[288,640]{1,0:T(8,128)(2,1)} %add_convert_fusion.3), channel_id=1, source_target_pairs={{0,2},{1,3},{2,0},{3,1},{4,6},{5,7},{6,4},{7,5},{8,10},{9,11},{10,... | collective-permute-start | bytes 1105928 | tf_op jit(solution)/shard_map/ppermute | solution.py:73
  349.9 29.0 %collective-permute-start.43 = (bf16[2,288,512]{2,1,0:T(8,128)(2,1)}, bf16[2,288,512]{2,1,0:T(8,128)(2,1)S(1)}, u32[]{:S(2)}, u32[]{:S(2)}) collective-permute-start(bf16[2,288,512]{2,1,0:T(8,128)(2,1)} %get-tuple-element.248), channel_id=1, source_target_pairs={{0,1},{1,0},{2,3},{3,2},{4,5},{5,4},{6,7},{7,6},{8,9},{9,8},{10,11... | collective-permute-start | bytes 1769480 | tf_op jit(solution)/shard_map/ppermute | solution.py:73
  350.2 29.1 %collective-permute-start.44 = (bf16[2,288,512]{2,1,0:T(8,128)(2,1)}, bf16[2,288,512]{2,1,0:T(8,128)(2,1)S(1)}, u32[]{:S(2)}, u32[]{:S(2)}) collective-permute-start(bf16[2,288,512]{2,1,0:T(8,128)(2,1)} %get-tuple-element.249), channel_id=1, source_target_pairs={{0,2},{1,3},{2,0},{3,1},{4,6},{5,7},{6,4},{7,5},{8,10},{9,11},{10,... | collective-permute-start | bytes 1769480 | tf_op jit(solution)/shard_map/ppermute | solution.py:73
  350.4 28.8 %collective-permute-start.45 = (bf16[2,288,512]{2,1,0:T(8,128)(2,1)S(1)}, bf16[2,288,512]{2,1,0:T(8,128)(2,1)S(1)}, u32[]{:S(2)}, u32[]{:S(2)}) collective-permute-start(bf16[2,288,512]{2,1,0:T(8,128)(2,1)S(1)} %copy-done.76), channel_id=1, source_target_pairs={{0,3},{1,2},{2,1},{3,0},{4,7},{5,6},{6,5},{7,4},{8,11},{9,10},{10,... | collective-permute-start | bytes 1769480 | tf_op jit(solution)/shard_map/ppermute | solution.py:73
  377.1 54.0 %collective-permute-start.46 = (bf16[2,288,256]{2,1,0:T(8,128)(2,1)}, bf16[2,288,256]{2,1,0:T(8,128)(2,1)S(1)}, u32[]{:S(2)}, u32[]{:S(2)}) collective-permute-start(bf16[2,288,256]{2,1,0:T(8,128)(2,1)} %get-tuple-element.259), channel_id=1, source_target_pairs={{0,2},{1,3},{2,0},{3,1},{4,6},{5,7},{6,4},{7,5},{8,10},{9,11},{10,... | collective-permute-start | bytes 884744 | tf_op jit(solution)/shard_map/ppermute | solution.py:73
  377.4 54.9 %collective-permute-start.47 = (bf16[2,288,256]{2,1,0:T(8,128)(2,1)}, bf16[2,288,256]{2,1,0:T(8,128)(2,1)}, u32[]{:S(2)}, u32[]{:S(2)}) collective-permute-start(bf16[2,288,256]{2,1,0:T(8,128)(2,1)} %get-tuple-element.260), channel_id=1, source_target_pairs={{0,3},{1,2},{2,1},{3,0},{4,7},{5,6},{6,5},{7,4},{8,11},{9,10},{10,... | collective-permute-start | bytes 884744 | tf_op jit(solution)/shard_map/ppermute | solution.py:73
  378.9 82.8 %collective-permute-start.50 = (bf16[2,288,256]{2,1,0:T(8,128)(2,1)}, bf16[2,288,256]{2,1,0:T(8,128)(2,1)}, u32[]{:S(2)}, u32[]{:S(2)}) collective-permute-start(bf16[2,288,256]{2,1,0:T(8,128)(2,1)} %get-tuple-element.266), channel_id=1, source_target_pairs={{0,1},{1,0},{2,3},{3,2},{4,5},{5,4},{6,7},{7,6},{8,9},{9,8},{10,11... | collective-permute-start | bytes 884744 | tf_op jit(solution)/shard_map/ppermute | solution.py:73
  381.4 51.3 %collective-permute-start.48 = (bf16[2304,384]{1,0:T(8,128)(2,1)}, bf16[2304,384]{1,0:T(8,128)(2,1)S(1)}, u32[]{:S(2)}, u32[]{:S(2)}) collective-permute-start(bf16[2304,384]{1,0:T(8,128)(2,1)} %pad_maximum_fusion.1.refs_0_), channel_id=1, source_target_pairs={{0,4},{1,5},{2,6},{3,7},{4,0},{5,1},{6,2},{7,3},{8,12},{9,13},{10,... | collective-permute-start | bytes 5308424 | tf_op jit(solution)/shard_map/ppermute | solution.py:73
  383.3 55.1 %collective-permute-start.49 = (bf16[2304,384]{1,0:T(8,128)(2,1)}, bf16[2304,384]{1,0:T(8,128)(2,1)S(1)}, u32[]{:S(2)}, u32[]{:S(2)}) collective-permute-start(bf16[2304,384]{1,0:T(8,128)(2,1)} %pad_maximum_fusion.2.refs_2_), channel_id=1, source_target_pairs={{0,8},{1,9},{2,10},{3,11},{4,12},{5,13},{6,14},{7,15},{8,0},{9,1},... | collective-permute-start | bytes 5308424 | tf_op jit(solution)/shard_map/ppermute | solution.py:73
  431.9 29.9 %collective-permute-start.51 = (bf16[2,288,512]{2,1,0:T(8,128)(2,1)}, bf16[2,288,512]{2,1,0:T(8,128)(2,1)}, u32[]{:S(2)}, u32[]{:S(2)}) collective-permute-start(bf16[2,288,512]{2,1,0:T(8,128)(2,1)} %get-tuple-element.270), channel_id=1, source_target_pairs={{0,1},{1,0},{2,3},{3,2},{4,5},{5,4},{6,7},{7,6},{8,9},{9,8},{10,11... | collective-permute-start | bytes 1769480 | tf_op jit(solution)/shard_map/ppermute | solution.py:73
  432.3 29.4 %collective-permute-start.52 = (bf16[2,288,512]{2,1,0:T(8,128)(2,1)}, bf16[2,288,512]{2,1,0:T(8,128)(2,1)}, u32[]{:S(2)}, u32[]{:S(2)}) collective-permute-start(bf16[2,288,512]{2,1,0:T(8,128)(2,1)} %get-tuple-element.271), channel_id=1, source_target_pairs={{0,2},{1,3},{2,0},{3,1},{4,6},{5,7},{6,4},{7,5},{8,10},{9,11},{10,... | collective-permute-start | bytes 1769480 | tf_op jit(solution)/shard_map/ppermute | solution.py:73
  432.7 29.1 %collective-permute-start.53 = (bf16[2,288,512]{2,1,0:T(8,128)(2,1)}, bf16[2,288,512]{2,1,0:T(8,128)(2,1)}, u32[]{:S(2)}, u32[]{:S(2)}) collective-permute-start(bf16[2,288,512]{2,1,0:T(8,128)(2,1)} %get-tuple-element.272), channel_id=1, source_target_pairs={{0,3},{1,2},{2,1},{3,0},{4,7},{5,6},{6,5},{7,4},{8,11},{9,10},{10,... | collective-permute-start | bytes 1769480 | tf_op jit(solution)/shard_map/ppermute | solution.py:73
  (103 other events, 792.7 us)
Sparse Core Ops, SparseCore 0:
  117.2 88.6 all-gather.2
  209.4 93.7 all-gather.4
  350.0 104.2 all-reduce.2

commit v5 on v4

--- a/solution.py
+++ b/solution.py
@@ -619,7 +619,7 @@
         ),
         out_shape=jax.ShapeDtypeStruct((2, wide // 256, 8 * half, 256), BF),
         input_output_aliases={2 + len(sources): 0} if base else {},
-        compiler_params=pltpu.CompilerParams(vmem_limit_bytes=VMEM_ALL),
+        compiler_params=pltpu.CompilerParams(vmem_limit_bytes=VMEM_LIMIT),
         name="lay",
     )(sides, rows, *sources, *base)
 
@@ -863,7 +863,7 @@
         + [jax.ShapeDtypeStruct((half, model), F32), jax.ShapeDtypeStruct((half, model), BF)],
         scratch_shapes=[pltpu.VMEM((2 * half, width), BF)] * (1 if forward else 2)
         + [pltpu.VMEM((2 * half, model), F32)],
-        compiler_params=pltpu.CompilerParams(vmem_limit_bytes=VMEM_ALL),
+        compiler_params=pltpu.CompilerParams(vmem_limit_bytes=24 * 2**20),
         cost_estimate=pl.CostEstimate(
             flops=12 * half * model * wide,
             bytes_accessed=6 * model * wide + 16 * half * wide,
@@ -1167,7 +1167,7 @@
     rest = lax.psum(join(early, tail).astype(BF), "ctx")
     shared_flow = Flow(exchange_results(pieces, down))
     ranges, grad_down = [], None
-    for first, last in ((4, 5), (5, count)):
+    for first, last in ((4, 5), (5, 6), (6, count)):
         *pieces, grad_down = ffn_gradients(
             jnp.stack([mine, *[jnp.int32(i) for i in range(first, last)]]),
             *both,
@@ -1178,16 +1178,17 @@
             grad_down,
             False,
         )
-        over_x = [sent[2:] for sent in ranges]
-        both, grad_down, over_x = pace((both, grad_down, over_x), shared_flow)
-        for sent, arrays in zip(ranges, over_x):
-            sent[2:] = arrays
+        flying = [sent[1:] for sent in ranges]
+        flows = () if first == 5 else (shared_flow,)
+        both, grad_down, flying = pace((both, grad_down, flying), *flows)
+        for sent, arrays in zip(ranges, flying):
+            sent[1:] = arrays
         ranges.append([pieces[0]] + [swap(pieces[o], o) for o in (1, 2, 3)])
     shared = shared_flow.result
     grad_down = fill_rows(block_info, part, count, shared, grad_down)
-    rest, grad_down = pace((rest, grad_down))
+    grad_in = unfold(block_info, part, shared, ranges)
+    rest, grad_down, grad_in = pace((rest, grad_down, grad_in))
     early, tail = rest[:early_rows], rest[early_rows:]
-    grad_in = unfold(block_info, part, shared, ranges)
     early, tail = early.astype(F32), tail.astype(F32)
     grad_query = early[:quarter, : H * HD]
     grad_out = early[quarter:]

time: 490 us -> 483 us (0.986)
  Pallas kernels: 203 us -> 192 us
  local copies, waits for them, and re-layouts: 51.5 us -> 61.9 us
  other arithmetic: 29.3 us -> 24.2 us
    unnamed x168 -> x190, local copies, waits for them, and re-layouts: 33.8 us -> 48.6 us
    all_gather x1, waiting for transfers between devices: 3.52 us -> 14.9 us  [body(): d_ffn_all = lax.all_gather(d_ffn_low, AXES, axis=0, tiled=True)]
    psum x1, waiting for transfers between devices: 9.61 us -> 0.01 us  [body(): rest = lax.psum(join(early, tail).astype(BF), 'ctx')]
    pallas_call x2, Pallas kernels: 13.5 us -> 5.04 us  [lay(): pl.pallas_call(functools.partial(lay_kernel, counts), grid_spec=pltpu.Pre...]
    pallas_call x2, Pallas kernels: 28 us -> 20 us  [ffn_group(): pl.pallas_call(kernel, grid=(wide // width,), in_specs=[rows, rows] + [co...]
    pallas_call x3 -> x4, Pallas kernels: 110 us -> 116 us  [ffn_gradients(): pl.pallas_call(functools.partial(ffn_gradients_kernel, part, apart, down_...]
    ppermute x54 -> x57, waiting for transfers between devices: 113 us -> 109 us  [swap(): return lax.ppermute(value, AXES, [(i, i ^ offset) for i in range(count)])]
    ppermute x54 -> x57, starting transfers between devices: 54.9 us -> 56.3 us  [swap(): return lax.ppermute(value, AXES, [(i, i ^ offset) for i in range(count)])]
  transfers between devices with their start and end apart: 57 -> 60, of which waited for: 26 -> 24; matrix products, arithmetic and copies ran while one was open for 10% -> 7% of each run, Pallas kernels for 39% -> 40%
where the time goes in v5:
time: 483 us; the launch traced here: 474 us
  Pallas kernels  192 us (40%)
  waiting for transfers between devices  123 us (25%)
  local copies, waits for them, and re-layouts  61.9 us (13%)
  starting transfers between devices  56.6 us (12%)
  other arithmetic  24.2 us (5%)
  between operations  15.4 us (3%)
    pallas_call x4, Pallas kernels, ffn_gradients(): pl.pallas_call(functools.partial(ffn_gradients_kernel, part, apart, down_...  116 us
    ppermute x57, waiting for transfers between devices, swap(): return lax.ppermute(value, AXES, [(i, i ^ offset) for i in range(count)])  109 us
    ppermute x57, starting transfers between devices, swap(): return lax.ppermute(value, AXES, [(i, i ^ offset) for i in range(count)])  56.3 us
    unnamed x190, local copies, waits for them, and re-layouts  48.6 us
    pallas_call x2, Pallas kernels, ffn_group(): pl.pallas_call(kernel, grid=(wide // width,), in_specs=[rows, rows] + [co...  20 us
    all_gather x1, waiting for transfers between devices, body(): d_ffn_all = lax.all_gather(d_ffn_low, AXES, axis=0, tiled=True)  14.9 us
    pallas_call x9, Pallas kernels, kernel_call(): pl.pallas_call(kernel, out_shape=[jax.ShapeDtypeStruct(shape, dtype) for...  11.1 us
    pallas_call x1, Pallas kernels, unfold(): pl.pallas_call(functools.partial(unfold_kernel, part), grid_spec=pltpu.Pr...  10.5 us
  transfers between devices with their start and end apart: 60, of which 24 were waited for; matrix products, arithmetic and copies ran while one was open for 7% of the time, Pallas kernels for 40%

profile of v5, /device:TPU:1, one launch (start us, length us, event | category | flops | bytes accessed | tf_op | source)
XLA Modules:
  0.0 473.7 jit_solution(822201754289403270)
XLA Ops:
  17.7 5.9 %carve_quarters.1 = (bf16[1,144,1792]{2,1,0:T(8,128)(2,1)}, bf16[1,144,1792]{2,1,0:T(8,128)(2,1)}) custom-call(s32[3]{0:T(128)} %pad_add_fusion.1.place, bf16[288,2,6912]{2,1,0:T(2,128)(2,1)} %w.1), custom_call_target="tpu_custom_call" | custom-call | tf_op jit(solution)/shard_map/carve_quarters/pallas_call | solution.py:531
  36.6 4.0 copy.45
  43.2 8.1 %collective-permute-done.6.refs_5_ = bf16[1,144,1792]{2,1,0:T(8,128)(2,1)} collective-permute-done((bf16[1,144,1792]{2,1,0:T(8,128)(2,1)}, bf16[1,144,1792]{2,1,0:T(8,128)(2,1)}, u32[]{:S(2)}, u32[]{:S(2)}) %collective-permute-start.6) | collective-permute-done | bytes 516128 | tf_op jit(solution)/shard_map/ppermute | solution.py:73
  59.4 10.3 %collective-permute-done.9.refs_3_ = bf16[1,144,1792]{2,1,0:T(8,128)(2,1)S(1)} collective-permute-done((bf16[1,144,1792]{2,1,0:T(8,128)(2,1)}, bf16[1,144,1792]{2,1,0:T(8,128)(2,1)S(1)}, u32[]{:S(2)}, u32[]{:S(2)}) %collective-permute-start.9) | collective-permute-done | bytes 516128 | tf_op jit(solution)/shard_map/ppermute | solution.py:73
  74.5 7.2 %collective-permute-done.13.refs_7_ = bf16[1,144,1792]{2,1,0:T(8,128)(2,1)S(1)} collective-permute-done((bf16[1,144,1792]{2,1,0:T(8,128)(2,1)}, bf16[1,144,1792]{2,1,0:T(8,128)(2,1)S(1)}, u32[]{:S(2)}, u32[]{:S(2)}) %collective-permute-start.13) | collective-permute-done | bytes 516128 | tf_op jit(solution)/shard_map/ppermute | solution.py:73
  83.2 5.6 %collective-permute-done.11 = bf16[256,512]{1,0:T(8,128)(2,1)S(1)} collective-permute-done((bf16[256,512]{1,0:T(8,128)(2,1)S(1)}, bf16[256,512]{1,0:T(8,128)(2,1)S(1)}, u32[]{:S(2)}, u32[]{:S(2)}) %collective-permute-start.11) | collective-permute-done | bytes 262176 | tf_op jit(solution)/shard_map/ppermute | solution.py:73
  93.0 3.5 collective-permute-done.16.refs_1_
  98.8 7.2 %attend.1 = (bf16[2048,512]{1,0:T(8,128)(2,1)S(1)}, bf16[2048,512]{1,0:T(8,128)(2,1)S(1)}, f32[256,512]{1,0:T(8,128)S(1)}, f32[1,512]{1,0:T(1,128)S(1)}) custom-call(s32[64]{0:T(128)S(1)} %select_reduce_fusion.blocks, bf16[512,256]{1,0:T(8,128)(2,1)S(1)} %get-tuple-element.185.q, s32[1,512]{1,0:T(1,128)S(1)} %bitcast.41, s32[1,512]{1,0:T(1,128)S(1)} %bitcast.42, ...), custom_call_target="tpu_custom_call" | custom-call | flops 2147483648 | bytes 8388608 | tf_op jit(solution)/shard_map/attend/pallas_call | solution.py:275
  128.3 4.0 lay.2.refs_1_
  137.3 10.1 %ffn_forward.1 = (bf16[512,1792]{1,0:T(8,128)(2,1)S(1)}, bf16[512,1792]{1,0:T(8,128)(2,1)S(1)}, f32[256,1152]{1,0:T(8,128)S(1)}, bf16[256,1152]{1,0:T(8,128)(2,1)S(1)}) custom-call(bf16[256,1152]{1,0:T(8,128)(2,1)S(1)} %constant_dynamic-update-slice_fusion.16.near, bf16[256,1152]{1,0:T(8,128)(2,1)S(1)} %collective-permute-done.24.far, ...), custom_call_target="tpu_custom_call" | custom-call | flops 6341787648 | bytes 19726336 | tf_op jit(solution)/shard_map/ffn_forward/pallas_call | solution.py:851
  153.2 9.1 %collective-permute-done.26.other = bf16[128,1152]{1,0:T(8,128)(2,1)S(1)} collective-permute-done((bf16[128,1152]{1,0:T(8,128)(2,1)S(1)}, bf16[128,1152]{1,0:T(8,128)(2,1)S(1)}, u32[]{:S(2)}, u32[]{:S(2)}) %collective-permute-start.26) | collective-permute-done | bytes 294944 | tf_op jit(solution)/shard_map/ppermute | solution.py:73
  165.3 8.4 %collective-permute-done.27 = bf16[128,1152]{1,0:T(8,128)(2,1)S(1)} collective-permute-done((bf16[128,1152]{1,0:T(8,128)(2,1)}, bf16[128,1152]{1,0:T(8,128)(2,1)S(1)}, u32[]{:S(2)}, u32[]{:S(2)}) %collective-permute-start.27) | collective-permute-done | bytes 294944 | tf_op jit(solution)/shard_map/ppermute | solution.py:73
  173.7 3.4 collective-permute-start.28
  178.8 3.3 copy-done.1
  187.4 9.9 %ffn_backward.1 = (f32[256,1152]{1,0:T(8,128)S(1)}, bf16[256,1152]{1,0:T(8,128)(2,1)S(1)}) custom-call(bf16[256,1152]{1,0:T(8,128)(2,1)S(1)} %constant_dynamic-update-slice_fusion.18.near, bf16[256,1152]{1,0:T(8,128)(2,1)S(1)} %collective-permute-done.28.far, bf16[512,1792]{1,0:T(8,128)(2,1)S(1)} %copy-done.24, bf16[512,1792]{1,0:T(8,128)(2,1)S(1)} %copy-done.26, ...), custom_call_target="tpu_custom_call" | custom-call | flops 6341787648 | bytes 19726336 | tf_op jit(solution)/shard_map/ffn_backward/pallas_call | solution.py:851
  200.1 8.2 %collective-permute-done.30.other = bf16[128,1152]{1,0:T(8,128)(2,1)S(1)} collective-permute-done((bf16[128,1152]{1,0:T(8,128)(2,1)S(1)}, bf16[128,1152]{1,0:T(8,128)(2,1)S(1)}, u32[]{:S(2)}, u32[]{:S(2)}) %collective-permute-start.30) | collective-permute-done | bytes 294944 | tf_op jit(solution)/shard_map/ppermute | solution.py:73
  210.8 7.0 %attend_back.1 = (f32[256,512]{1,0:T(8,128)S(1)}, bf16[2048,512]{1,0:T(8,128)(2,1)S(1)}, bf16[2048,512]{1,0:T(8,128)(2,1)S(1)}) custom-call(bf16[512,256]{1,0:T(8,128)(2,1)S(1)} %copy-done.59, bf16[512,256]{1,0:T(8,128)(2,1)S(1)} %get-tuple-element.219.d_heads, f32[1,512]{1,0:T(1,128)S(1)} %get-tuple-element.196.mass, f32[1,512]{1,0:T(1,128)S(1)} %get-tuple-element.220.dots, ...), custom_call_target="tpu_custom_call" | custom-call | flops 4294967296 | bytes 12582912 | tf_op jit(solution)/shard_map/attend_back/pallas_call | solution.py:389
  219.1 2.9 query_back.1
  226.1 6.4 %collective-permute-done.32 = bf16[256,512]{1,0:T(8,128)(2,1)S(1)} collective-permute-done((bf16[256,512]{1,0:T(8,128)(2,1)S(1)}, bf16[256,512]{1,0:T(8,128)(2,1)S(1)}, u32[]{:S(2)}, u32[]{:S(2)}) %collective-permute-start.32) | collective-permute-done | bytes 262176 | tf_op jit(solution)/shard_map/ppermute | solution.py:73
  235.3 15.0 %collective-permute-done.34 = bf16[512,512]{1,0:T(8,128)(2,1)S(1)} collective-permute-done((bf16[512,512]{1,0:T(8,128)(2,1)S(1)}, bf16[512,512]{1,0:T(8,128)(2,1)S(1)}, u32[]{:S(2)}, u32[]{:S(2)}) %collective-permute-start.34) | collective-permute-done | bytes 524320 | tf_op jit(solution)/shard_map/ppermute | solution.py:73
  250.2 4.0 collective-permute-done.35
  263.3 6.0 %collective-permute-done.39.refs_2_ = bf16[128,512]{1,0:T(8,128)(2,1)S(1)} collective-permute-done((bf16[128,512]{1,0:T(8,128)(2,1)}, bf16[128,512]{1,0:T(8,128)(2,1)S(1)}, u32[]{:S(2)}, u32[]{:S(2)}) %collective-permute-start.39) | collective-permute-done | bytes 131104 | tf_op jit(solution)/shard_map/ppermute | solution.py:73
  272.4 7.1 %collective-permute-start.40 = (bf16[576,640]{1,0:T(8,128)(2,1)S(1)}, bf16[576,640]{1,0:T(8,128)(2,1)S(1)}, u32[]{:S(2)}, u32[]{:S(2)}) collective-permute-start(bf16[576,640]{1,0:T(8,128)(2,1)S(1)} %get-tuple-element.257), channel_id=1, source_target_pairs={{0,1},{1,0},{2,3},{3,2},{4,5},{5,4},{6,7},{7,6},{8,9},{9,8},{10,11... | collective-permute-start | bytes 2211848 | tf_op jit(solution)/shard_map/ppermute | solution.py:73
  280.1 3.0 add_convert_fusion.1
  285.4 14.9 %all-gather.5.cloned.1.call-done.d_ffn = bf16[4096,1152]{1,0:T(8,128)(2,1)} async-done(((bf16[128,1152]{1,0:T(8,128)(2,1)}), bf16[4096,1152]{1,0:T(8,128)(2,1)}) %all-gather.5.cloned.1.call-update) | async-done | bytes 9437200 | tf_op jit(solution)/shard_map/all_gather | solution.py:1071
  300.3 41.8 %ffn_gradients.4 = (bf16[2,288,512]{2,1,0:T(8,128)(2,1)}, bf16[2,288,512]{2,1,0:T(8,128)(2,1)}, bf16[2,288,512]{2,1,0:T(8,128)(2,1)}, bf16[2,288,512]{2,1,0:T(8,128)(2,1)}, bf16[9,512,128]{2,1,0:T(8,128)(2,1)}) custom-call(s32[3]{0:T(128)} %gather_fusion, bf16[4096,1152]{1,0:T(8,128)(2,1)} %all-gather.3.cloned.1.call-done.second, ...), custom_call_target="tpu_custom_call" | custom-call | flops 28991029248 | bytes 37748736 | tf_op jit(solution)/shard_map/ffn_gradients/pallas_call | solution.py:753
  349.4 25.1 %ffn_gradients.5 = (bf16[2,288,256]{2,1,0:T(8,128)(2,1)}, bf16[2,288,256]{2,1,0:T(8,128)(2,1)}, bf16[2,288,256]{2,1,0:T(8,128)(2,1)}, bf16[2,288,256]{2,1,0:T(8,128)(2,1)}, f32[1728,1152]{1,0:T(8,128)}) custom-call(s32[2]{0:T(128)} %get-tuple-element.349.info, bf16[4096,1152]{1,0:T(8,128)(2,1)} %all-gather.3.cloned.1.call-done.second, ...), custom_call_target="tpu_custom_call" | custom-call | flops 14495514624 | bytes 18874368 | tf_op jit(solution)/shard_map/ffn_gradients/pallas_call | solution.py:753
  381.4 24.6 %ffn_gradients.6 = (bf16[2,288,256]{2,1,0:T(8,128)(2,1)}, bf16[2,288,256]{2,1,0:T(8,128)(2,1)}, bf16[2,288,256]{2,1,0:T(8,128)(2,1)}, bf16[2,288,256]{2,1,0:T(8,128)(2,1)}, f32[1728,1152]{1,0:T(8,128)}) custom-call(s32[2]{0:T(128)} %get-tuple-element.350.info, ...), custom_call_target="tpu_custom_call", output_to_operand_aliasing={{4}: (6, {})} | custom-call | flops 14495514624 | bytes 18874368 | tf_op jit(solution)/shard_map/ffn_gradients/pallas_call | solution.py:753
  408.3 24.6 %ffn_gradients.7 = (bf16[2,288,256]{2,1,0:T(8,128)(2,1)}, bf16[2,288,256]{2,1,0:T(8,128)(2,1)}, bf16[2,288,256]{2,1,0:T(8,128)(2,1)}, bf16[2,288,256]{2,1,0:T(8,128)(2,1)}, f32[1728,1152]{1,0:T(8,128)}) custom-call(s32[2]{0:T(128)} %pad_add_fusion.4.info, bf16[4096,1152]{1,0:T(8,128)(2,1)} %all-gather.3.cloned.1.call-done.second, ...), custom_call_target="tpu_custom_call", output_to_operand_aliasing={{4}: (6, {})} | custom-call | flops 14495514624 | bytes 18874368 | tf_op jit(solution)/shard_map/ffn_gradients/pallas_call | solution.py:753
  437.1 6.4 %fill_rows.1 = f32[1728,1152]{1,0:T(8,128)} custom-call(s32[5]{0:T(128)S(1)} %stack.113.info, bf16[2304,384]{1,0:T(8,128)(2,1)} %pad_maximum_fusion.1.refs_0_, bf16[2304,384]{1,0:T(8,128)(2,1)S(1)} %collective-permute-done.52.refs_1_, bf16[2304,384]{1,0:T(8,128)(2,1)} %pad_maximum_fusion.2.refs_2_, ...), custom_call_target="tpu_custom_call", output_to_operand_aliasing={{}: (5, {})} | custom-call | tf_op jit(solution)/shard_map/fill_rows/pallas_call | solution.py:682
  443.5 5.3 %collective-permute-done.56.refs_15_ = bf16[2,288,256]{2,1,0:T(8,128)(2,1)S(1)} collective-permute-done((bf16[2,288,256]{2,1,0:T(8,128)(2,1)}, bf16[2,288,256]{2,1,0:T(8,128)(2,1)S(1)}, u32[]{:S(2)}, u32[]{:S(2)}) %collective-permute-start.56) | collective-permute-done | bytes 294944 | tf_op jit(solution)/shard_map/ppermute | solution.py:73
  448.8 10.5 %unfold.1 = f32[288,2,6912]{2,1,0:T(2,128)} custom-call(s32[5]{0:T(128)S(1)} %stack.113.info, bf16[4,2,288,384]{3,2,1,0:T(8,128)(2,1)S(1)} %pad_maximum_fusion.3.refs_0_, bf16[4,2,288,384]{3,2,1,0:T(8,128)(2,1)S(1)} %bitcast.39, bf16[4,2,288,384]{3,2,1,0:T(8,128)(2,1)S(1)} %pad_maximum_fusion.4.refs_2_, bf16[4,2,288,384]{3,2,1,0:T(8,128)(2,1)S(1)} %bitcast.40, ...), custom_call_target="tpu_custom_call" | custom-call | tf_op jit(solution)/shard_map/unfold/pallas_call | solution.py:905
  (374 shorter events, 145.6 us)
Async XLA Ops:
  7.2 278.2 %all-gather.3.cloned.1.call-start = ((), (), s32[]{:S(2)}) async-start(), calls=%async_computation | async-start | bytes 9732096 | tf_op jit(solution)/shard_map/all_gather | solution.py:1047
  26.3 16.9 %collective-permute-start.5 = (bf16[1,144,1792]{2,1,0:T(8,128)(2,1)}, bf16[1,144,1792]{2,1,0:T(8,128)(2,1)}, u32[]{:S(2)}, u32[]{:S(2)}) collective-permute-start(bf16[1,144,1792]{2,1,0:T(8,128)(2,1)} %get-tuple-element.173), channel_id=1, source_target_pairs={{0,2},{1,3},{2,0},{3,1},{4,6},{5,7},{6,4},{7,5},{8,10},{9,11},{10,... | collective-permute-start | bytes 1548296 | tf_op jit(solution)/shard_map/ppermute | solution.py:73
  26.8 24.4 %collective-permute-start.6 = (bf16[1,144,1792]{2,1,0:T(8,128)(2,1)}, bf16[1,144,1792]{2,1,0:T(8,128)(2,1)}, u32[]{:S(2)}, u32[]{:S(2)}) collective-permute-start(bf16[1,144,1792]{2,1,0:T(8,128)(2,1)} %get-tuple-element.174), channel_id=1, source_target_pairs={{0,3},{1,2},{2,1},{3,0},{4,7},{5,6},{6,5},{7,4},{8,11},{9,10},{10,... | collective-permute-start | bytes 1548296 | tf_op jit(solution)/shard_map/ppermute | solution.py:73
  30.0 21.2 %collective-permute-start.2 = (bf16[128,512]{1,0:T(8,128)(2,1)}, bf16[128,512]{1,0:T(8,128)(2,1)}, u32[]{:S(2)}, u32[]{:S(2)}) collective-permute-start(bf16[128,512]{1,0:T(8,128)(2,1)} %get-tuple-element.172), channel_id=1, source_target_pairs={{0,8},{1,9},{2,10},{3,11},{4,12},{5,13},{6,14},{7,15},{8,0},{9,1},... | collective-permute-start | bytes 393224 | tf_op jit(solution)/shard_map/ppermute | solution.py:73
  31.3 19.9 %collective-permute-start.3 = (bf16[128,512]{1,0:T(8,128)(2,1)}, bf16[128,512]{1,0:T(8,128)(2,1)}, u32[]{:S(2)}, u32[]{:S(2)}) collective-permute-start(bf16[128,512]{1,0:T(8,128)(2,1)} %get-tuple-element.172), channel_id=1, source_target_pairs={{0,16},{1,17},{2,18},{3,19},{4,20},{5,21},{6,22},{7,23},{8,24},{9,... | collective-permute-start | bytes 393224 | tf_op jit(solution)/shard_map/ppermute | solution.py:73
  33.6 17.6 %collective-permute-start.4 = (bf16[128,512]{1,0:T(8,128)(2,1)}, bf16[128,512]{1,0:T(8,128)(2,1)}, u32[]{:S(2)}, u32[]{:S(2)}) collective-permute-start(bf16[128,512]{1,0:T(8,128)(2,1)} %get-tuple-element.172), channel_id=1, source_target_pairs={{0,24},{1,25},{2,26},{3,27},{4,28},{5,29},{6,30},{7,31},{8,16},{9,... | collective-permute-start | bytes 393224 | tf_op jit(solution)/shard_map/ppermute | solution.py:73
  51.2 19.9 %collective-permute-start.10 = (bf16[2,288,1792]{2,1,0:T(8,128)(2,1)S(1)}, bf16[2,288,1792]{2,1,0:T(8,128)(2,1)S(1)}, u32[]{:S(2)}, u32[]{:S(2)}) collective-permute-start(bf16[2,288,1792]{2,1,0:T(8,128)(2,1)S(1)} %get-tuple-element.180), channel_id=1, source_target_pairs={{0,1},{1,0},{2,3},{3,2},{4,5},{5,4},{6,7},{7,6},{8,9},{9,8},{10,11... | collective-permute-start | bytes 6193160 | tf_op jit(solution)/shard_map/ppermute | solution.py:73
  55.3 15.6 %collective-permute-start.7 = (bf16[512,512]{1,0:T(8,128)(2,1)S(1)}, bf16[512,512]{1,0:T(8,128)(2,1)S(1)}, u32[]{:S(2)}, u32[]{:S(2)}) collective-permute-start(bf16[512,512]{1,0:T(8,128)(2,1)S(1)} %get-tuple-element.336), channel_id=1, source_target_pairs={{0,4},{1,5},{2,6},{3,7},{4,0},{5,1},{6,2},{7,3},{8,12},{9,13},{10,... | collective-permute-start | bytes 1572872 | tf_op jit(solution)/shard_map/ppermute | solution.py:73
  58.3 24.8 %collective-permute-start.15 = (bf16[288,1024]{1,0:T(8,128)(2,1)S(1)}, bf16[288,1024]{1,0:T(8,128)(2,1)S(1)}, u32[]{:S(2)}, u32[]{:S(2)}) collective-permute-start(bf16[288,1024]{1,0:T(8,128)(2,1)S(1)} %copy-done.83), channel_id=1, source_target_pairs={{0,2},{1,3},{2,0},{3,1},{4,6},{5,7},{6,4},{7,5},{8,10},{9,11},{10,... | collective-permute-start | bytes 1769480 | tf_op jit(solution)/shard_map/ppermute | solution.py:73
  72.6 16.3 %collective-permute-start.11 = (bf16[256,512]{1,0:T(8,128)(2,1)S(1)}, bf16[256,512]{1,0:T(8,128)(2,1)S(1)}, u32[]{:S(2)}, u32[]{:S(2)}) collective-permute-start(bf16[256,512]{1,0:T(8,128)(2,1)S(1)} %slice.147), channel_id=1, source_target_pairs={{0,2},{1,3},{2,0},{3,1},{4,6},{5,7},{6,4},{7,5},{8,10},{9,11},{10,... | collective-permute-start | bytes 786440 | tf_op jit(solution)/shard_map/ppermute | solution.py:73
  73.1 15.7 %collective-permute-start.12 = (bf16[256,512]{1,0:T(8,128)(2,1)S(1)}, bf16[256,512]{1,0:T(8,128)(2,1)S(1)}, u32[]{:S(2)}, u32[]{:S(2)}) collective-permute-start(bf16[256,512]{1,0:T(8,128)(2,1)S(1)} %slice.148), channel_id=1, source_target_pairs={{0,4},{1,5},{2,6},{3,7},{4,0},{5,1},{6,2},{7,3},{8,12},{9,13},{10,... | collective-permute-start | bytes 786440 | tf_op jit(solution)/shard_map/ppermute | solution.py:73
  91.2 16.1 %collective-permute-start.19 = (bf16[1,144,1792]{2,1,0:T(8,128)(2,1)S(1)}, bf16[1,144,1792]{2,1,0:T(8,128)(2,1)S(1)}, u32[]{:S(2)}, u32[]{:S(2)}) collective-permute-start(bf16[1,144,1792]{2,1,0:T(8,128)(2,1)S(1)} %collective-permute-done.9.refs_3_), channel_id=1, source_target_pairs={{0,4},{1,5},{2,6},{3,7},{4,0},{5,1},{6,2},{7,3},{8,12},{9,13},{10,... | collective-permute-start | bytes 1548296 | tf_op jit(solution)/shard_map/ppermute | solution.py:73
  117.7 182.6 %all-gather.5.cloned.1.call-start = ((), (), s32[]{:S(2)}) async-start(), calls=%async_computation.1 | async-start | bytes 9732096 | tf_op jit(solution)/shard_map/all_gather | solution.py:1071
  117.9 15.4 %collective-permute-start.23 = (bf16[1,144,1792]{2,1,0:T(8,128)(2,1)}, bf16[1,144,1792]{2,1,0:T(8,128)(2,1)}, u32[]{:S(2)}, u32[]{:S(2)}) collective-permute-start(bf16[1,144,1792]{2,1,0:T(8,128)(2,1)} %collective-permute-done.5.refs_2_), channel_id=1, source_target_pairs={{0,4},{1,5},{2,6},{3,7},{4,0},{5,1},{6,2},{7,3},{8,12},{9,13},{10,... | collective-permute-start | bytes 1548296 | tf_op jit(solution)/shard_map/ppermute | solution.py:73
  164.2 295.1 %all-reduce.3.cloned.1.call-start = ((), (), s32[]{:S(2)}) async-start(), calls=%async_computation.2 | async-start | bytes 3833856 | tf_op jit(solution)/shard_map/psum | solution.py:1167
  222.9 31.3 %collective-permute-start.36 = (bf16[1088,1152]{1,0:T(8,128)(2,1)S(1)}, bf16[1088,1152]{1,0:T(8,128)(2,1)S(1)}, u32[]{:S(2)}, u32[]{:S(2)}) collective-permute-start(bf16[1088,1152]{1,0:T(8,128)(2,1)S(1)} %get-tuple-element.235), channel_id=1, source_target_pairs={{0,1},{1,0},{2,3},{3,2},{4,5},{5,4},{6,7},{7,6},{8,9},{9,8},{10,11... | collective-permute-start | bytes 7520264 | tf_op jit(solution)/shard_map/ppermute | solution.py:73
  232.7 17.5 %collective-permute-start.34 = (bf16[512,512]{1,0:T(8,128)(2,1)S(1)}, bf16[512,512]{1,0:T(8,128)(2,1)S(1)}, u32[]{:S(2)}, u32[]{:S(2)}) collective-permute-start(bf16[512,512]{1,0:T(8,128)(2,1)S(1)} %pad_maximum_fusion.6), channel_id=1, source_target_pairs={{0,4},{1,5},{2,6},{3,7},{4,0},{5,1},{6,2},{7,3},{8,12},{9,13},{10,... | collective-permute-start | bytes 1572872 | tf_op jit(solution)/shard_map/ppermute | solution.py:73
  234.1 20.1 %collective-permute-start.35 = (bf16[512,512]{1,0:T(8,128)(2,1)S(1)}, bf16[512,512]{1,0:T(8,128)(2,1)S(1)}, u32[]{:S(2)}, u32[]{:S(2)}) collective-permute-start(bf16[512,512]{1,0:T(8,128)(2,1)S(1)} %pad_maximum_fusion.7), channel_id=1, source_target_pairs={{0,2},{1,3},{2,0},{3,1},{4,6},{5,7},{6,4},{7,5},{8,10},{9,11},{10,... | collective-permute-start | bytes 1572872 | tf_op jit(solution)/shard_map/ppermute | solution.py:73
  283.1 59.0 %collective-permute-start.42 = (bf16[544,1152]{1,0:T(8,128)(2,1)}, bf16[544,1152]{1,0:T(8,128)(2,1)S(1)}, u32[]{:S(2)}, u32[]{:S(2)}) collective-permute-start(bf16[544,1152]{1,0:T(8,128)(2,1)} %add_convert_fusion.1), channel_id=1, source_target_pairs={{0,2},{1,3},{2,0},{3,1},{4,6},{5,7},{6,4},{7,5},{8,10},{9,11},{10,... | collective-permute-start | bytes 3760136 | tf_op jit(solution)/shard_map/ppermute | solution.py:73
  284.3 57.8 %collective-permute-start.41 = (bf16[288,640]{1,0:T(8,128)(2,1)}, bf16[288,640]{1,0:T(8,128)(2,1)}, u32[]{:S(2)}, u32[]{:S(2)}) collective-permute-start(bf16[288,640]{1,0:T(8,128)(2,1)} %add_convert_fusion.3), channel_id=1, source_target_pairs={{0,2},{1,3},{2,0},{3,1},{4,6},{5,7},{6,4},{7,5},{8,10},{9,11},{10,... | collective-permute-start | bytes 1105928 | tf_op jit(solution)/shard_map/ppermute | solution.py:73
  347.2 27.9 %collective-permute-start.43 = (bf16[2,288,512]{2,1,0:T(8,128)(2,1)}, bf16[2,288,512]{2,1,0:T(8,128)(2,1)S(1)}, u32[]{:S(2)}, u32[]{:S(2)}) collective-permute-start(bf16[2,288,512]{2,1,0:T(8,128)(2,1)} %get-tuple-element.264), channel_id=1, source_target_pairs={{0,1},{1,0},{2,3},{3,2},{4,5},{5,4},{6,7},{7,6},{8,9},{9,8},{10,11... | collective-permute-start | bytes 1769480 | tf_op jit(solution)/shard_map/ppermute | solution.py:73
  347.5 29.5 %collective-permute-start.44 = (bf16[2,288,512]{2,1,0:T(8,128)(2,1)}, bf16[2,288,512]{2,1,0:T(8,128)(2,1)S(1)}, u32[]{:S(2)}, u32[]{:S(2)}) collective-permute-start(bf16[2,288,512]{2,1,0:T(8,128)(2,1)} %get-tuple-element.265), channel_id=1, source_target_pairs={{0,2},{1,3},{2,0},{3,1},{4,6},{5,7},{6,4},{7,5},{8,10},{9,11},{10,... | collective-permute-start | bytes 1769480 | tf_op jit(solution)/shard_map/ppermute | solution.py:73
  347.8 29.2 %collective-permute-start.45 = (bf16[2,288,512]{2,1,0:T(8,128)(2,1)S(1)}, bf16[2,288,512]{2,1,0:T(8,128)(2,1)S(1)}, u32[]{:S(2)}, u32[]{:S(2)}) collective-permute-start(bf16[2,288,512]{2,1,0:T(8,128)(2,1)S(1)} %copy-done.87), channel_id=1, source_target_pairs={{0,3},{1,2},{2,1},{3,0},{4,7},{5,6},{6,5},{7,4},{8,11},{9,10},{10,... | collective-permute-start | bytes 1769480 | tf_op jit(solution)/shard_map/ppermute | solution.py:73
  374.6 31.5 %collective-permute-start.46 = (bf16[2,288,256]{2,1,0:T(8,128)(2,1)}, bf16[2,288,256]{2,1,0:T(8,128)(2,1)S(1)}, u32[]{:S(2)}, u32[]{:S(2)}) collective-permute-start(bf16[2,288,256]{2,1,0:T(8,128)(2,1)} %get-tuple-element.275), channel_id=1, source_target_pairs={{0,1},{1,0},{2,3},{3,2},{4,5},{5,4},{6,7},{7,6},{8,9},{9,8},{10,11... | collective-permute-start | bytes 884744 | tf_op jit(solution)/shard_map/ppermute | solution.py:73
  374.6 31.4 %collective-permute-start.47 = (bf16[2,288,256]{2,1,0:T(8,128)(2,1)}, bf16[2,288,256]{2,1,0:T(8,128)(2,1)}, u32[]{:S(2)}, u32[]{:S(2)}) collective-permute-start(bf16[2,288,256]{2,1,0:T(8,128)(2,1)} %get-tuple-element.276), channel_id=1, source_target_pairs={{0,2},{1,3},{2,0},{3,1},{4,6},{5,7},{6,4},{7,5},{8,10},{9,11},{10,... | collective-permute-start | bytes 884744 | tf_op jit(solution)/shard_map/ppermute | solution.py:73
  375.1 31.0 %collective-permute-start.48 = (bf16[2,288,256]{2,1,0:T(8,128)(2,1)}, bf16[2,288,256]{2,1,0:T(8,128)(2,1)}, u32[]{:S(2)}, u32[]{:S(2)}) collective-permute-start(bf16[2,288,256]{2,1,0:T(8,128)(2,1)} %get-tuple-element.277), channel_id=1, source_target_pairs={{0,3},{1,2},{2,1},{3,0},{4,7},{5,6},{6,5},{7,4},{8,11},{9,10},{10,... | collective-permute-start | bytes 884744 | tf_op jit(solution)/shard_map/ppermute | solution.py:73
  378.9 58.1 %collective-permute-start.52 = (bf16[2304,384]{1,0:T(8,128)(2,1)}, bf16[2304,384]{1,0:T(8,128)(2,1)S(1)}, u32[]{:S(2)}, u32[]{:S(2)}) collective-permute-start(bf16[2304,384]{1,0:T(8,128)(2,1)} %pad_maximum_fusion.1.refs_0_), channel_id=1, source_target_pairs={{0,4},{1,5},{2,6},{3,7},{4,0},{5,1},{6,2},{7,3},{8,12},{9,13},{10,... | collective-permute-start | bytes 5308424 | tf_op jit(solution)/shard_map/ppermute | solution.py:73
  381.4 55.6 %collective-permute-start.53 = (bf16[2304,384]{1,0:T(8,128)(2,1)}, bf16[2304,384]{1,0:T(8,128)(2,1)S(1)}, u32[]{:S(2)}, u32[]{:S(2)}) collective-permute-start(bf16[2304,384]{1,0:T(8,128)(2,1)} %pad_maximum_fusion.2.refs_2_), channel_id=1, source_target_pairs={{0,8},{1,9},{2,10},{3,11},{4,12},{5,13},{6,14},{7,15},{8,0},{9,1},... | collective-permute-start | bytes 5308424 | tf_op jit(solution)/shard_map/ppermute | solution.py:73
  406.1 26.9 %collective-permute-start.49 = (bf16[2,288,256]{2,1,0:T(8,128)(2,1)}, bf16[2,288,256]{2,1,0:T(8,128)(2,1)}, u32[]{:S(2)}, u32[]{:S(2)}) collective-permute-start(bf16[2,288,256]{2,1,0:T(8,128)(2,1)} %get-tuple-element.285), channel_id=1, source_target_pairs={{0,1},{1,0},{2,3},{3,2},{4,5},{5,4},{6,7},{7,6},{8,9},{9,8},{10,11... | collective-permute-start | bytes 884744 | tf_op jit(solution)/shard_map/ppermute | solution.py:73
  406.2 26.8 %collective-permute-start.50 = (bf16[2,288,256]{2,1,0:T(8,128)(2,1)}, bf16[2,288,256]{2,1,0:T(8,128)(2,1)}, u32[]{:S(2)}, u32[]{:S(2)}) collective-permute-start(bf16[2,288,256]{2,1,0:T(8,128)(2,1)} %get-tuple-element.286), channel_id=1, source_target_pairs={{0,2},{1,3},{2,0},{3,1},{4,6},{5,7},{6,4},{7,5},{8,10},{9,11},{10,... | collective-permute-start | bytes 884744 | tf_op jit(solution)/shard_map/ppermute | solution.py:73
  407.0 26.5 %collective-permute-start.51 = (bf16[2,288,256]{2,1,0:T(8,128)(2,1)}, bf16[2,288,256]{2,1,0:T(8,128)(2,1)}, u32[]{:S(2)}, u32[]{:S(2)}) collective-permute-start(bf16[2,288,256]{2,1,0:T(8,128)(2,1)} %get-tuple-element.287), channel_id=1, source_target_pairs={{0,3},{1,2},{2,1},{3,0},{4,7},{5,6},{6,5},{7,4},{8,11},{9,10},{10,... | collective-permute-start | bytes 884744 | tf_op jit(solution)/shard_map/ppermute | solution.py:73
  433.5 15.3 %collective-permute-start.56 = (bf16[2,288,256]{2,1,0:T(8,128)(2,1)}, bf16[2,288,256]{2,1,0:T(8,128)(2,1)S(1)}, u32[]{:S(2)}, u32[]{:S(2)}) collective-permute-start(bf16[2,288,256]{2,1,0:T(8,128)(2,1)} %get-tuple-element.302), channel_id=1, source_target_pairs={{0,3},{1,2},{2,1},{3,0},{4,7},{5,6},{6,5},{7,4},{8,11},{9,10},{10,... | collective-permute-start | bytes 884744 | tf_op jit(solution)/shard_map/ppermute | solution.py:73
  (117 other events, 925.7 us)
Sparse Core Ops, SparseCore 0:
  117.8 86.9 all-gather.2
  208.2 91.9 all-gather.4
  347.3 104.5 all-reduce.2
